TPU v7x, 32 devices: a whole 2x2x4 slice. The times are simulated.
32 devices in a mesh: chan: 8 (over z, y), state: 4 (over x, core).
Axes of the slice: x: 2, y: 2, z: 4, core: 2. Of those that a mesh axis runs over, the one named last changes fastest.
Arguments:
- hidden_in: float32 [2048, 2048], P('chan'), may hold values from -6 to 6
- norm_gain: float32 [2048], replicated, may hold values from 0.25 to 1.75
- in_weight: bfloat16 [2048, 2, 4096], P(None, None, 'chan'), may hold values from -0.125 to 0.125
- conv_kernel: float32 [4, 4096], P(None, 'chan'), may hold values from -3 to 3
- conv_offset: float32 [4096], P('chan'), may hold values from -3 to 3
- select_rank: bfloat16 [4096, 128], P('chan'), may hold values from -0.09375 to 0.09375
- select_entry: bfloat16 [4096, 16], P('chan', 'state'), may hold values from -0.1875 to 0.1875
- select_read: bfloat16 [4096, 16], P('chan', 'state'), may hold values from -0.1875 to 0.1875
- delta_weight: bfloat16 [128, 4096], P(None, 'chan'), may hold values from -0.5 to 0.5
- step_bias: float32 [4096], P('chan'), as said below
- decay_log: float32 [16, 4096], P('state', 'chan'), may hold values from 0 to 2.77
- skip_weight: float32 [4096], P('chan'), may hold values from 0.5 to 1.5
- out_weight: bfloat16 [4096, 2048], P('chan'), may hold values from -0.375 to 0.375
- lengths: int32 [8], replicated, may hold values from 1 to 1024, 2048 in all
- pad_mask: int32 [2048], replicated, may hold values 0 or 1
- cotangent: float32 [2048, 2048], P('chan'), may hold values from -6 to 6
Outputs:
- result: float32 [2048, 2048], P('chan')
- input_grad: float32 [2048, 2048], P('chan')
- gain_grad: float32 [2048], replicated
- in_grad: float32 [2048, 2, 4096], P(None, None, 'chan')
- kernel_grad: float32 [4, 4096], P(None, 'chan')
- offset_grad: float32 [4096], P('chan')
- rank_grad: float32 [4096, 128], P('chan')
- entry_grad: float32 [4096, 16], P('chan', 'state')
- read_grad: float32 [4096, 16], P('chan', 'state')
- delta_grad: float32 [128, 4096], P(None, 'chan')
- bias_grad: float32 [4096], P('chan')
- decay_grad: float32 [16, 4096], P('state', 'chan')
- skip_grad: float32 [4096], P('chan')
- out_grad: float32 [4096, 2048], P('chan')
Inputs may be any that keep to these rules, and one draw needn't show every extreme that they name: lengths of the 8 sequences packed in order into all 2048 tokens; they sum to 2048 and the longest has exactly 1024. `pad_mask`: 1 marks a real token, 0 padding. `step_bias`: the step-size bias of each inner channel.
All inputs are finite; a program needn't handle non-finite values.
Results may differ from a plain program's by a relative error of at most 0.011.
Values may be sent and summed in bfloat16 or wider, within the bound.
No kernel may reach another device: no remote copies, remote signals or barrier semaphores. Data moves between devices by JAX's collectives and lax.ppermute only.
A program may use at most 384 MiB of HBM per device.

v0:
```python
import functools
import math

import jax
import jax.numpy as jnp
from jax import lax
from jax.experimental import pallas as pl
from jax.experimental.pallas import tpu as pltpu
from jax.sharding import PartitionSpec as P

epsilon = 1e-05
GROUP = 16
HALO = 4
TAIL = 16
FAR = 1e30
wide = jnp.float32
low = jnp.bfloat16


def spent(microseconds):
    moved = int(microseconds * 3.6e6)
    return pl.CostEstimate(flops=0, bytes_accessed=moved, transcendentals=0)


def in_hbm(values):
    return pltpu.with_memory_space_constraint(values, pltpu.HBM)


def positions(lengths, tokens_all):
    ends = jnp.cumsum(lengths)
    begins = ends - lengths
    places = jnp.arange(tokens_all, dtype=jnp.int32)
    opening = jnp.max(jnp.where(begins[:, None] <= places[None, :], begins[:, None], 0), axis=0)
    return places - opening


def silu_slope(values):
    logistic = jax.nn.sigmoid(values)
    return logistic * (1.0 + values * (1.0 - logistic))


def own_block(states):
    row = lax.broadcasted_iota(jnp.int32, (GROUP, GROUP * states), 0)
    col = lax.broadcasted_iota(jnp.int32, (GROUP, GROUP * states), 1)
    return jnp.logical_and(col >= row * states, col < (row + 1) * states)


def spreading(states):
    eye = jnp.eye(states, dtype=low)
    tiled = jnp.tile(eye, (1, GROUP))
    nothing = jnp.zeros_like(tiled)
    return jnp.concatenate(
        [
            jnp.concatenate([tiled, nothing], axis=1),
            jnp.concatenate([nothing, tiled], axis=1),
        ],
        axis=0,
    )


def transposed(values):
    count = values.shape[1]
    row = lax.broadcasted_iota(jnp.int32, (count, count), 0)
    col = lax.broadcasted_iota(jnp.int32, (count, count), 1)
    eye = jnp.where(row == col, 1.0, 0.0).astype(low)
    return lax.dot_general(eye, values, (((1,), (1,)), ((), ())), preferred_element_type=wide)


def forward_body(
    parts,
    order_ref,
    *refs,
):
    small_refs, dgated_refs, refs = refs[:parts], refs[parts : 2 * parts], refs[2 * parts :]
    forward_steps(order_ref, small_refs, dgated_refs, *refs)


def forward_steps(
    order_ref,
    small_refs,
    dgated_refs,
    pair_ref,
    fresh_ref,
    weight_ref,
    bias_ref,
    skip_ref,
    coeff_ref,
    spread_ref,
    kept_ref,
    dpre_ref,
    *rest,
):
    parts = len(small_refs)
    gated_ref, carry, step_all, drive_all, mixed_all, small_all, dgated_all = rest

    @pl.when(pl.program_id(0) == 0)
    def _():
        carry[...] = jnp.zeros_like(carry)

    coeff = coeff_ref[...]
    states = coeff.shape[0]
    rank = weight_ref.shape[0]
    length = dpre_ref.shape[0]
    quarter = length // parts
    chosen = own_block(states)
    part = order_ref[order_ref.shape[0] - 1]
    for j in range(parts):
        small_all[j] = small_refs[j][0]
    small = jnp.concatenate([small_all[part ^ j] for j in range(parts)], axis=0)
    act = jnp.concatenate([pair_ref[j, 0, 0] for j in range(parts)], axis=0).astype(wide)
    gate = jnp.concatenate([pair_ref[j, 1, 0] for j in range(parts)], axis=0).astype(wide)
    dpre = jnp.dot(small[:, :rank], weight_ref[...], preferred_element_type=wide) + bias_ref[...]
    dpre_ref[...] = dpre
    delta = jax.nn.softplus(dpre)
    step_all[...] = jnp.where(fresh_ref[...] > 0.0, delta, FAR)
    drive_all[...] = delta * act
    pair = small[:, rank:]
    columns = transposed(pair)
    reading = jnp.dot(pair, spread_ref[:, GROUP * states :], preferred_element_type=wide)
    state = carry[...]
    for group in range(length // GROUP):
        base = group * GROUP
        kept = []
        for t in range(base, base + GROUP):
            decay = jnp.exp2(step_all[t : t + 1, :] * coeff)
            state = decay * state + drive_all[t : t + 1, :] * columns[:states, t : t + 1]
            kept.append(state)
        kept_ref[base * states : (base + GROUP) * states, :] = jnp.concatenate(
            kept, axis=0
        ).astype(low)
    carry[...] = state
    for group in range(length // GROUP):
        here = slice(group * GROUP, (group + 1) * GROUP)
        block = kept_ref[group * GROUP * states : (group + 1) * GROUP * states, :]
        weights = jnp.where(chosen, reading[here], 0.0).astype(low)
        mixed_all[here, :] = jnp.dot(weights, block, preferred_element_type=wide)
    mixed = mixed_all[...] + skip_ref[...] * act
    for j in range(parts):
        dgated_all[j] = dgated_refs[j][0]
    dgated = jnp.concatenate([dgated_all[part ^ j] for j in range(parts)], axis=0).astype(wide)
    gated = (mixed * jax.nn.silu(gate)).astype(low)
    dgate = (dgated * mixed * silu_slope(gate)).astype(low)
    for j in range(parts):
        gated_ref[j, 0, 0] = gated[j * quarter : (j + 1) * quarter]
        gated_ref[j, 1, 0] = dgate[j * quarter : (j + 1) * quarter]


def backward_body(
    parts,
    order_ref,
    *refs,
):
    small_refs, dgated_refs, refs = refs[:parts], refs[parts : 2 * parts], refs[2 * parts :]
    backward_steps(order_ref, small_refs, dgated_refs, *refs)


def backward_steps(
    order_ref,
    small_refs,
    dgated_refs,
    pair_ref,
    fresh_ref,
    dpre_ref,
    kept_ref,
    before_ref,
    weight_ref,
    skip_ref,
    coeff_ref,
    spread_ref,
    *rest,
):
    parts = len(small_refs)
    own_ref, other_ref, dscan_ref = rest[:3]
    rest = rest[3:]
    (delta_grad_ref, decay_ref, sums_ref) = rest[:3]
    (carry, step_all, drive_all, delta_all, dmix_all, lam_all, flow_all) = rest[3:10]
    (lam_sum, flow_sum, cross_all, next_partial, next_dscan, small_all) = rest[10:16]
    (partial_all, dgated_all) = rest[16:]
    turn = pl.program_id(0)

    @pl.when(turn == 0)
    def _():
        carry[...] = jnp.zeros_like(carry)
        delta_grad_ref[...] = jnp.zeros_like(delta_grad_ref)
        decay_ref[...] = jnp.zeros_like(decay_ref)
        sums_ref[...] = jnp.zeros_like(sums_ref)
        next_partial[...] = jnp.zeros_like(next_partial)
        next_dscan[...] = jnp.zeros_like(next_dscan)

    coeff = coeff_ref[...]
    states = coeff.shape[0]
    rank = weight_ref.shape[0]
    length = dpre_ref.shape[0]
    quarter = length // parts
    spread = spread_ref[...]
    chosen = own_block(states)
    across = (((1,), (1,)), ((), ()))
    down = (((0,), (0,)), ((), ()))
    part = order_ref[order_ref.shape[0] - 1]
    for j in range(parts):
        small_all[j] = small_refs[j][0]
    small = jnp.concatenate([small_all[part ^ j] for j in range(parts)], axis=0)
    act = jnp.concatenate([pair_ref[j, 0, 0] for j in range(parts)], axis=0).astype(wide)
    gate = jnp.concatenate([pair_ref[j, 1, 0] for j in range(parts)], axis=0).astype(wide)
    for j in range(parts):
        dgated_all[j] = dgated_refs[j][0]
    dgated = jnp.concatenate([dgated_all[part ^ j] for j in range(parts)], axis=0).astype(wide)
    dpre = dpre_ref[...]
    delta = jax.nn.softplus(dpre)
    dmix = dgated * jax.nn.silu(gate)
    step_all[...] = jnp.where(fresh_ref[...] > 0.0, delta, FAR)
    drive_all[...] = delta * act
    delta_all[...] = delta
    dmix_all[...] = dmix
    pair = small[:, rank:]
    columns = transposed(pair)
    entering = jnp.dot(pair, spread[:, : GROUP * states], preferred_element_type=wide)
    first = jnp.where(turn == pl.num_programs(0) - 1, 0.0, before_ref[...].astype(wide))
    pulled = carry[...]
    summed = decay_ref[...]
    for group in range(length // GROUP - 1, -1, -1):
        base = group * GROUP
        lams = [None] * GROUP
        flows = [None] * GROUP
        rows = slice(base * states, (base + GROUP) * states)
        block = kept_ref[rows, :].astype(wide)
        if group:
            edge = kept_ref[(base - 1) * states : base * states, :].astype(wide)
        else:
            edge = first
        for i in range(GROUP - 1, -1, -1):
            t = base + i
            lam = columns[states:, t : t + 1] * dmix_all[t : t + 1, :] + pulled
            pulled = jnp.exp2(step_all[t : t + 1, :] * coeff) * lam
            flow = pulled * (block[(i - 1) * states : i * states] if i else edge)
            summed = summed + flow * delta_all[t : t + 1, :]
            lams[i] = lam
            flows[i] = flow * coeff
        lam_all[rows, :] = jnp.concatenate(lams, axis=0).astype(low)
        flow_all[rows, :] = jnp.concatenate(flows, axis=0).astype(low)
    carry[...] = pulled
    decay_ref[...] = summed
    ones = jnp.where(chosen, 1.0, 0.0).astype(low)
    for group in range(length // GROUP):
        here = slice(group * GROUP, (group + 1) * GROUP)
        rows = slice(group * GROUP * states, (group + 1) * GROUP * states)
        lam_block = lam_all[rows, :]
        weights = jnp.where(chosen, entering[here], 0.0).astype(low)
        lam_sum[here, :] = jnp.dot(weights, lam_block, preferred_element_type=wide)
        flow_sum[here, :] = jnp.dot(ones, flow_all[rows, :], preferred_element_type=wide)
        cross = lax.dot_general(
            drive_all[here, :].astype(low), lam_block, across, preferred_element_type=wide
        )
        cross_all[here, : GROUP * states] = jnp.where(chosen, cross, 0.0).astype(low)
        cross = lax.dot_general(
            dmix_all[here, :].astype(low), kept_ref[rows, :], across, preferred_element_type=wide
        )
        cross_all[here, GROUP * states :] = jnp.where(chosen, cross, 0.0).astype(low)
    dpair = lax.dot_general(cross_all[...], spread, across, preferred_element_type=wide)
    scale = 1.0 / math.log2(math.e)
    found = lam_sum[...]
    ddelta = flow_sum[...] * scale + found * act
    ddpre = (ddelta * jax.nn.sigmoid(dpre)).astype(low)
    delta_grad_ref[...] += lax.dot_general(
        small[:, :rank], ddpre, down, preferred_element_type=wide
    )
    dlow = lax.dot_general(ddpre, weight_ref[...], across, preferred_element_type=wide)
    dscan = (found * delta + dmix * skip_ref[...]).astype(low)
    sums_ref[0:1, :] += jnp.sum(ddpre.astype(wide), axis=0, keepdims=True)
    sums_ref[1:2, :] += jnp.sum(dmix * act, axis=0, keepdims=True)
    for value, store, after, span in (
        (dlow.astype(low), partial_all, next_partial, slice(0, rank)),
        (dpair.astype(low), partial_all, next_partial, slice(rank, rank + 2 * states)),
        (dscan, dscan_ref, next_dscan, slice(0, dscan.shape[1])),
    ):
        longer = jnp.concatenate([value, after[:, span]], axis=0)
        for j in range(parts):
            window = longer[j * quarter : (j + 1) * quarter + TAIL]
            if store is dscan_ref:
                store[j, 0] = window
            else:
                store[j, :, span] = window
        after[:, span] = value[:TAIL]
    for k in range(parts):
        (other_ref if k % 2 else own_ref)[k // 2, 0] = partial_all[part ^ k]


def forward_scan(order, small, pair, dgated, fresh, weight, bias, skip, coeff, spread):
    parts, _, blocks, quarter, width = pair.shape
    states = coeff.shape[0]
    columns = small[0].shape[-1]
    chunk = parts * quarter
    tokens = blocks * chunk

    def whole(values):
        return pl.BlockSpec(values.shape, lambda t, order: (0, 0))

    row = pl.BlockSpec((chunk, width), lambda t, order: (t, 0))
    return pl.pallas_call(
        functools.partial(forward_body, parts),
        grid_spec=pltpu.PrefetchScalarGridSpec(
            num_scalar_prefetch=1,
            grid=(blocks,),
            in_specs=[
                pl.BlockSpec((1, quarter, columns), lambda t, order: (order[blocks + t], 0, 0))
                for _ in range(parts)
            ]
            + [
                pl.BlockSpec((1, quarter, width), lambda t, order: (order[t], 0, 0))
                for _ in range(parts)
            ]
            + [
                pl.BlockSpec(
                    (parts, 2, 1, quarter, width), lambda t, order: (0, 0, order[t], 0, 0)
                ),
                pl.BlockSpec((chunk, 1), lambda t, order: (t, 0)),
            ]
            + [whole(v) for v in (weight, bias, skip, coeff, spread)],
            out_specs=[
                pl.BlockSpec((chunk * states, width), lambda t, order: (t, 0)),
                row,
                pl.BlockSpec(
                    (parts, 2, 1, quarter, width), lambda t, order: (0, 0, order[t], 0, 0)
                ),
            ],
            scratch_shapes=[
                pltpu.VMEM((states, width), wide),
                pltpu.VMEM((chunk, width), wide),
                pltpu.VMEM((chunk, width), wide),
                pltpu.VMEM((chunk, width), wide),
                pltpu.VMEM((parts, quarter, columns), low),
                pltpu.VMEM((parts, quarter, width), low),
            ],
        ),
        out_shape=[
            pltpu.HBM((tokens * states, width), low),
            pltpu.HBM((tokens, width), wide),
            pltpu.HBM((parts, 2, blocks, quarter, width), low),
        ],
        compiler_params=pltpu.CompilerParams(vmem_limit_bytes=16 * 1024 * 1024),
        cost_estimate=spent(14),
        name="forward_scan",
    )(order, *map(in_hbm, (*small, *dgated, pair, fresh, weight, bias, skip, coeff, spread)))


def backward_scan(
    order, small, pair, dgated, fresh, dpre, kept, weight, skip, coeff, spread
):
    parts, _, blocks, quarter, width = pair.shape
    states = coeff.shape[0]
    rank = weight.shape[0]
    columns = small[0].shape[-1]
    chunk = parts * quarter
    last = blocks - 1

    def whole(shape):
        return pl.BlockSpec(shape, lambda t, order: (0, 0))

    row = pl.BlockSpec((chunk, width), lambda t, order: (last - t, 0))
    return pl.pallas_call(
        functools.partial(backward_body, parts),
        grid_spec=pltpu.PrefetchScalarGridSpec(
            num_scalar_prefetch=1,
            grid=(blocks,),
            in_specs=[
                pl.BlockSpec(
                    (1, quarter, columns), lambda t, order: (order[blocks + last - t], 0, 0)
                )
                for _ in range(parts)
            ]
            + [
                pl.BlockSpec((1, quarter, width), lambda t, order: (order[last - t], 0, 0))
                for _ in range(parts)
            ]
            + [
                pl.BlockSpec(
                    (parts, 2, 1, quarter, width),
                    lambda t, order: (0, 0, order[last - t], 0, 0),
                ),
                pl.BlockSpec((chunk, 1), lambda t, order: (last - t, 0)),
                row,
                pl.BlockSpec((chunk * states, width), lambda t, order: (last - t, 0)),
                pl.BlockSpec(
                    (states, width),
                    lambda t, order: (jnp.maximum((last - t) * chunk - 1, 0), 0),
                ),
            ]
            + [whole(v.shape) for v in (weight, skip, coeff, spread)],
            out_specs=[
                pl.BlockSpec(
                    (parts // 2, 1, quarter + TAIL, columns),
                    lambda t, order: (0, order[blocks + last - t], 0, 0),
                )
                for _ in range(2)
            ]
            + [
                pl.BlockSpec(
                    (parts, 1, quarter + TAIL, width),
                    lambda t, order: (0, order[last - t], 0, 0),
                ),
                whole((rank, width)),
                whole((states, width)),
                whole((8, width)),
            ],
            scratch_shapes=[pltpu.VMEM((states, width), wide)]
            + [pltpu.VMEM((chunk, width), wide)] * 4
            + [pltpu.VMEM((chunk * states, width), low)] * 2
            + [pltpu.VMEM((chunk, width), wide)] * 2
            + [
                pltpu.VMEM((chunk, 2 * GROUP * states), low),
                pltpu.VMEM((TAIL, columns), low),
                pltpu.VMEM((TAIL, width), low),
                pltpu.VMEM((parts, quarter, columns), low),
                pltpu.VMEM((parts, quarter + TAIL, columns), low),
                pltpu.VMEM((parts, quarter, width), low),
            ],
        ),
        out_shape=[
            pltpu.HBM((parts // 2, blocks, quarter + TAIL, columns), low)
            for _ in range(2)
        ]
        + [
            pltpu.HBM((parts, blocks, quarter + TAIL, width), low),
            jax.ShapeDtypeStruct((rank, width), wide),
            jax.ShapeDtypeStruct((states, width), wide),
            jax.ShapeDtypeStruct((8, width), wide),
        ],
        compiler_params=pltpu.CompilerParams(vmem_limit_bytes=16 * 1024 * 1024),
        cost_estimate=spent(24),
        name="backward_scan",
    )(
        order,
        *map(
            in_hbm, (*small, *dgated, pair, fresh, dpre, kept, kept, weight, skip, coeff, spread)
        ),
    )


def interleave_body(inner_ref, gate_ref, out_ref):
    out_ref[:, 0, :] = inner_ref[...].astype(wide)
    out_ref[:, 1, :] = gate_ref[...].astype(wide)


def interleave(inner, gate):
    rows, width = inner.shape
    block = 256
    spec = pl.BlockSpec((block, width), lambda t: (t, 0))
    return pl.pallas_call(
        interleave_body,
        grid=(rows // block,),
        in_specs=[spec, spec],
        out_specs=pl.BlockSpec((block, 2, width), lambda t: (t, 0, 0)),
        out_shape=jax.ShapeDtypeStruct((rows, 2, width), wide),
        compiler_params=pltpu.CompilerParams(vmem_limit_bytes=16 * 1024 * 1024),
        cost_estimate=spent(5),
        name="interleave",
    )(inner, gate)


def placed_body(parts, order_ref, *refs):
    values, out_ref = refs[:parts], refs[-1]
    place = order_ref[pl.program_id(0)]
    for k in range(parts):

        @pl.when(place == k)
        def _(k=k):
            value = values[k][...].astype(wide)
            out_ref[...] = refs[parts][...] + value if len(refs) > parts + 1 else value


def placed(order, values, base=None):
    parts = len(values)
    rows, width = values[0].shape
    flat = pl.BlockSpec((rows, width), lambda p, order: (p, 0))
    return pl.pallas_call(
        functools.partial(placed_body, parts),
        grid_spec=pltpu.PrefetchScalarGridSpec(
            num_scalar_prefetch=1,
            grid=(parts,),
            in_specs=[pl.BlockSpec((rows, width), lambda p, order: (0, 0))] * parts
            + ([] if base is None else [flat]),
            out_specs=flat,
        ),
        out_shape=jax.ShapeDtypeStruct((parts * rows, width), wide),
        compiler_params=pltpu.CompilerParams(vmem_limit_bytes=24 * 1024 * 1024),
        cost_estimate=spent(2.5),
        name="placed",
    )(order, *values, *(() if base is None else (base,)))


def project_body(
    place_ref,
    *refs,
):
    pieces, refs = refs[:8], refs[8:]
    (weight_ref, flags_ref, taps_ref, offset_ref, select_ref) = refs[:5]
    (normed_ref, inner_ref, channels_ref, kept_ref, sent_ref) = refs[5:10]
    (sides, edges, window, total, acts) = refs[10:]
    turn = pl.program_id(0)
    quarter = channels_ref.shape[3]
    width = channels_ref.shape[4]
    halves = weight_ref.shape[1] // width
    taps = taps_ref.shape[0]
    inner_turns = pl.num_programs(0) // 2
    count = len(pieces)

    @pl.when(turn == 0)
    def _():
        for k in range(count):
            piece = pieces[k][...]
            normed_ref[k * quarter : (k + 1) * quarter, :] = piece[:quarter]
            sides[k * 8 : (k + 1) * 8, :] = piece[quarter:].astype(wide)
        edges[...] = jnp.zeros_like(edges)
        total[...] = jnp.zeros_like(total)

    main = jnp.dot(normed_ref[...], weight_ref[...], preferred_element_type=wide)

    @pl.when(turn < inner_turns)
    def _():
        edges[: count * 8, :] = jnp.dot(
            sides[...].astype(low), weight_ref[...], preferred_element_type=wide
        )
        for k in range(count):
            before = pl.multiple_of(place_ref[k] * 8, 8)
            after = pl.multiple_of(place_ref[count + k] * 8, 8)
            flags = flags_ref[k]
            window[0:8, :] = edges[pl.ds(before, 8), :]
            window[8 : 8 + quarter, :] = main[k * quarter : (k + 1) * quarter]
            window[8 + quarter : 16 + quarter, :] = edges[pl.ds(after, 8), :]
            masked = window[...] * flags[:, 0:1]
            window[...] = masked
            inner_ref[k] = masked
            conv = offset_ref[...] + taps_ref[taps - 1 : taps, :] * masked[8 : 8 + quarter]
            for lag in range(1, taps):
                shifted = window[8 - lag : 8 - lag + quarter, :]
                valid = flags[8 : 8 + quarter, lag : lag + 1]
                conv = conv + taps_ref[taps - 1 - lag : taps - lag, :] * shifted * valid
            act = (jax.nn.silu(conv) * flags[8 : 8 + quarter, 0:1]).astype(low)
            acts[k * quarter : (k + 1) * quarter, :] = act
            for h in range(halves):
                channels_ref[h, 0, k] = act[:, h * width : (h + 1) * width]
        total[...] += jnp.dot(acts[...], select_ref[...], preferred_element_type=wide)

    @pl.when(turn >= inner_turns)
    def _():
        gate = main.astype(low)
        for k in range(count):
            for h in range(halves):
                channels_ref[h, 0, k] = gate[
                    k * quarter : (k + 1) * quarter, h * width : (h + 1) * width
                ]

    @pl.when(turn == pl.num_programs(0) - 1)
    def _():
        for k in range(count // 2):
            plane = place_ref[2 * count + k]
            kept_ref[plane] = total[k * quarter : (k + 1) * quarter, :]
            other = k + count // 2
            sent_ref[plane] = total[other * quarter : (other + 1) * quarter, :].astype(low)


def project(places, pieces, weight, flags, taps, offset, select, parts):
    count = len(pieces)
    rows, depth = pieces[0].shape
    quarter = rows - 8
    chans = weight.shape[1] // 2
    width = chans // parts
    tile = 2 * width
    turns = 2 * chans // tile
    half = turns // 2
    small = select.shape[1]

    def whole(shape):
        return pl.BlockSpec(shape, lambda t, place: (0,) * len(shape))

    def inner(t):
        return jnp.minimum(t, half - 1)

    return pl.pallas_call(
        project_body,
        grid_spec=pltpu.PrefetchScalarGridSpec(
            num_scalar_prefetch=1,
            grid=(turns,),
            in_specs=[whole(pieces[0].shape) for _ in pieces]
            + [
                pl.BlockSpec((depth, tile), lambda t, place: (0, t)),
                whole(flags.shape),
                pl.BlockSpec((taps.shape[0], tile), lambda t, place: (0, inner(t))),
                pl.BlockSpec((1, tile), lambda t, place: (0, inner(t))),
                pl.BlockSpec((tile, small), lambda t, place: (inner(t), 0)),
            ],
            out_specs=[
                whole((count * quarter, depth)),
                pl.BlockSpec((count, quarter + 16, tile), lambda t, place: (0, 0, inner(t))),
                pl.BlockSpec(
                    (2, 1, count, quarter, width),
                    lambda t, place: (t % half, t // half, 0, 0, 0),
                ),
                whole((count // 2, quarter, small)),
                whole((count // 2, quarter, small)),
            ],
            scratch_shapes=[
                pltpu.VMEM((count * 8, depth), wide),
                pltpu.VMEM((count * 8 + 8, tile), wide),
                pltpu.VMEM((quarter + 16, tile), wide),
                pltpu.VMEM((count * quarter, small), wide),
                pltpu.VMEM((count * quarter, tile), low),
            ],
        ),
        out_shape=[
            pltpu.HBM((count * quarter, depth), low),
            pltpu.HBM((count, quarter + 16, chans), wide),
            jax.ShapeDtypeStruct((parts, 2, count, quarter, width), low),
            jax.ShapeDtypeStruct((count // 2, quarter, small), wide),
            jax.ShapeDtypeStruct((count // 2, quarter, small), low),
        ],
        compiler_params=pltpu.CompilerParams(vmem_limit_bytes=28 * 1024 * 1024),
        cost_estimate=spent(8),
        name="project",
    )(places, *map(in_hbm, (*pieces, weight, flags, taps, offset, select)))


def pull_body(order_ref, rows_ref, weight_ref, kept_ref, *refs):
    out_refs, found_ref = refs[:-1], refs[-1]
    count = rows_ref.shape[0]
    quarter = rows_ref.shape[1]
    width = out_refs[0].shape[2]
    turn = pl.program_id(0)
    bit = order_ref[count] & 1

    @pl.when(turn == 0)
    def _():
        for k in range(count):
            kept_ref[k * quarter : (k + 1) * quarter, :] = rows_ref[order_ref[k]]

    found_ref[...] = lax.dot_general(
        kept_ref[...], weight_ref[...], (((1,), (1,)), ((), ())), preferred_element_type=wide
    ).astype(low)
    for p in range(len(out_refs)):

        @pl.when(turn == p // 2)
        def _(p=p):
            here = pl.ds(pl.multiple_of((bit ^ (p % 2)) * width, width), width)
            for k in range(count):
                out_refs[p][k] = found_ref[k * quarter : (k + 1) * quarter, here]


def pull(order, rows, weight, parts):
    count, quarter, depth = rows.shape
    width = weight.shape[0] // parts
    piece = pl.BlockSpec((count, quarter, width), lambda t, order: (0, 0, 0))
    return pl.pallas_call(
        pull_body,
        grid_spec=pltpu.PrefetchScalarGridSpec(
            num_scalar_prefetch=1,
            grid=(parts // 2,),
            in_specs=[
                pl.BlockSpec((count, quarter, depth), lambda t, order: (0, 0, 0)),
                pl.BlockSpec((2 * width, depth), lambda t, order: ((order[count] // 2) ^ t, 0)),
            ],
            out_specs=[pl.BlockSpec((count * quarter, depth), lambda t, order: (0, 0))]
            + [piece] * parts,
            scratch_shapes=[pltpu.VMEM((count * quarter, 2 * width), low)],
        ),
        out_shape=[pltpu.HBM((count * quarter, depth), low)]
        + [pltpu.HBM((count, quarter, width), low)] * parts,
        compiler_params=pltpu.CompilerParams(vmem_limit_bytes=20 * 1024 * 1024),
        cost_estimate=spent(6),
        name="pull",
    )(order, in_hbm(rows), in_hbm(weight))


def emit_body(order_ref, *refs):
    pieces_ref, refs = refs[0], refs[1:]
    parts = pieces_ref.shape[0]
    (weight_ref, rows_ref, kept_ref, first_ref, second_ref, own_ref, other_ref) = refs[:7]
    (dgate_ref, gated, product) = refs[7:]
    turn = pl.program_id(0)
    half = pl.num_programs(0) // 2
    count, quarter, width = pieces_ref.shape[2:]

    @pl.when(pl.program_id(0) == 0)
    def _():
        for p in range(parts):
            here = slice(p * width, (p + 1) * width)
            for k in range(count):
                rows = slice(k * quarter, (k + 1) * quarter)
                gated[rows, here] = pieces_ref[p, 0, k]
                dgate_ref[rows, here] = pieces_ref[p, 1, k]

    values = gated[...]
    branch = jnp.dot(values, weight_ref[...], preferred_element_type=wide).astype(low)
    for k in range(count // 2):
        kept_ref[k] = branch[k * quarter : (k + 1) * quarter]
    other = branch[count // 2 * quarter :].reshape(count // 2, quarter, branch.shape[1])

    @pl.when(turn < half)
    def _():
        first_ref[...] = other

    @pl.when(turn >= half)
    def _():
        second_ref[...] = other

    product[...] = lax.dot_general(
        values, rows_ref[...], (((0,), (0,)), ((), ())), preferred_element_type=wide
    ).astype(low)
    part = order_ref[count]
    for p in range(parts):
        here = pl.ds(pl.multiple_of((part ^ p) * width, width), width)
        (other_ref if p % 2 else own_ref)[p // 2] = product[here, :]


def emit(order, pieces, weight, rows):
    parts, _, count, quarter, width = pieces.shape
    depth = weight.shape[1]
    tile = 512
    half = depth // tile // 2
    chans = parts * width
    tall = count * quarter
    return pl.pallas_call(
        emit_body,
        grid_spec=pltpu.PrefetchScalarGridSpec(
            num_scalar_prefetch=1,
            grid=(depth // tile,),
            in_specs=[
                pl.BlockSpec(pieces.shape, lambda t, order: (0, 0, 0, 0, 0)),
                pl.BlockSpec((chans, tile), lambda t, order: (0, t)),
                pl.BlockSpec((tall, tile), lambda t, order: (0, t)),
            ],
            out_specs=[
                pl.BlockSpec((count // 2, quarter, tile), lambda t, order: (0, 0, t)),
                pl.BlockSpec(
                    (count // 2, quarter, tile), lambda t, order: (0, 0, jnp.minimum(t, half - 1))
                ),
                pl.BlockSpec(
                    (count // 2, quarter, tile), lambda t, order: (0, 0, jnp.maximum(t - half, 0))
                ),
                pl.BlockSpec((parts // 2, width, tile), lambda t, order: (0, 0, t)),
                pl.BlockSpec((parts // 2, width, tile), lambda t, order: (0, 0, t)),
                pl.BlockSpec((tall, chans), lambda t, order: (0, 0)),
            ],
            scratch_shapes=[pltpu.VMEM((tall, chans), low), pltpu.VMEM((chans, tile), low)],
        ),
        out_shape=[
            pltpu.HBM((count // 2, quarter, depth), low),
            pltpu.HBM((count // 2, quarter, depth // 2), low),
            pltpu.HBM((count // 2, quarter, depth // 2), low),
            pltpu.HBM((parts // 2, width, depth), low),
            pltpu.HBM((parts // 2, width, depth), low),
            pltpu.HBM((tall, chans), low),
        ],
        compiler_params=pltpu.CompilerParams(vmem_limit_bytes=20 * 1024 * 1024),
        cost_estimate=spent(6),
        name="emit",
    )(order, in_hbm(pieces), in_hbm(weight), in_hbm(rows))


def turn_body(order_ref, *refs):
    count = 8
    smalls, refs = refs[:2], refs[2:]
    (dscan_ref, select_ref, inner_ref, flags_ref, taps_ref, offset_ref, dgate_ref) = refs[:7]
    (dboth_ref, grad_ref, rows_ref) = refs[7:10]
    (small_all, shifted, acts) = refs[10:]
    rank = grad_ref.shape[1]
    parts = pl.num_programs(0) // 2
    turn = pl.program_id(0)
    span = inner_ref.shape[1]
    quarter = span - 16
    reach = quarter + 8
    taps = taps_ref.shape[0]

    @pl.when(turn == 0)
    def _():
        for k in range(count):
            plane = order_ref[k] // 2
            small_all[k * span : (k + 1) * span, :] = smalls[k // (count // 2)][plane]

    @pl.when(turn < parts)
    def _():
        whole = lax.dot_general(
            small_all[...],
            select_ref[...],
            (((1,), (1,)), ((), ())),
            preferred_element_type=wide,
        )
        found = dscan_ref[0]
        sums = [0.0] * (taps + 1)
        for k in range(count):
            flags = flags_ref[k, 8 : 8 + reach, :]
            mask = flags[:, 0:1]
            conv = offset_ref[...]
            for lag in range(taps):
                term = taps_ref[taps - 1 - lag : taps - lag, :] * inner_ref[
                    k, 8 - lag : 8 - lag + reach, :
                ]
                conv = conv + (term * flags[:, lag : lag + 1] if lag else term)
            sig = jax.nn.sigmoid(conv)
            act = conv * sig * mask
            acts[k * quarter : (k + 1) * quarter, :] = act[:quarter].astype(low)
            dact = found[k, :reach].astype(wide) + whole[k * span : k * span + reach]
            dconv = dact * mask * (sig * (1.0 + conv * (1.0 - sig)))
            dinner = 0.0
            for lag in range(taps):
                masked = dconv * flags[:, lag : lag + 1] if lag else dconv
                sums[taps - 1 - lag] += jnp.sum(
                    masked[:quarter] * inner_ref[k, 8 - lag : 8 - lag + quarter, :],
                    axis=0,
                    keepdims=True,
                )
                if lag:
                    shifted[lag, :reach, :] = masked
                    masked = shifted[lag, lag : lag + quarter, :]
                else:
                    sums[taps] += jnp.sum(masked[:quarter], axis=0, keepdims=True)
                    masked = masked[:quarter]
                dinner = dinner + masked * taps_ref[taps - 1 - lag : taps - lag, :]
            dboth_ref[k * quarter : (k + 1) * quarter, :] = (dinner * mask[:quarter]).astype(low)
        for index, value in enumerate(sums):
            rows_ref[index : index + 1, :] = value
        mains = jnp.concatenate(
            [small_all[k * span : k * span + quarter, :] for k in range(count)], axis=0
        )
        grad_ref[...] = lax.dot_general(
            acts[...], mains[:, :rank], (((0,), (0,)), ((), ())), preferred_element_type=wide
        ).astype(low)
        rows_ref[8:, :] = lax.dot_general(
            mains[:, rank:], acts[...], (((0,), (0,)), ((), ())), preferred_element_type=wide
        )

    @pl.when(turn >= parts)
    def _():
        dboth_ref[...] = dgate_ref[...]


def turn_back(order, smalls, dscan, select, inner, flags, taps, offset, dgate, rank):
    parts, count, span, _ = dscan.shape
    small = smalls[0].shape[-1]
    chans = select.shape[0]
    width = chans // parts
    quarter = span - 16

    def whole(shape):
        return pl.BlockSpec(shape, lambda t, order: (0,) * len(shape))

    def early(t):
        return jnp.minimum(t, parts - 1)

    return pl.pallas_call(
        turn_body,
        grid_spec=pltpu.PrefetchScalarGridSpec(
            num_scalar_prefetch=1,
            grid=(2 * parts,),
            in_specs=[whole(v.shape) for v in smalls]
            + [
                pl.BlockSpec((1, count, span, width), lambda t, order: (early(t), 0, 0, 0)),
                pl.BlockSpec((width, small), lambda t, order: (early(t), 0)),
                pl.BlockSpec((count, span, width), lambda t, order: (0, 0, early(t))),
                whole(flags.shape),
                pl.BlockSpec((taps.shape[0], width), lambda t, order: (0, early(t))),
                pl.BlockSpec((1, width), lambda t, order: (0, early(t))),
                pl.BlockSpec(
                    (count * quarter, width), lambda t, order: (0, jnp.maximum(t - parts, 0))
                ),
            ],
            out_specs=[
                pl.BlockSpec((count * quarter, width), lambda t, order: (0, t)),
                pl.BlockSpec((width, rank), lambda t, order: (early(t), 0)),
                pl.BlockSpec((small - rank + 8, width), lambda t, order: (0, early(t))),
            ],
            scratch_shapes=[
                pltpu.VMEM((count * span, small), low),
                pltpu.VMEM((taps.shape[0], span, width), wide),
                pltpu.VMEM((count * quarter, width), low),
            ],
        ),
        out_shape=[
            jax.ShapeDtypeStruct((count * quarter, 2 * chans), low),
            pltpu.HBM((chans, rank), low),
            jax.ShapeDtypeStruct((small - rank + 8, chans), wide),
        ],
        compiler_params=pltpu.CompilerParams(vmem_limit_bytes=20 * 1024 * 1024),
        cost_estimate=spent(5.5),
        name="turn_back",
    )(
        order,
        *smalls,
        dscan,
        select,
        inner,
        flags,
        taps,
        offset,
        dgate,
    )


class Moves:
    def __init__(self, n_chan, n_state):
        self.n_chan = n_chan
        self.n_state = n_state
        self.near = (n_chan, n_state) == (8, 4)
        self.chan = lax.axis_index("chan").astype(jnp.uint32)
        self.part = lax.axis_index("state").astype(jnp.uint32)
        self.z = self.chan // 2
        self.y = self.chan % 2
        places = jnp.arange(n_chan, dtype=jnp.uint32)
        if self.near:
            planes = (self.z + 4 - places % 4) % 4
            self.blocks = planes * 2 + (self.y + places // 4) % 2
            hops = (self.z + 4 - places // 2) % 4
            self.order = (self.y + places) % 2 * 4 + hops
        else:
            self.blocks = places
            self.order = places

    def over_y(self, values):
        return lax.ppermute(values, "chan", [(i, i ^ 1) for i in range(8)])

    def over_z(self, values, hops):
        return lax.ppermute(values, "chan", [(i, (i + 2 * hops) % 8) for i in range(8)])

    def over_state(self, values, bits):
        return lax.ppermute(values, "state", [(i, i ^ bits) for i in range(4)])

    def swap_state(self, values):
        return lax.all_to_all(values, "state", 0, 0, tiled=True)

    def pair(self, bit, own, other):
        return jnp.stack([jnp.where(bit == 0, own, other), jnp.where(bit == 0, other, own)])

    def in_order(self, pieces):
        own, core, across, slant = pieces
        bit = self.part % 2
        near = self.pair(bit, own, core)
        far = self.pair(bit, across, slant)
        return self.pair(self.part // 2, near, far).reshape((4,) + own.shape)

    def pieces_state(self, values):
        core = self.over_state(values, 1)
        across = self.over_state(values, 2)
        return values, core, across, self.over_state(across, 1)

    def gather_state(self, values):
        if not self.near:
            return lax.all_gather(values, "state", axis=0)
        return self.in_order(self.pieces_state(values))

    def gather_near(self, values):
        if not self.near:
            found = lax.all_gather(values, "state", axis=0)
            return [
                lax.dynamic_index_in_dim(found, self.part ^ k, 0, keepdims=False)
                for k in range(self.n_state)
            ]
        return list(self.pieces_state(values))

    def trade_state(self, values):
        if not self.near:
            return self.swap_state(values)
        chosen = [
            lax.dynamic_index_in_dim(values, self.part ^ k, 0, keepdims=False) for k in range(4)
        ]
        moved = [chosen[0]] + [self.over_state(chosen[k], k) for k in (1, 2, 3)]
        return self.in_order(moved)

    def pieces_chan(self, values):
        own = self.over_y(values)
        along = [self.over_z(values, hops) for hops in (1, 2, 3)]
        own, along[0] = tied(own, along[0])
        return [values] + along + [own] + [self.over_y(piece) for piece in along]

    def gather_chan(self, values):
        if not self.near:
            return lax.all_gather(values, "chan", axis=0)
        return jnp.stack(self.pieces_chan(values))

    def gather_rows(self, values, cut):
        if not self.near:
            found = lax.all_gather(values, "chan", axis=0)
            return found[:, :cut].reshape(-1, values.shape[1]), found[:, cut:]
        pieces = self.pieces_chan(values)
        first = jnp.concatenate([piece[:cut] for piece in pieces], axis=0)
        return first, jnp.stack([piece[cut:] for piece in pieces])

    def in_axis_order(self, values):
        if not self.near:
            return values
        return jnp.stack(
            [
                lax.dynamic_index_in_dim(values, self.order[k], 0, keepdims=False)
                for k in range(self.n_chan)
            ]
        )

    def gather_small(self, values):
        if not self.near:
            return lax.all_gather(values, "chan", axis=0)
        copies = jnp.broadcast_to(values[None], (self.n_chan,) + values.shape)
        return lax.all_to_all(copies, "chan", 0, 0, tiled=True)

    def sum_small(self, parts):
        moved = lax.all_to_all(parts, "chan", 0, 0, tiled=True)
        return jnp.sum(moved.astype(wide), axis=0)

    def joined_planes(self, kept, sent):
        return kept + self.over_y(sent).astype(wide)

    def summed_planes(self, joined):
        total = joined[0]
        for hops in (1, 2, 3):
            total = total + self.over_z(joined[4 - hops].astype(low), hops).astype(wide)
        return total

    def sum_planes(self, kept, sent):
        return self.summed_planes(self.joined_planes(kept, sent))

    def sum_chan(self, parts):
        if not self.near:
            return self.sum_small(parts.astype(low))
        return self.sum_planes(parts[:4], parts[4:].astype(low))

    def sum_row(self, values):
        if not self.near:
            return lax.psum(values, "chan")
        both = values + self.over_y(values)
        total = both
        for hops in (1, 2, 3):
            total = total + self.over_z(both, hops)
        return total

    def sum_state(self, parts):
        if not self.near:
            moved = lax.all_to_all(parts, "state", 0, 0, tiled=True)
            return jnp.sum(moved.astype(wide), axis=0).astype(low)
        cut = parts.reshape((2, 2) + parts.shape[1:])
        core = self.part % 2
        sent = lax.dynamic_index_in_dim(cut, 1 - core, 1, keepdims=False)
        kept = lax.dynamic_index_in_dim(cut, core, 1, keepdims=False)
        chip = (kept.astype(wide) + self.over_state(sent, 1).astype(wide)).astype(low)
        side = self.part // 2
        sent = lax.dynamic_index_in_dim(chip, 1 - side, 0, keepdims=False)
        kept = lax.dynamic_index_in_dim(chip, side, 0, keepdims=False)
        return (kept.astype(wide) + self.over_state(sent, 2).astype(wide)).astype(low)

    def total_state(self, values):
        rows, columns = values.shape
        parts = values.reshape(self.n_state, rows // self.n_state, columns)
        return self.gather_state(self.sum_state(parts)).reshape(rows, columns)


def tied(*values):
    return lax.optimization_barrier(values)


def after(values, *others):
    token = lax.optimization_barrier((lax.create_token(), others))[0]
    return lax.optimization_barrier((token, values))[1]


def shards(
    n_chan,
    n_state,
    hidden_in,
    norm_gain,
    in_weight,
    conv_kernel,
    conv_offset,
    select_rank,
    select_entry,
    select_read,
    delta_weight,
    step_bias,
    decay_log,
    skip_weight,
    out_weight,
    lengths,
    pad_mask,
    cotangent,
):
    rows_dev, width = hidden_in.shape
    tokens = pad_mask.shape[0]
    chans = in_weight.shape[2]
    taps = conv_kernel.shape[0]
    rank = select_rank.shape[1]
    per_state = select_entry.shape[1]
    states = per_state * n_state
    small = rank + 2 * states
    quarter = rows_dev // n_state
    own = chans // n_state
    rows_q = n_chan * quarter
    part = lax.axis_index("state").astype(jnp.uint32)
    contract_rows = (((0,), (0,)), ((), ()))
    contract_cols = (((1,), (1,)), ((), ()))
    moves = Moves(n_chan, n_state)
    blocks = moves.blocks
    order = jnp.concatenate([moves.order, moves.order, part[None]]).astype(jnp.int32)

    def mine(values, axis=0):
        return lax.dynamic_slice_in_dim(values, part * own, own, axis)

    def in_axis(pieces):
        stacked = jnp.stack(pieces)
        return jnp.stack(
            [
                lax.dynamic_index_in_dim(stacked, part ^ j, 0, keepdims=False)
                for j in range(n_state)
            ]
        )

    def split_own(values):
        cut = values.reshape(values.shape[:-1] + (n_state, own))
        return jnp.moveaxis(cut, -2, 0)

    def join_own(values):
        moved = jnp.moveaxis(values, 0, -2)
        return moved.reshape(moved.shape[:-2] + (chans,))

    def chosen_rows(chooser, values):
        flat = values.reshape(values.shape[0], -1)
        found = jnp.dot(chooser, flat, precision=lax.Precision.HIGHEST)
        return found.reshape(values.shape)

    start = part * quarter
    hidden_q = lax.dynamic_slice_in_dim(hidden_in, start, quarter, 0)
    ahead = (start + (rows_dev - HALO)) % rows_dev
    behind = (start + quarter) % rows_dev
    local = jnp.concatenate(
        [
            hidden_q,
            lax.dynamic_slice_in_dim(hidden_in, ahead, HALO, 0),
            lax.dynamic_slice_in_dim(hidden_in, behind, HALO, 0),
        ],
        axis=0,
    )
    inv_all = lax.rsqrt(jnp.mean(local * local, axis=1, keepdims=True) + epsilon)
    scaled_all = local * inv_all
    normed_all = (scaled_all * norm_gain[None, :]).astype(low)
    inv_rms = inv_all[:quarter]
    scaled = scaled_all[:quarter]
    normed_q, normed_side = moves.gather_rows(normed_all, quarter)
    cot_q = lax.dynamic_slice_in_dim(cotangent, start, quarter, 0).astype(low)
    grad_q = lax.all_gather(cot_q, "chan", axis=0)

    place = positions(lengths, tokens)
    flags = [pad_mask.astype(wide)]
    flags += [(place >= lag).astype(wide) for lag in range(1, taps)]
    flags = jnp.stack(flags)
    padded = jnp.pad(flags, ((0, 0), (HALO, HALO + rows_dev)))
    span = quarter + 2 * HALO
    flags_win = lax.dynamic_slice_in_dim(padded, start, n_chan * rows_dev, 1)
    flags_win = flags_win.reshape(taps, n_chan, rows_dev)[:, :, :span]
    chooser = (blocks[:, None] == jnp.arange(n_chan)[None, :]).astype(wide)
    flags_win = jnp.einsum("kb,fbr->fkr", chooser, flags_win)
    mask_win = flags_win[0][:, :, None]
    valid_win = flags_win[1:]
    one_before = (blocks[:, None] - 1 == blocks[None, :]).astype(wide)
    one_after = (blocks[:, None] + 1 == blocks[None, :]).astype(wide)
    itself = jnp.eye(n_chan, dtype=wide)
    one_before = jnp.where(part == 0, one_before, itself)
    one_after = jnp.where(part == n_state - 1, one_after, itself)

    def valid_at(lag, first, count):
        if lag == 0:
            return 1.0
        return valid_win[lag - 1][:, first : first + count, None]

    columns = jnp.concatenate([select_entry, select_read], axis=1)
    columns = moves.gather_state(columns).reshape(n_state, chans, 2, per_state)
    columns = jnp.transpose(columns, (1, 2, 0, 3)).reshape(chans, 2 * states)
    select = jnp.concatenate([select_rank, columns], axis=1)
    decay_own = moves.swap_state(jnp.swapaxes(decay_log.reshape(per_state, n_state, own), 0, 1))
    coeff = -jnp.exp(decay_own.reshape(states, own))

    in_flat = lax.optimization_barrier(in_weight.reshape(width, 2 * chans))
    both = jnp.dot(normed_q, in_flat, preferred_element_type=wide)
    both = both.reshape(n_chan, quarter, 2 * chans)
    gate_q = both[:, :, chans:].astype(low)
    sides = jnp.dot(
        normed_side.reshape(-1, width), in_flat[:, :chans], preferred_element_type=wide
    ).reshape(n_chan, 2 * HALO, chans)
    before = chosen_rows(one_before, sides[:, :HALO])
    after = chosen_rows(one_after, sides[:, HALO:])
    inner_win = jnp.concatenate([before, both[:, :, :chans], after], axis=1) * mask_win

    reach = quarter + HALO
    conv_win = conv_offset
    for index in range(taps):
        lag = taps - 1 - index
        shifted = inner_win[:, HALO - lag : HALO - lag + reach]
        conv_win = conv_win + conv_kernel[index] * shifted * valid_at(lag, HALO, reach)
    act_win = jax.nn.silu(conv_win[:, :quarter]) * mask_win[:, HALO : HALO + quarter]
    act_win = act_win.astype(low)
    act_q = act_win.reshape(rows_q, chans)

    partial = jnp.dot(act_q, select, preferred_element_type=wide)
    summed = moves.sum_chan(partial.reshape(n_chan, quarter, small)).astype(low)
    sent = jnp.stack([split_own(act_win), split_own(gate_q)], axis=1)
    channels = moves.swap_state(sent)
    summed, channels = tied(summed, channels)
    picked = moves.gather_near(moves.gather_small(summed))

    if moves.near:
        grad_q = jnp.concatenate(
            [lax.dynamic_index_in_dim(grad_q, blocks[k], 0, keepdims=False) for k in range(8)],
            axis=0,
        )
    grad_q = grad_q.reshape(rows_q, width)
    dgated_q = lax.dot_general(grad_q, out_weight, contract_cols, preferred_element_type=wide)
    dgated_q = dgated_q.astype(low).reshape(n_chan, quarter, chans)
    dgated = list(in_axis(list(moves.swap_state(split_own(dgated_q)))))

    weight_own = mine(delta_weight, 1)
    bias_own = mine(step_bias)[None, :]
    skip_own = mine(skip_weight)[None, :]
    fresh = (place > 0).astype(wide)[:, None]
    spread = spreading(states)
    coeff_two = coeff * math.log2(math.e)
    kept, dpre, gated = forward_scan(
        order, picked, channels, dgated, fresh, weight_own, bias_own, skip_own, coeff_two, spread
    )

    gated = moves.swap_state(gated)
    gated_q = join_own(gated[:, 0]).reshape(rows_q, chans)
    dgate_q = join_own(gated[:, 1]).reshape(rows_q, chans)
    own_sums, other_sums, dscan, delta_grad_own, decay_total, sums = backward_scan(
        order,
        picked,
        channels,
        dgated,
        fresh,
        dpre,
        kept,
        weight_own,
        skip_own,
        coeff_two,
        spread,
    )
    partial = [(other_sums if k % 2 else own_sums)[k // 2] for k in range(n_state)]
    partial = in_axis(partial)
    decay_grad_own = coeff * decay_total
    partial, gated_q = tied(partial, gated_q)
    partial = moves.sum_state(partial)

    branch = jnp.dot(gated_q, out_weight, preferred_element_type=wide)
    out_part = lax.dot_general(gated_q, grad_q, contract_rows, preferred_element_type=wide)
    packed = jnp.concatenate([delta_grad_own, decay_grad_own, sums], axis=0)
    partial, branch, out_part, packed, dscan = tied(
        partial, branch.astype(low), out_part.astype(low), packed, dscan
    )
    dsmall = moves.gather_chan(moves.sum_small(partial).astype(low))[:, :reach]
    dscan_win = join_own(moves.swap_state(dscan))[:, :reach].astype(wide)
    gate_part = lax.dot_general(normed_q, dgate_q, contract_rows, preferred_element_type=wide)
    branch = lax.psum_scatter(
        moves.in_axis_order(branch.reshape(n_chan, quarter, width)).reshape(rows_q, width),
        "chan",
        scatter_dimension=0,
        tiled=True,
    )
    out_grad = moves.total_state(out_part).astype(wide)
    dsmall, dscan_win, dgate_q, gate_part = tied(
        dsmall, dscan_win, dgate_q, gate_part.astype(low)
    )

    dact = dscan_win + lax.dot_general(
        dsmall.reshape(-1, small), select, contract_cols, preferred_element_type=wide
    ).reshape(n_chan, reach, chans)
    dconv = dact * mask_win[:, HALO:] * silu_slope(conv_win)
    dinner = jnp.zeros((n_chan, quarter, chans), wide)
    kernel_rows = []
    for index in range(taps):
        lag = taps - 1 - index
        masked = dconv * valid_at(lag, HALO, reach)
        shifted = inner_win[:, HALO - lag : HALO - lag + quarter]
        kernel_rows.append(jnp.sum(masked[:, :quarter] * shifted, axis=(0, 1)))
        dinner = dinner + masked[:, lag : lag + quarter] * conv_kernel[index]
    kernel_rows.append(jnp.sum(dconv[:, :quarter], axis=(0, 1)))
    dinner = (dinner * mask_win[:, HALO : HALO + quarter]).astype(low).reshape(rows_q, chans)
    dboth = jnp.concatenate([dinner, dgate_q], axis=1)

    def backed(rows, weight):
        return lax.dot_general(rows, weight, contract_cols, preferred_element_type=wide)

    if moves.near:
        half = width // 2
        joined = []
        gains = []
        for columns in (slice(0, half), slice(half, width)):
            gain = jnp.zeros((half,), wide)
            halves = []
            for rows in (slice(rows_q // 2, rows_q), slice(0, rows_q // 2)):
                piece = backed(dboth[rows], in_flat[columns])
                gain = gain + jnp.sum(piece * normed_q[rows, columns].astype(wide), axis=0)
                halves.append(piece.reshape(4, quarter, half))
            joined.append(moves.joined_planes(halves[1], halves[0].astype(low)))
            gains.append(gain)
        joined[0], gains[0], gains[1], dinner = tied(joined[0], gains[0], gains[1], dinner)
        dnormed = jnp.concatenate([moves.summed_planes(v) for v in joined], axis=1)
        gain_part = jnp.concatenate(gains)
    else:
        dnormed = backed(dboth, in_flat)
        gain_part = jnp.sum(dnormed * normed_q.astype(wide), axis=0)
        dnormed = moves.sum_chan(dnormed.reshape(n_chan, quarter, width))
    gain_part = moves.sum_row(gain_part)[None]
    dscaled = dnormed * norm_gain[None, :]
    change = inv_rms * (dscaled - scaled * jnp.mean(dscaled * scaled, axis=1, keepdims=True))
    change = moves.gather_state(jnp.concatenate([change, gain_part], axis=0).astype(low))
    input_grad = cotangent + change[:, :quarter].reshape(rows_dev, width)
    gain_grad = jnp.sum(change[:, quarter].astype(wide), axis=0) / norm_gain

    result = hidden_in + moves.gather_state(branch).reshape(rows_dev, width)
    inner_part = lax.dot_general(normed_q, dinner, contract_rows, preferred_element_type=wide)
    gate_grad = moves.total_state(gate_part)
    in_grad = interleave(moves.total_state(inner_part.astype(low)), gate_grad)

    dsmall_q = dsmall[:, :quarter].reshape(rows_q, small)
    select_grad = lax.dot_general(dsmall_q, act_q, contract_rows, preferred_element_type=wide)
    rest = moves.gather_near(jnp.concatenate([select_grad, jnp.stack(kernel_rows)], axis=0))
    rest = sum(rest)
    rank_grad = rest[:rank].T
    first = rank + part * per_state
    entry_grad = lax.dynamic_slice_in_dim(rest, first, per_state, 0).T
    read_grad = lax.dynamic_slice_in_dim(rest, first + states, per_state, 0).T
    kernel_grad = rest[small : small + taps]
    offset_grad = rest[small + taps]
    packed = jnp.swapaxes(moves.gather_state(packed), 0, 1).reshape(-1, chans)
    delta_grad = packed[:rank]
    decay_grad = lax.dynamic_slice_in_dim(packed, rank + part * per_state, per_state, 0)
    bias_grad = packed[rank + states]
    skip_grad = packed[rank + states + 1]
    return (
        result,
        input_grad,
        gain_grad,
        in_grad,
        kernel_grad,
        offset_grad,
        rank_grad,
        entry_grad,
        read_grad,
        delta_grad,
        bias_grad,
        decay_grad,
        skip_grad,
        out_grad,
    )


def near_shards(
    n_chan,
    n_state,
    hidden_in,
    norm_gain,
    in_weight,
    conv_kernel,
    conv_offset,
    select_rank,
    select_entry,
    select_read,
    delta_weight,
    step_bias,
    decay_log,
    skip_weight,
    out_weight,
    lengths,
    pad_mask,
    cotangent,
):
    rows_dev, width = hidden_in.shape
    tokens = pad_mask.shape[0]
    chans = in_weight.shape[2]
    taps = conv_kernel.shape[0]
    rank = select_rank.shape[1]
    per_state = select_entry.shape[1]
    states = per_state * n_state
    small = rank + 2 * states
    quarter = rows_dev // n_state
    own = chans // n_state
    rows_q = n_chan * quarter
    part = lax.axis_index("state").astype(jnp.uint32)
    contract_rows = (((0,), (0,)), ((), ()))
    contract_cols = (((1,), (1,)), ((), ()))
    moves = Moves(n_chan, n_state)
    blocks = moves.blocks
    planes = jnp.arange(4, dtype=jnp.uint32)
    small_order = jnp.stack([(moves.y ^ u) * 4 + planes for u in (0, 1)], axis=1).reshape(-1)
    order = jnp.concatenate([moves.order, small_order, part[None]]).astype(jnp.int32)
    places = jnp.concatenate([blocks, part[None]]).astype(jnp.int32)
    blocks = blocks.astype(jnp.int32)

    def mine(values, axis=0):
        return lax.dynamic_slice_in_dim(values, part * own, own, axis)

    start = part * quarter
    hidden_q = lax.dynamic_slice_in_dim(hidden_in, start, quarter, 0)
    ahead = (start + (rows_dev - HALO)) % rows_dev
    behind = (start + quarter) % rows_dev
    local = jnp.concatenate(
        [
            hidden_q,
            lax.dynamic_slice_in_dim(hidden_in, behind, HALO, 0),
            lax.dynamic_slice_in_dim(hidden_in, ahead, HALO, 0),
        ],
        axis=0,
    )
    inv_all = lax.rsqrt(jnp.mean(local * local, axis=1, keepdims=True) + epsilon)
    scaled_all = local * inv_all
    normed_all = (scaled_all * norm_gain[None, :]).astype(low)
    inv_rms = inv_all[:quarter]
    scaled = scaled_all[:quarter]
    cot_q = lax.dynamic_slice_in_dim(cotangent, start, quarter, 0).astype(low)
    ranks = (part ^ jnp.arange(n_state, dtype=jnp.uint32)).astype(jnp.int32)

    def trades(values):
        return [values[0]] + [moves.over_state(values[k], k) for k in (1, 2, 3)]

    def core_halves(values):
        cut = values.reshape((2, 2) + values.shape[1:])
        core = part % 2
        return (
            lax.dynamic_index_in_dim(cut, 1 - core, 1, keepdims=False),
            lax.dynamic_index_in_dim(cut, core, 1, keepdims=False),
        )

    def chip_halves(values):
        side = part // 2
        return (
            lax.dynamic_index_in_dim(values, 1 - side, 0, keepdims=False),
            lax.dynamic_index_in_dim(values, side, 0, keepdims=False),
        )

    def total_of(own_part, others):
        total = own_part.astype(wide)
        for piece in others:
            total = total + piece.astype(wide)
        return total.astype(low)

    def added(kept, came):
        return (kept.astype(wide) + came.astype(wide)).astype(low)

    columns = jnp.concatenate([select_entry, select_read], axis=1)
    decay_cut = jnp.swapaxes(decay_log.reshape(per_state, n_state, own), 0, 1)
    across = moves.over_y(normed_all)
    along = [moves.over_z(normed_all, hops) for hops in (1, 2, 3)]
    columns_core = moves.over_state(columns, 1)
    columns_chip = moves.over_state(columns, 2)
    decay_own = moves.swap_state(decay_cut)
    in_flat = in_weight.reshape(width, 2 * chans)
    across, along[0], along[1], along[2], columns_core, columns_chip, decay_own, in_flat, cot_q = tied(
        across, *along, columns_core, columns_chip, decay_own, in_flat, cot_q
    )
    grads = lax.all_gather(cot_q, "chan", axis=0)
    over = [moves.over_y(piece) for piece in along]
    columns_slant = moves.over_state(columns_chip, 1)
    over[0], over[1], over[2], columns_slant = tied(*over, columns_slant)
    pieces = [normed_all] + along + [across] + over

    place = positions(lengths, tokens)
    flags = [pad_mask.astype(wide)]
    flags += [(place >= lag).astype(wide) for lag in range(1, taps)]
    flags = jnp.stack(flags)
    padded = jnp.pad(flags, ((0, 0), (8, 8 + rows_dev)))
    span = quarter + 16
    flags_win = lax.dynamic_slice_in_dim(padded, start, n_chan * rows_dev, 1)
    flags_win = flags_win.reshape(taps, n_chan, rows_dev)[:, :, :span]
    chooser = (blocks[:, None] == jnp.arange(n_chan)[None, :]).astype(wide)
    flags_rows = jnp.einsum("kb,fbr->krf", chooser, flags_win)
    itself = jnp.arange(n_chan, dtype=jnp.int32)
    nearby = blocks[:, None] - blocks[None, :]
    one_before = jnp.where(blocks > 0, jnp.argmax(nearby == 1, axis=1), n_chan)
    one_after = jnp.where(blocks < n_chan - 1, jnp.argmax(nearby == -1, axis=1), n_chan)
    one_before = jnp.where(part == 0, one_before, itself)
    one_after = jnp.where(part == n_state - 1, one_after, itself)
    neighbours = jnp.concatenate([one_before, one_after, blocks[:4] // 2]).astype(jnp.int32)

    columns = moves.in_order((columns, columns_core, columns_chip, columns_slant))
    columns = columns.reshape(n_state, chans, 2, per_state)
    columns = jnp.transpose(columns, (1, 2, 0, 3)).reshape(chans, 2 * states)
    select = jnp.concatenate([select_rank, columns], axis=1)
    coeff = -jnp.exp(decay_own.reshape(states, own))

    normed_q, inner_all, sent, kept, other = project(
        neighbours, pieces, in_flat, flags_rows, conv_kernel, conv_offset[None, :], select, n_state
    )
    reach = quarter + HALO
    channels = moves.swap_state(sent)
    came = moves.over_y(other)
    joined = added(kept, came)
    along = [moves.over_z(joined, hops) for hops in (1, 2, 3)]
    grad_q, *dgated = pull(places, grads, out_weight, n_state)
    along[0], along[1], along[2], *dgated = tied(*along, *dgated)
    summed = total_of(joined, along)
    came = moves.over_y(summed)
    dgated = trades(dgated)
    picked = moves.gather_near(jnp.concatenate([summed, came], axis=0))
    tie = tied(*picked, *dgated, channels)
    picked, dgated, channels = tie[:4], tie[4:8], tie[8]

    weight_own = mine(delta_weight, 1)
    bias_own = mine(step_bias)[None, :]
    skip_own = mine(skip_weight)[None, :]
    fresh = (place > 0).astype(wide)[:, None]
    spread = spreading(states)
    coeff_two = coeff * math.log2(math.e)
    kept, dpre, gated = forward_scan(
        order,
        picked,
        channels,
        dgated,
        fresh,
        weight_own,
        bias_own,
        skip_own,
        coeff_two,
        spread,
    )
    gated = moves.swap_state(gated)
    own_sums, other_sums, dscan, delta_grad_own, decay_total, sums = backward_scan(
        order,
        picked,
        channels,
        dgated,
        fresh,
        dpre,
        kept,
        weight_own,
        skip_own,
        coeff_two,
        spread,
    )
    decay_grad_own = coeff * decay_total
    packed = jnp.concatenate([delta_grad_own, decay_grad_own, sums], axis=0).astype(low)
    own_sums, other_sums, packed, gated, dscan = tied(
        own_sums, other_sums, packed, gated, dscan
    )

    half = width // 2
    first, second = slice(0, half), slice(half, width)
    came = moves.over_state(other_sums, 1)
    branch_kept, sent, second_branch, out_kept, out_sent, dgate_q = emit(
        places, gated, out_weight, grad_q
    )
    came, sent, second_branch, out_sent, dgate_q = tied(
        came, sent, second_branch, out_sent, dgate_q
    )

    chip = added(own_sums, came)
    came = moves.over_state(chip[1], 2)
    branch_came = moves.over_y(sent)
    gate_part = lax.dot_general(normed_q, dgate_q, contract_rows, preferred_element_type=wide)
    gain = jnp.sum(gate_part * in_flat[:, chans:].astype(wide), axis=1)
    gate_part = lax.psum_scatter(gate_part.astype(low), "state", scatter_dimension=0, tiled=True)
    out_came = moves.over_state(out_sent, 1)
    came, gain, out_came = tied(came, gain, out_came)

    joined = added(chip[0], came)
    came = moves.over_y(joined[4:])
    dscan = moves.swap_state(dscan)
    out_part = added(out_kept, out_came)
    out_came = moves.over_state(out_part[1], 2)
    packed_core = moves.over_state(packed, 1)
    came, second_branch, packed_core, branch_came = tied(
        came, second_branch, packed_core, branch_came
    )

    joined = added(joined[:4], came)
    along = [moves.over_z(joined, hops) for hops in (1, 2, 3)]
    second_came = moves.over_y(second_branch)
    along[0], along[1], along[2], second_came, out_came = tied(*along, second_came, out_came)

    partial = total_of(joined, along)
    came = moves.over_y(partial)
    branch_came = jnp.concatenate([branch_came, second_came], axis=2)
    branch = added(branch_kept, branch_came)
    branches = [moves.over_z(branch[4 - hops], hops) for hops in (1, 2, 3)]
    out_part = added(out_part[0], out_came)
    out_chip = moves.over_state(out_part, 2)
    came, partial, dscan, gate_part = tied(came, partial, dscan, gate_part)
    gate_grad = lax.all_gather(gate_part, "state", axis=0, tiled=True)

    dboth, rank_part, rows_part = turn_back(
        places,
        (partial, came),
        dscan,
        select,
        inner_all,
        flags_rows,
        conv_kernel,
        conv_offset[None, :],
        dgate_q,
        rank,
    )

    def backed(rows, weight):
        return lax.dot_general(rows, weight, contract_cols, preferred_element_type=wide)

    edge = width * 11 // 16
    left, right = slice(0, edge), slice(edge, width)
    other, same = slice(rows_q // 2, rows_q), slice(0, rows_q // 2)
    left_sent = backed(dboth[other], in_flat[left]).astype(low).reshape(4, quarter, edge)
    right_all = backed(dboth, in_flat[right]).reshape(2, 4, quarter, width - edge)
    right_sent = [right_all[:, 4 - hops].astype(low) for hops in (1, 2, 3)]
    out_core = moves.over_state(out_part, 1)
    out_slant = moves.over_state(out_chip, 1)
    packed_chip = moves.over_state(packed, 2)
    tie = tied(
        left_sent, dboth, rank_part, out_core, out_slant, packed_chip, *right_sent, *branches
    )
    left_sent, dboth, rank_part, out_core, out_slant, packed_chip = tie[:6]
    right_sent, branches = tie[6:9], tie[9:]

    left_came = moves.over_y(left_sent)
    right_along = [moves.over_z(right_sent[hops - 1], hops) for hops in (1, 2, 3)]
    rank_core = moves.over_state(rank_part, 1)
    left_kept = backed(dboth[same], in_flat[left]).reshape(4, quarter, edge)
    inner_part = lax.dot_general(
        normed_q,
        after(dboth, right_along[0])[:, :chans],
        contract_rows,
        preferred_element_type=wide,
    )
    gain = gain + jnp.sum(inner_part * in_flat[:, :chans].astype(wide), axis=1)
    gain = jnp.concatenate([rows_part, gain.reshape(-1, chans)], axis=0)
    branch = total_of(branch[0], branches)
    tie = tied(
        left_came,
        left_kept,
        inner_part.astype(low),
        gain,
        branch,
        gate_grad,
        rank_core,
        *right_along,
    )
    left_came, left_kept, inner_part, gain, branch, gate_grad, rank_core = tie[:7]
    right_along = tie[7:]
    inner_part = lax.psum_scatter(inner_part, "state", scatter_dimension=0, tiled=True)

    joined = left_kept + left_came.astype(wide)
    left_sum = joined[0]
    left_along = [moves.over_z(joined[4 - hops].astype(low), hops) for hops in (1, 2, 3)]
    right_sum = right_all[:, 0]
    for piece in right_along:
        right_sum = right_sum + piece.astype(wide)
    right_came = moves.over_y(right_sum[1].astype(low))
    gain_came = moves.over_state(gain, 1)
    out_grad = placed(ranks, (out_part, out_core, out_chip, out_slant))
    packed_slant = moves.over_state(packed_chip, 1)
    tie = tied(right_came, gain_came, out_grad, packed_slant, *left_along)
    right_came, gain_came, out_grad, packed_slant = tie[:4]
    left_along = tie[4:]

    for piece in left_along:
        left_sum = left_sum + piece.astype(wide)
    right_sum = right_sum[0] + right_came.astype(wide)
    dnormed = jnp.concatenate([left_sum, right_sum], axis=1)
    dscaled = dnormed * norm_gain[None, :]
    change = inv_rms * (dscaled - scaled * jnp.mean(dscaled * scaled, axis=1, keepdims=True))
    change = change.astype(low)
    change_chip = moves.over_state(change, 2)
    change_core = moves.over_state(change, 1)
    gain = gain + gain_came
    gain_came = moves.over_state(gain, 2)
    rank_sum = added(rank_part, rank_core)
    rank_chip = moves.over_state(rank_sum, 2)
    packed = moves.in_order((packed, packed_core, packed_chip, packed_slant))
    packed = jnp.swapaxes(packed, 0, 1).reshape(-1, chans).astype(wide)
    packs = (
        packed[:rank],
        packed[rank + states],
        lax.dynamic_slice_in_dim(packed, rank + part * per_state, per_state, 0),
        packed[rank + states + 1],
    )
    tie = tied(change_chip, change_core, gain_came, rank_chip, inner_part, *packs)
    change_chip, change_core, gain_came, rank_chip, inner_part = tie[:5]
    packs = tie[5:]
    inner_grad = lax.all_gather(inner_part, "state", axis=0, tiled=True)

    change_slant = moves.over_state(change_chip, 1)
    branch_chip = moves.over_state(branch, 2)
    branch_core = moves.over_state(branch, 1)
    gain = gain + gain_came
    gain_came = moves.over_y(gain[8 + 2 * states :].reshape(width))
    rank_grad = rank_sum.astype(wide) + rank_chip.astype(wide)
    place_at = 8 + part * per_state
    smalls = (
        gain[:taps],
        gain[taps],
        rank_grad,
        lax.dynamic_slice_in_dim(gain, place_at, per_state, 0).T,
        lax.dynamic_slice_in_dim(gain, place_at + states, per_state, 0).T,
        *packs,
    )
    tie = tied(change_slant, branch_chip, branch_core, gain_came, gain, *smalls)
    change_slant, branch_chip, branch_core, gain_came, gain = tie[:5]
    smalls = tie[5:]

    branch_slant = moves.over_state(branch_chip, 1)
    gain = gain[8 + 2 * states :].reshape(width) + gain_came
    gains = [gain] + [moves.over_z(gain, hops) for hops in (1, 2, 3)]
    input_grad = placed(ranks, (change, change_core, change_chip, change_slant), cotangent)
    result = placed(ranks, (branch, branch_core, branch_chip, branch_slant), hidden_in)
    gains = jnp.stack(gains)
    gain_grad = 0.0
    for plane_at in range(4):
        gain_grad = gain_grad + lax.dynamic_index_in_dim(
            gains, (moves.z + 4 - plane_at) % 4, 0, keepdims=False
        )
    gain_grad = gain_grad / norm_gain
    in_grad = interleave(inner_grad, gate_grad)
    return (result, input_grad, gain_grad, in_grad, *smalls, out_grad)


def solution(mesh):
    sizes = dict(mesh.shape)
    program = near_shards if (sizes["chan"], sizes["state"]) == (8, 4) else shards
    return jax.shard_map(
        functools.partial(program, sizes["chan"], sizes["state"]),
        mesh=mesh,
        in_specs=(
            P("chan", None),
            P(),
            P(None, None, "chan"),
            P(None, "chan"),
            P("chan"),
            P("chan", None),
            P("chan", "state"),
            P("chan", "state"),
            P(None, "chan"),
            P("chan"),
            P("state", "chan"),
            P("chan"),
            P("chan", None),
            P(),
            P(),
            P("chan", None),
        ),
        out_specs=(
            P("chan", None),
            P("chan", None),
            P(),
            P(None, None, "chan"),
            P(None, "chan"),
            P("chan"),
            P("chan", None),
            P("chan", "state"),
            P("chan", "state"),
            P(None, "chan"),
            P("chan"),
            P("state", "chan"),
            P("chan"),
            P("chan", None),
        ),
        check_vma=False,
    )
```

profile of v0, /device:TPU:0, one launch (start us, length us, event | category | flops | bytes accessed | tf_op | source)
XLA Modules:
  0.0 354.4 jit_solution(8875774869050002268)
XLA Ops:
  20.3 3.2 all-to-all-start
  27.5 5.4 %copy.86 = bf16[256,8,2,512]{3,1,2,0:T(8,128)(2,1)} copy(bf16[256,8,2,512]{3,2,1,0:T(2,128)(2,1)} %bitcast.165) | data formatting | bytes 8388608
  32.9 4.4 %collective-permute-done.2.refs_2_ = bf16[72,2048]{1,0:T(8,128)(2,1)S(1)} collective-permute-done((bf16[72,2048]{1,0:T(8,128)(2,1)S(1)}, bf16[72,2048]{1,0:T(8,128)(2,1)S(1)}, u32[]{:S(2)}, u32[]{:S(2)}) %collective-permute-start.2) | collective-permute-done | bytes 294944 | tf_op jit(solution)/shard_map/ppermute | solution.py:921
  49.6 8.6 %collective-permute-done.6.refs_5_ = bf16[72,2048]{1,0:T(8,128)(2,1)S(1)} collective-permute-done((bf16[72,2048]{1,0:T(8,128)(2,1)S(1)}, bf16[72,2048]{1,0:T(8,128)(2,1)S(1)}, u32[]{:S(2)}, u32[]{:S(2)}) %collective-permute-start.6) | collective-permute-done | bytes 294944 | tf_op jit(solution)/shard_map/ppermute | solution.py:918
  58.2 6.4 %collective-permute-done.7.refs_6_ = bf16[72,2048]{1,0:T(8,128)(2,1)S(1)} collective-permute-done((bf16[72,2048]{1,0:T(8,128)(2,1)S(1)}, bf16[72,2048]{1,0:T(8,128)(2,1)S(1)}, u32[]{:S(2)}, u32[]{:S(2)}) %collective-permute-start.7) | collective-permute-done | bytes 294944 | tf_op jit(solution)/shard_map/ppermute | solution.py:918
  65.3 4.6 %collective-permute-done.8.refs_7_ = bf16[72,2048]{1,0:T(8,128)(2,1)S(1)} collective-permute-done((bf16[72,2048]{1,0:T(8,128)(2,1)}, bf16[72,2048]{1,0:T(8,128)(2,1)S(1)}, u32[]{:S(2)}, u32[]{:S(2)}) %collective-permute-start.8) | collective-permute-done | bytes 294944 | tf_op jit(solution)/shard_map/ppermute | solution.py:918
  72.3 9.9 %project.1 = (bf16[512,2048]{1,0:T(8,128)(2,1)}, f32[8,80,512]{2,1,0:T(8,128)}, bf16[4,2,8,64,128]{4,3,2,1,0:T(8,128)(2,1)}, f32[4,64,160]{2,1,0:T(8,128)S(1)}, bf16[4,64,160]{2,1,0:T(8,128)(2,1)S(1)}) custom-call(s32[20]{0:T(128)S(1)} %pad_add_fusion.1.place_ref, bf16[72,2048]{1,0:T(8,128)(2,1)} %copy-done.23, bf16[72,2048]{1,0:T(8,128)(2,1)} %copy-done.30, ...), custom_call_target="tpu_custom_call" | custom-call | bytes 28800000 | tf_op jit(solution)/shard_map/project/pallas_call | solution.py:579
  82.8 4.5 %collective-permute-done.10 = bf16[4,64,160]{2,1,0:T(8,128)(2,1)S(1)} collective-permute-done((bf16[4,64,160]{2,1,0:T(8,128)(2,1)S(1)}, bf16[4,64,160]{2,1,0:T(8,128)(2,1)S(1)}, u32[]{:S(2)}, u32[]{:S(2)}) %collective-permute-start.10) | collective-permute-done | bytes 81952 | tf_op jit(solution)/shard_map/ppermute | solution.py:918
  87.3 7.7 %collective-permute-start.11 = (bf16[4,64,160]{2,1,0:T(8,128)(2,1)S(1)}, bf16[4,64,160]{2,1,0:T(8,128)(2,1)S(1)}, u32[]{:S(2)}, u32[]{:S(2)}) collective-permute-start(bf16[4,64,160]{2,1,0:T(8,128)(2,1)S(1)} %add_convert_fusion.7), channel_id=1, source_target_pairs={{0,8},{4,12},{8,16},{12,20},{16,24},{20,28},{24,0},{28,4},{1,9},{5... | collective-permute-start | bytes 245768 | tf_op jit(solution)/shard_map/ppermute | solution.py:921
  97.6 3.5 all-to-all-start.1
  101.1 5.7 %pull.1 = (bf16[512,2048]{1,0:T(8,128)(2,1)}, bf16[8,64,128]{2,1,0:T(8,128)(2,1)}, bf16[8,64,128]{2,1,0:T(8,128)(2,1)}, bf16[8,64,128]{2,1,0:T(8,128)(2,1)}, bf16[8,64,128]{2,1,0:T(8,128)(2,1)}) custom-call(s32[9]{0:T(128)S(1)} %add_convert_fusion.8.order_ref, bf16[8,64,2048]{2,1,0:T(8,128)(2,1)} %bitcast.166, bf16[512,2048]{1,0:T(8,128)(2,1)} %refs_1_.1), custom_call_target="tpu_custom_call" | custom-call | bytes 21600000 | tf_op jit(solution)/shard_map/pull/pallas_call | solution.py:652
  108.6 5.2 %collective-permute-done.14 = bf16[4,64,160]{2,1,0:T(8,128)(2,1)S(1)} collective-permute-done((bf16[4,64,160]{2,1,0:T(8,128)(2,1)S(1)}, bf16[4,64,160]{2,1,0:T(8,128)(2,1)S(1)}, u32[]{:S(2)}, u32[]{:S(2)}) %collective-permute-start.14) | collective-permute-done | bytes 81952 | tf_op jit(solution)/shard_map/ppermute | solution.py:918
  117.8 5.5 %collective-permute-done.16.refs_2_ = bf16[8,64,160]{2,1,0:T(8,128)(2,1)} collective-permute-done((bf16[8,64,160]{2,1,0:T(8,128)(2,1)S(1)}, bf16[8,64,160]{2,1,0:T(8,128)(2,1)}, u32[]{:S(2)}, u32[]{:S(2)}) %collective-permute-start.16) | collective-permute-done | bytes 163872 | tf_op jit(solution)/shard_map/ppermute | solution.py:924
  126.4 14.9 %forward_scan.1 = (bf16[32768,128]{1,0:T(8,128)(2,1)}, f32[2048,128]{1,0:T(8,128)}, bf16[4,2,8,64,128]{4,3,2,1,0:T(8,128)(2,1)}) custom-call(s32[17]{0:T(128)S(1)} %add_convert_fusion.9.order_ref, bf16[8,64,160]{2,1,0:T(8,128)(2,1)} %copy-done.22, bf16[8,64,160]{2,1,0:T(8,128)(2,1)} %collective-permute-done.15.refs_1_, ...), custom_call_target="tpu_custom_call" | custom-call | bytes 50400000 | tf_op jit(solution)/shard_map/forward_scan/pallas_call | solution.py:299
  141.3 3.5 all-to-all-start.2
  145.0 24.9 %backward_scan.1 = (bf16[2,8,80,160]{3,2,1,0:T(8,128)(2,1)}, bf16[2,8,80,160]{3,2,1,0:T(8,128)(2,1)}, bf16[4,8,80,128]{3,2,1,0:T(8,128)(2,1)}, f32[128,128]{1,0:...) custom-call(s32[17]{0:T(128)S(1)} %add_convert_fusion.9.order_ref, bf16[8,64,160]{2,1,0:T(8,128)(2,1)} %copy-done.22, ...), custom_call_target="tpu_custom_call" | custom-call | bytes 86400000 | tf_op jit(solution)/shard_map/backward_scan/pallas_call | solution.py:360
  171.5 7.9 %emit.1 = (bf16[4,64,2048]{2,1,0:T(8,128)(2,1)}, bf16[4,64,1024]{2,1,0:T(8,128)(2,1)}, bf16[4,64,1024]{2,1,0:T(8,128)(2,1)}, bf16[2,128,2048]{2,1,0:T(8,128)(2,1...) custom-call(s32[9]{0:T(128)S(1)} %add_convert_fusion.8.order_ref, bf16[4,2,8,64,128]{4,3,2,1,0:T(8,128)(2,1)} %copy-done.21, ...), custom_call_target="tpu_custom_call" | custom-call | bytes 21600000 | tf_op jit(solution)/shard_map/emit/pallas_call | solution.py:721
  179.4 4.4 %fusion.45 = (bf16[2048,512]{1,0:T(8,128)(2,1)}, f32[2048]{0:T(1024)S(1)}) fusion(bf16[2048,1024]{1,0:T(8,128)(2,1)S(1)} %bitcast.160, bf16[512,2048]{1,0:T(8,128)(2,1)} %get-tuple-element.211, bf16[512,512]{1,0:T(8,128)(2,1)} %get-tuple-element.212.refs_8_), kind=kOutput, calls=%fused_computation.174 | convolution fusion | flops 1077934080 | bytes 6823936 | tf_op jit(solution)/shard_map/dot_general | solution.py:1550
  188.8 8.0 %collective-permute-done.22 = bf16[8,80,160]{2,1,0:T(8,128)(2,1)S(1)} collective-permute-done((bf16[8,80,160]{2,1,0:T(8,128)(2,1)S(1)}, bf16[8,80,160]{2,1,0:T(8,128)(2,1)S(1)}, u32[]{:S(2)}, u32[]{:S(2)}) %collective-permute-start.22) | collective-permute-done | bytes 204832 | tf_op jit(solution)/shard_map/ppermute | solution.py:924
  206.6 3.5 all-to-all-start.3
  215.4 3.7 %collective-permute-done.27 = bf16[4,80,160]{2,1,0:T(8,128)(2,1)S(1)} collective-permute-done((bf16[4,80,160]{2,1,0:T(8,128)(2,1)S(1)}, bf16[4,80,160]{2,1,0:T(8,128)(2,1)S(1)}, u32[]{:S(2)}, u32[]{:S(2)}) %collective-permute-start.27) | collective-permute-done | bytes 102432 | tf_op jit(solution)/shard_map/ppermute | solution.py:921
  221.1 4.1 %collective-permute-done.28 = bf16[4,80,160]{2,1,0:T(8,128)(2,1)S(1)} collective-permute-done((bf16[4,80,160]{2,1,0:T(8,128)(2,1)S(1)}, bf16[4,80,160]{2,1,0:T(8,128)(2,1)S(1)}, u32[]{:S(2)}, u32[]{:S(2)}) %collective-permute-start.28) | collective-permute-done | bytes 102432 | tf_op jit(solution)/shard_map/ppermute | solution.py:921
  234.4 3.6 %collective-permute-start.37 = (bf16[64,2048]{1,0:T(8,128)(2,1)S(1)}, bf16[64,2048]{1,0:T(8,128)(2,1)S(1)}, u32[]{:S(2)}, u32[]{:S(2)}) collective-permute-start(bf16[64,2048]{1,0:T(8,128)(2,1)S(1)} %get-tuple-element.308), channel_id=1, source_target_pairs={{0,8},{4,12},{8,16},{12,20},{16,24},{20,28},{24,0},{28,4},{1,9},{5... | collective-permute-start | bytes 786440 | tf_op jit(solution)/shard_map/ppermute | solution.py:921
  238.6 6.8 %turn_back.1 = (bf16[512,1024]{1,0:T(8,128)(2,1)S(1)}, bf16[512,128]{1,0:T(8,128)(2,1)}, f32[40,512]{1,0:T(8,128)S(1)}) custom-call(s32[9]{0:T(128)S(1)} %add_convert_fusion.8.order_ref, bf16[4,80,160]{2,1,0:T(8,128)(2,1)} %add_convert_fusion.3.refs_0_, bf16[4,80,160]{2,1,0:T(8,128)(2,1)} %collective-permute-done.32.refs_1_, ...), custom_call_target="tpu_custom_call" | custom-call | bytes 19800000 | tf_op jit(solution)/shard_map/turn_back/pallas_call | solution.py:849
  251.1 4.0 %collective-permute-done.38 = bf16[64,2048]{1,0:T(8,128)(2,1)S(1)} collective-permute-done((bf16[64,2048]{1,0:T(8,128)(2,1)S(1)}, bf16[64,2048]{1,0:T(8,128)(2,1)S(1)}, u32[]{:S(2)}, u32[]{:S(2)}) %collective-permute-start.38) | collective-permute-done | bytes 262176 | tf_op jit(solution)/shard_map/ppermute | solution.py:921
  255.1 4.2 %collective-permute-done.39 = bf16[64,2048]{1,0:T(8,128)(2,1)S(1)} collective-permute-done((bf16[64,2048]{1,0:T(8,128)(2,1)S(1)}, bf16[64,2048]{1,0:T(8,128)(2,1)S(1)}, u32[]{:S(2)}, u32[]{:S(2)}) %collective-permute-start.39) | collective-permute-done | bytes 262176 | tf_op jit(solution)/shard_map/ppermute | solution.py:921
  267.4 4.3 %placed.3 = f32[512,2048]{1,0:T(8,128)} custom-call(s32[4]{0:T(128)S(1)} %xor_convert_fusion.order_ref, bf16[128,2048]{1,0:T(8,128)(2,1)S(1)} %fusion.5.refs_0_, bf16[128,2048]{1,0:T(8,128)(2,1)} %collective-permute-done.33.refs_1_, bf16[128,2048]{1,0:T(8,128)(2,1)} %collective-permute-done.34.refs_2_, bf16[128,2048]{1,0:T(8,128)(2,1)S(1)} %collective-permute-done.35.refs_3_), custom_call_target="tpu_custom_call" | custom-call | bytes 9000000 | tf_op jit(solution)/shard_map/placed/pallas_call | solution.py:475
  274.9 4.4 %collective-permute-done.40 = bf16[4,64,1408]{2,1,0:T(8,128)(2,1)} collective-permute-done((bf16[4,64,1408]{2,1,0:T(8,128)(2,1)}, bf16[4,64,1408]{2,1,0:T(8,128)(2,1)}, u32[]{:S(2)}, u32[]{:S(2)}) %collective-permute-start.40) | collective-permute-done | bytes 720928 | tf_op jit(solution)/shard_map/ppermute | solution.py:918
  292.0 4.3 %collective-permute-done.49 = bf16[64,1408]{1,0:T(8,128)(2,1)S(1)} collective-permute-done((bf16[64,1408]{1,0:T(8,128)(2,1)S(1)}, bf16[64,1408]{1,0:T(8,128)(2,1)S(1)}, u32[]{:S(2)}, u32[]{:S(2)}) %collective-permute-start.49) | collective-permute-done | bytes 180256 | tf_op jit(solution)/shard_map/ppermute | solution.py:921
  301.9 13.1 %collective-permute-done.53 = f32[44,512]{1,0:T(8,128)S(1)} collective-permute-done((f32[44,512]{1,0:T(8,128)S(1)}, f32[44,512]{1,0:T(8,128)S(1)}, u32[]{:S(2)}, u32[]{:S(2)}) %collective-permute-start.53) | collective-permute-done | bytes 90144 | tf_op jit(solution)/shard_map/ppermute | solution.py:924
  327.6 3.1 collective-permute-start.61
  342.8 5.1 %interleave.1 = f32[2048,2,512]{2,1,0:T(2,128)} custom-call(bf16[2048,512]{1,0:T(8,128)(2,1)S(1)} %copy-done.7, bf16[2048,512]{1,0:T(8,128)(2,1)S(1)} %copy-done.6), custom_call_target="tpu_custom_call" | custom-call | bytes 18000000 | tf_op jit(solution)/shard_map/interleave/pallas_call | solution.py:448
  (352 shorter events, 137.3 us)
Async XLA Ops:
  11.2 21.7 %collective-permute-start = (bf16[72,2048]{1,0:T(8,128)(2,1)S(1)}, bf16[72,2048]{1,0:T(8,128)(2,1)S(1)}, u32[]{:S(2)}, u32[]{:S(2)}) collective-permute-start(bf16[72,2048]{1,0:T(8,128)(2,1)S(1)} %get-tuple-element.298.refs_0_), channel_id=1, source_target_pairs={{0,4},{4,0},{8,12},{12,8},{16,20},{20,16},{24,28},{28,24},{1,5},{5... | collective-permute-start | bytes 884744 | tf_op jit(solution)/shard_map/ppermute | solution.py:918
  14.2 18.7 %collective-permute-start.1 = (bf16[72,2048]{1,0:T(8,128)(2,1)S(1)}, bf16[72,2048]{1,0:T(8,128)(2,1)S(1)}, u32[]{:S(2)}, u32[]{:S(2)}) collective-permute-start(bf16[72,2048]{1,0:T(8,128)(2,1)S(1)} %get-tuple-element.298.refs_0_), channel_id=1, source_target_pairs={{0,8},{4,12},{8,16},{12,20},{16,24},{20,28},{24,0},{28,4},{1,9},{5... | collective-permute-start | bytes 884744 | tf_op jit(solution)/shard_map/ppermute | solution.py:921
  15.8 21.5 %collective-permute-start.2 = (bf16[72,2048]{1,0:T(8,128)(2,1)S(1)}, bf16[72,2048]{1,0:T(8,128)(2,1)S(1)}, u32[]{:S(2)}, u32[]{:S(2)}) collective-permute-start(bf16[72,2048]{1,0:T(8,128)(2,1)S(1)} %get-tuple-element.298.refs_0_), channel_id=1, source_target_pairs={{0,16},{4,20},{8,24},{12,28},{16,0},{20,4},{24,8},{28,12},{1,17},{... | collective-permute-start | bytes 884744 | tf_op jit(solution)/shard_map/ppermute | solution.py:921
  18.4 18.9 %collective-permute-start.3 = (bf16[72,2048]{1,0:T(8,128)(2,1)S(1)}, bf16[72,2048]{1,0:T(8,128)(2,1)}, u32[]{:S(2)}, u32[]{:S(2)}) collective-permute-start(bf16[72,2048]{1,0:T(8,128)(2,1)S(1)} %get-tuple-element.298.refs_0_), channel_id=1, source_target_pairs={{0,24},{4,28},{8,0},{12,4},{16,8},{20,12},{24,16},{28,20},{1,25},{... | collective-permute-start | bytes 884744 | tf_op jit(solution)/shard_map/ppermute | solution.py:921
  23.6 77.5 %all-gather.9.cloned.1.call-start = ((), (), s32[]{:S(2)}) async-start(), calls=%async_computation.10 | async-start | bytes 2359296 | tf_op jit(solution)/shard_map/all_gather | solution.py:1452
  46.1 18.5 %collective-permute-start.7 = (bf16[72,2048]{1,0:T(8,128)(2,1)S(1)}, bf16[72,2048]{1,0:T(8,128)(2,1)S(1)}, u32[]{:S(2)}, u32[]{:S(2)}) collective-permute-start(bf16[72,2048]{1,0:T(8,128)(2,1)S(1)} %collective-permute-done.2.refs_2_), channel_id=1, source_target_pairs={{0,4},{4,0},{8,12},{12,8},{16,20},{20,16},{24,28},{28,24},{1,5},{5... | collective-permute-start | bytes 884744 | tf_op jit(solution)/shard_map/ppermute | solution.py:918
  47.6 22.3 %collective-permute-start.8 = (bf16[72,2048]{1,0:T(8,128)(2,1)}, bf16[72,2048]{1,0:T(8,128)(2,1)S(1)}, u32[]{:S(2)}, u32[]{:S(2)}) collective-permute-start(bf16[72,2048]{1,0:T(8,128)(2,1)} %collective-permute-done.3.refs_3_), channel_id=1, source_target_pairs={{0,4},{4,0},{8,12},{12,8},{16,20},{20,16},{24,28},{28,24},{1,5},{5... | collective-permute-start | bytes 884744 | tf_op jit(solution)/shard_map/ppermute | solution.py:918
  87.3 19.5 %collective-permute-start.11 = (bf16[4,64,160]{2,1,0:T(8,128)(2,1)S(1)}, bf16[4,64,160]{2,1,0:T(8,128)(2,1)S(1)}, u32[]{:S(2)}, u32[]{:S(2)}) collective-permute-start(bf16[4,64,160]{2,1,0:T(8,128)(2,1)S(1)} %add_convert_fusion.7), channel_id=1, source_target_pairs={{0,8},{4,12},{8,16},{12,20},{16,24},{20,28},{24,0},{28,4},{1,9},{5... | collective-permute-start | bytes 245768 | tf_op jit(solution)/shard_map/ppermute | solution.py:921
  97.6 26.3 %all-to-all-start.1 = ((bf16[4,2,8,64,128]{4,3,2,1,0:T(8,128)(2,1)}), bf16[4,2,8,64,128]{4,3,2,1,0:T(8,128)(2,1)S(1)}, u32[]{:S(2)}, u32[]{:S(2)}) async-start(bf16[4,2,8,64,128]{4,3,2,1,0:T(8,128)(2,1)} %get-tuple-element.182), calls=%async_computation.1 | async-start | bytes 2097152 | tf_op jit(solution)/shard_map/all_to_all | solution.py:927
  141.3 29.3 %all-to-all-start.2 = ((bf16[4,2,8,64,128]{4,3,2,1,0:T(8,128)(2,1)}), bf16[4,2,8,64,128]{4,3,2,1,0:T(8,128)(2,1)S(1)}, u32[]{:S(2)}, u32[]{:S(2)}) async-start(bf16[4,2,8,64,128]{4,3,2,1,0:T(8,128)(2,1)} %get-tuple-element.200), calls=%async_computation.2 | async-start | bytes 2097152 | tf_op jit(solution)/shard_map/all_to_all | solution.py:927
  144.8 87.3 %reduce-scatter.3.cloned.1.call-start = ((), (), s32[]{:S(2)}) async-start(), calls=%async_computation.6 | async-start | bytes 2621440 | tf_op jit(solution)/shard_map/reduce_scatter | solution.py:1552
  187.9 13.8 %collective-permute-start.25 = (bf16[152,128]{1,0:T(8,128)(2,1)}, bf16[152,128]{1,0:T(8,128)(2,1)S(1)}, u32[]{:S(2)}, u32[]{:S(2)}) collective-permute-start(bf16[152,128]{1,0:T(8,128)(2,1)} %pad_maximum_fusion.7), channel_id=1, source_target_pairs={{0,1},{1,0},{2,3},{3,2},{4,5},{5,4},{6,7},{7,6},{8,9},{9,8},{10,11... | collective-permute-start | bytes 116744 | tf_op jit(solution)/shard_map/ppermute | solution.py:924
  188.2 15.0 %collective-permute-start.26 = (bf16[4,64,1024]{2,1,0:T(8,128)(2,1)}, bf16[4,64,1024]{2,1,0:T(8,128)(2,1)S(1)}, u32[]{:S(2)}, u32[]{:S(2)}) collective-permute-start(bf16[4,64,1024]{2,1,0:T(8,128)(2,1)} %get-tuple-element.217), channel_id=1, source_target_pairs={{0,4},{4,0},{8,12},{12,8},{16,20},{20,16},{24,28},{28,24},{1,5},{5... | collective-permute-start | bytes 1572872 | tf_op jit(solution)/shard_map/ppermute | solution.py:918
  200.4 24.9 %collective-permute-start.31 = (bf16[128,2048]{1,0:T(8,128)(2,1)}, bf16[128,2048]{1,0:T(8,128)(2,1)}, u32[]{:S(2)}, u32[]{:S(2)}) collective-permute-start(bf16[128,2048]{1,0:T(8,128)(2,1)} %slice_bitcast_fusion.1), channel_id=1, source_target_pairs={{0,2},{1,3},{2,0},{3,1},{4,6},{5,7},{6,4},{7,5},{8,10},{9,11},{10,... | collective-permute-start | bytes 1572872 | tf_op jit(solution)/shard_map/ppermute | solution.py:924
  206.0 19.3 %collective-permute-start.30 = (bf16[4,64,1024]{2,1,0:T(8,128)(2,1)}, bf16[4,64,1024]{2,1,0:T(8,128)(2,1)}, u32[]{:S(2)}, u32[]{:S(2)}) collective-permute-start(bf16[4,64,1024]{2,1,0:T(8,128)(2,1)} %get-tuple-element.219), channel_id=1, source_target_pairs={{0,4},{4,0},{8,12},{12,8},{16,20},{20,16},{24,28},{28,24},{1,5},{5... | collective-permute-start | bytes 1572872 | tf_op jit(solution)/shard_map/ppermute | solution.py:918
  206.6 25.5 %all-to-all-start.3 = ((bf16[4,8,80,128]{3,2,1,0:T(8,128)(2,1)}), bf16[4,8,80,128]{3,2,1,0:T(8,128)(2,1)S(1)}, u32[]{:S(2)}, u32[]{:S(2)}) async-start(bf16[4,8,80,128]{3,2,1,0:T(8,128)(2,1)} %get-tuple-element.225), calls=%async_computation.3 | async-start | bytes 1310720 | tf_op jit(solution)/shard_map/all_to_all | solution.py:927
  210.1 69.3 %all-gather.5.cloned.1.call-start = ((), (), s32[]{:S(2)}) async-start(), calls=%async_computation.7 | async-start | bytes 2621440 | tf_op jit(solution)/shard_map/all_gather | solution.py:1579
  210.2 15.0 %collective-permute-start.28 = (bf16[4,80,160]{2,1,0:T(8,128)(2,1)S(1)}, bf16[4,80,160]{2,1,0:T(8,128)(2,1)S(1)}, u32[]{:S(2)}, u32[]{:S(2)}) collective-permute-start(bf16[4,80,160]{2,1,0:T(8,128)(2,1)S(1)} %add_convert_fusion.4), channel_id=1, source_target_pairs={{0,16},{4,20},{8,24},{12,28},{16,0},{20,4},{24,8},{28,12},{1,17},{... | collective-permute-start | bytes 307208 | tf_op jit(solution)/shard_map/ppermute | solution.py:921
  219.2 28.2 %collective-permute-start.36 = (bf16[152,128]{1,0:T(8,128)(2,1)}, bf16[152,128]{1,0:T(8,128)(2,1)}, u32[]{:S(2)}, u32[]{:S(2)}) collective-permute-start(bf16[152,128]{1,0:T(8,128)(2,1)} %pad_maximum_fusion.7), channel_id=1, source_target_pairs={{0,2},{1,3},{2,0},{3,1},{4,6},{5,7},{6,4},{7,5},{8,10},{9,11},{10,... | collective-permute-start | bytes 116744 | tf_op jit(solution)/shard_map/ppermute | solution.py:924
  228.8 20.4 %collective-permute-start.34 = (bf16[128,2048]{1,0:T(8,128)(2,1)S(1)}, bf16[128,2048]{1,0:T(8,128)(2,1)}, u32[]{:S(2)}, u32[]{:S(2)}) collective-permute-start(bf16[128,2048]{1,0:T(8,128)(2,1)S(1)} %fusion.5.refs_0_), channel_id=1, source_target_pairs={{0,2},{1,3},{2,0},{3,1},{4,6},{5,7},{6,4},{7,5},{8,10},{9,11},{10,... | collective-permute-start | bytes 1572872 | tf_op jit(solution)/shard_map/ppermute | solution.py:924
  230.9 28.5 %collective-permute-start.33 = (bf16[128,2048]{1,0:T(8,128)(2,1)S(1)}, bf16[128,2048]{1,0:T(8,128)(2,1)}, u32[]{:S(2)}, u32[]{:S(2)}) collective-permute-start(bf16[128,2048]{1,0:T(8,128)(2,1)S(1)} %fusion.5.refs_0_), channel_id=1, source_target_pairs={{0,1},{1,0},{2,3},{3,2},{4,5},{5,4},{6,7},{7,6},{8,9},{9,8},{10,11... | collective-permute-start | bytes 1572872 | tf_op jit(solution)/shard_map/ppermute | solution.py:924
  232.1 85.0 %reduce-scatter.5.cloned.1.call-start = ((), (), s32[]{:S(2)}) async-start(), calls=%async_computation.8 | async-start | bytes 2621440 | tf_op jit(solution)/shard_map/reduce_scatter | solution.py:1637
  234.4 16.7 %collective-permute-start.37 = (bf16[64,2048]{1,0:T(8,128)(2,1)S(1)}, bf16[64,2048]{1,0:T(8,128)(2,1)S(1)}, u32[]{:S(2)}, u32[]{:S(2)}) collective-permute-start(bf16[64,2048]{1,0:T(8,128)(2,1)S(1)} %get-tuple-element.308), channel_id=1, source_target_pairs={{0,8},{4,12},{8,16},{12,20},{16,24},{20,28},{24,0},{28,4},{1,9},{5... | collective-permute-start | bytes 786440 | tf_op jit(solution)/shard_map/ppermute | solution.py:921
  238.1 17.1 %collective-permute-start.38 = (bf16[64,2048]{1,0:T(8,128)(2,1)S(1)}, bf16[64,2048]{1,0:T(8,128)(2,1)S(1)}, u32[]{:S(2)}, u32[]{:S(2)}) collective-permute-start(bf16[64,2048]{1,0:T(8,128)(2,1)S(1)} %get-tuple-element.307), channel_id=1, source_target_pairs={{0,16},{4,20},{8,24},{12,28},{16,0},{20,4},{24,8},{28,12},{1,17},{... | collective-permute-start | bytes 786440 | tf_op jit(solution)/shard_map/ppermute | solution.py:921
  261.2 18.1 %collective-permute-start.40 = (bf16[4,64,1408]{2,1,0:T(8,128)(2,1)}, bf16[4,64,1408]{2,1,0:T(8,128)(2,1)}, u32[]{:S(2)}, u32[]{:S(2)}) collective-permute-start(bf16[4,64,1408]{2,1,0:T(8,128)(2,1)} %bitcast.23), channel_id=1, source_target_pairs={{0,4},{4,0},{8,12},{12,8},{16,20},{20,16},{24,28},{28,24},{1,5},{5... | collective-permute-start | bytes 2162696 | tf_op jit(solution)/shard_map/ppermute | solution.py:918
  271.7 16.4 %collective-permute-start.47 = (bf16[152,128]{1,0:T(8,128)(2,1)}, bf16[152,128]{1,0:T(8,128)(2,1)S(1)}, u32[]{:S(2)}, u32[]{:S(2)}) collective-permute-start(bf16[152,128]{1,0:T(8,128)(2,1)} %collective-permute-done.36), channel_id=1, source_target_pairs={{0,1},{1,0},{2,3},{3,2},{4,5},{5,4},{6,7},{7,6},{8,9},{9,8},{10,11... | collective-permute-start | bytes 116744 | tf_op jit(solution)/shard_map/ppermute | solution.py:924
  279.4 61.8 %all-gather.7.cloned.1.call-start = ((), (), s32[]{:S(2)}) async-start(), calls=%async_computation.9 | async-start | bytes 2621440 | tf_op jit(solution)/shard_map/all_gather | solution.py:1677
  281.7 14.7 %collective-permute-start.49 = (bf16[64,1408]{1,0:T(8,128)(2,1)S(1)}, bf16[64,1408]{1,0:T(8,128)(2,1)S(1)}, u32[]{:S(2)}, u32[]{:S(2)}) collective-permute-start(bf16[64,1408]{1,0:T(8,128)(2,1)S(1)} %get-tuple-element.310), channel_id=1, source_target_pairs={{0,16},{4,20},{8,24},{12,28},{16,0},{20,4},{24,8},{28,12},{1,17},{... | collective-permute-start | bytes 540680 | tf_op jit(solution)/shard_map/ppermute | solution.py:921
  282.5 13.9 %collective-permute-start.50 = (bf16[64,1408]{1,0:T(8,128)(2,1)S(1)}, bf16[64,1408]{1,0:T(8,128)(2,1)S(1)}, u32[]{:S(2)}, u32[]{:S(2)}) collective-permute-start(bf16[64,1408]{1,0:T(8,128)(2,1)S(1)} %get-tuple-element.309), channel_id=1, source_target_pairs={{0,24},{4,28},{8,0},{12,4},{16,8},{20,12},{24,16},{28,20},{1,25},{... | collective-permute-start | bytes 540680 | tf_op jit(solution)/shard_map/ppermute | solution.py:921
  296.8 18.2 %collective-permute-start.51 = (bf16[64,2048]{1,0:T(8,128)(2,1)S(1)}, bf16[64,2048]{1,0:T(8,128)(2,1)S(1)}, u32[]{:S(2)}, u32[]{:S(2)}) collective-permute-start(bf16[64,2048]{1,0:T(8,128)(2,1)S(1)} %multiply_convert_fusion.1.refs_0_), channel_id=1, source_target_pairs={{0,2},{1,3},{2,0},{3,1},{4,6},{5,7},{6,4},{7,5},{8,10},{9,11},{10,... | collective-permute-start | bytes 786440 | tf_op jit(solution)/shard_map/ppermute | solution.py:924
  297.9 17.8 %collective-permute-start.52 = (bf16[64,2048]{1,0:T(8,128)(2,1)S(1)}, bf16[64,2048]{1,0:T(8,128)(2,1)S(1)}, u32[]{:S(2)}, u32[]{:S(2)}) collective-permute-start(bf16[64,2048]{1,0:T(8,128)(2,1)S(1)} %multiply_convert_fusion.1.refs_0_), channel_id=1, source_target_pairs={{0,1},{1,0},{2,3},{3,2},{4,5},{5,4},{6,7},{7,6},{8,9},{9,8},{10,11... | collective-permute-start | bytes 786440 | tf_op jit(solution)/shard_map/ppermute | solution.py:924
  300.2 14.8 %collective-permute-start.53 = (f32[44,512]{1,0:T(8,128)S(1)}, f32[44,512]{1,0:T(8,128)S(1)}, u32[]{:S(2)}, u32[]{:S(2)}) collective-permute-start(f32[44,512]{1,0:T(8,128)S(1)} %add.258), channel_id=1, source_target_pairs={{0,2},{1,3},{2,0},{3,1},{4,6},{5,7},{6,4},{7,5},{8,10},{9,11},{10,... | collective-permute-start | bytes 270344 | tf_op jit(solution)/shard_map/ppermute | solution.py:924
  (98 other events, 978.5 us)
Sparse Core Ops, SparseCore 0:
  37.4 57.6 all-gather.8
  183.9 40.9 reduce-scatter.2
  232.2 24.1 all-gather.4
  279.5 37.6 reduce-scatter.4
  318.6 22.5 all-gather.6
where the time goes:
time: 356 us; the launch traced here: 354 us
  waiting for transfers between devices  102 us (29%)
  starting transfers between devices  88 us (25%)
  Pallas kernels  84.3 us (24%)
  other arithmetic  28.3 us (8%)
  local copies, waits for them, and re-layouts  24.7 us (7%)
  between operations  14.8 us (4%)
  matrix products  12.3 us (3%)
    ppermute x13, waiting for transfers between devices, over_y(): return lax.ppermute(values, 'chan', [(i, i ^ 1) for i in range(8)])  40.8 us
    ppermute x21, starting transfers between devices, over_z(): lax.ppermute(values, 'chan', [(i, (i + 2 * hops) % 8) for i in range(8)])  39.2 us
    ppermute x29, waiting for transfers between devices, over_state(): return lax.ppermute(values, 'state', [(i, i ^ bits) for i in range(4)])  31.3 us
    pallas_call x1, Pallas kernels, backward_scan(): pl.pallas_call(functools.partial(backward_body, parts), grid_spec=pltpu.P...  24.9 us
    ppermute x21, waiting for transfers between devices, over_z(): lax.ppermute(values, 'chan', [(i, (i + 2 * hops) % 8) for i in range(8)])  24.8 us
    ppermute x29, starting transfers between devices, over_state(): return lax.ppermute(values, 'state', [(i, i ^ bits) for i in range(4)])  20 us
    pallas_call x1, Pallas kernels, forward_scan(): pl.pallas_call(functools.partial(forward_body, parts), grid_spec=pltpu.Pr...  14.9 us
    ppermute x13, starting transfers between devices, over_y(): return lax.ppermute(values, 'chan', [(i, i ^ 1) for i in range(8)])  14.6 us
  transfers between devices with their start and end apart: 72, of which 25 were waited for; matrix products, arithmetic and copies ran while one was open for 14% of the time, Pallas kernels for 18%

commit v1 on v0

--- a/solution.py
+++ b/solution.py
@@ -34,9 +34,220 @@
     return places - opening
 
 
+def delayed(values, amount):
+    if amount == 0:
+        return values
+    padding = jnp.zeros((amount,) + values.shape[1:], values.dtype)
+    return jnp.concatenate([padding, values[: values.shape[0] - amount]], axis=0)
+
+
+def advanced(values, amount):
+    if amount == 0:
+        return values
+    padding = jnp.zeros((amount,) + values.shape[1:], values.dtype)
+    return jnp.concatenate([values[amount:], padding], axis=0)
+
+
 def silu_slope(values):
     logistic = jax.nn.sigmoid(values)
     return logistic * (1.0 + values * (1.0 - logistic))
+
+
+def linear_scan(decays, drive):
+    total_rows = decays.shape[0]
+    blocks = total_rows // 16
+    factors = jnp.swapaxes(decays.reshape((blocks, 16) + decays.shape[1:]), 0, 1)
+    sources = jnp.swapaxes(drive.reshape((blocks, 16) + drive.shape[1:]), 0, 1)
+
+    def advance(totals, item):
+        state_now, product_now = totals
+        factor_now, source_now = item
+        state_now = factor_now * state_now + source_now
+        product_now = factor_now * product_now
+        return ((state_now, product_now), (state_now, product_now))
+
+    initial = (jnp.zeros(factors.shape[1:], jnp.float32), jnp.ones(factors.shape[1:], jnp.float32))
+    final_pair, (local_states, products) = lax.scan(advance, initial, (factors, sources))
+
+    def combine(early, later):
+        return (early[0] * later[0], later[0] * early[1] + later[1])
+
+    joined_factor, joined_state = lax.associative_scan(
+        combine, (products[-1], local_states[-1]), axis=0
+    )
+    entering = jnp.concatenate([jnp.zeros_like(joined_state[:1]), joined_state[:-1]], axis=0)
+    states = local_states + products * entering[None]
+    return jnp.swapaxes(states, 0, 1).reshape(decays.shape)
+
+
+def shards(
+    hidden_in,
+    norm_gain,
+    in_weight,
+    conv_kernel,
+    conv_offset,
+    select_rank,
+    select_entry,
+    select_read,
+    delta_weight,
+    step_bias,
+    decay_log,
+    skip_weight,
+    out_weight,
+    lengths,
+    pad_mask,
+    cotangent,
+):
+    rows_dev, width = hidden_in.shape
+    tokens_all = pad_mask.shape[0]
+    chans = in_weight.shape[2]
+    kernel_len = conv_kernel.shape[0]
+    per_state = select_entry.shape[1]
+    contract_rows = (((0,), (0,)), ((), ()))
+    contract_cols = (((1,), (1,)), ((), ()))
+    place = positions(lengths, tokens_all)
+    fresh = (place > 0).astype(jnp.float32)
+    maskf = pad_mask.astype(jnp.float32)[:, None]
+    square = jnp.mean(hidden_in * hidden_in, axis=1, keepdims=True)
+    inv_rms = lax.rsqrt(square + epsilon)
+    scaled = hidden_in * inv_rms
+    normed = (scaled * norm_gain[None, :]).astype(jnp.bfloat16)
+    in_flat = in_weight.reshape(width, 2 * chans)
+    both = jnp.dot(
+        lax.all_gather(normed, "chan", axis=0, tiled=True),
+        in_flat,
+        preferred_element_type=jnp.float32,
+    )
+    inner = both[:, :chans] * maskf
+    gate_in = both[:, chans:]
+    valids = []
+    shifted = []
+    conv = jnp.zeros((tokens_all, chans), jnp.float32) + conv_offset[None, :]
+    for index in range(kernel_len):
+        lag = kernel_len - 1 - index
+        valids.append((place >= lag).astype(jnp.float32)[:, None])
+        shifted.append(delayed(inner, lag))
+        conv = conv + conv_kernel[index][None, :] * shifted[index] * valids[index]
+    act = (jax.nn.silu(conv) * maskf).astype(jnp.bfloat16)
+    act_wide = act.astype(jnp.float32)
+    pair_map = jnp.concatenate([select_entry, select_read], axis=1)
+    rank_part = jnp.dot(act, select_rank, preferred_element_type=jnp.float32)
+    pair_part = jnp.dot(act, pair_map, preferred_element_type=jnp.float32)
+    raw_sum, pair_sum = lax.psum((rank_part, pair_part), "chan")
+    entry = pair_sum[:, :per_state]
+    readout = pair_sum[:, per_state:]
+    lowrank = raw_sum.astype(jnp.bfloat16)
+    dpre = jnp.dot(lowrank, delta_weight, preferred_element_type=jnp.float32) + step_bias[None, :]
+    delta = jax.nn.softplus(dpre)
+    coeff = -jnp.exp(decay_log)
+    decays = jnp.exp(delta[:, None, :] * coeff[None]) * fresh[:, None, None]
+    drive = (delta * act_wide)[:, None, :] * entry[:, :, None]
+    states = linear_scan(decays, drive)
+    scan_part = jnp.sum(readout[:, :, None] * states, axis=1)
+    scanned = lax.psum(scan_part, "state")
+    mixed = scanned + skip_weight[None, :] * act_wide
+    gate_act = jax.nn.silu(gate_in)
+    gated = (mixed * gate_act).astype(jnp.bfloat16)
+    gated_rows = gated
+    branch = lax.psum_scatter(
+        jnp.dot(gated_rows, out_weight, preferred_element_type=jnp.float32),
+        "chan",
+        scatter_dimension=0,
+        tiled=True,
+    )
+    result = hidden_in + branch
+    grad_low = cotangent.astype(jnp.bfloat16)
+    pieces = lax.all_gather(grad_low, "chan", axis=0, tiled=True)
+    gated_rows = gated
+    product = lax.dot_general(pieces, out_weight, contract_cols, preferred_element_type=jnp.float32)
+    outw_acc = lax.dot_general(
+        gated_rows, pieces, contract_rows, preferred_element_type=jnp.float32
+    )
+    dmix = product * gate_act
+    dgate = product * mixed * silu_slope(gate_in)
+    skip_grad = jnp.sum(dmix * act_wide, axis=0)
+    emitted = readout[:, :, None] * dmix[:, None, :]
+    following = jnp.concatenate([decays[1:], jnp.zeros_like(decays[:1])], axis=0)
+    adjoint = jnp.flip(linear_scan(jnp.flip(following, 0), jnp.flip(emitted, 0)), 0)
+    earlier = jnp.concatenate([jnp.zeros_like(states[:1]), states[:-1]], axis=0)
+    flow = adjoint * earlier * decays
+    dread_part = jnp.sum(states * dmix[:, None, :], axis=2)
+    dentry_part = jnp.sum(adjoint * (delta * act_wide)[:, None, :], axis=2)
+    ddelta_part = jnp.sum(
+        flow * coeff[None] + adjoint * entry[:, :, None] * act_wide[:, None, :], axis=1
+    )
+    decay_grad = coeff * jnp.sum(flow * delta[:, None, :], axis=0)
+    dact_scan = jnp.sum(adjoint * entry[:, :, None], axis=1) * delta
+    dentry_sum, dread_sum = lax.psum((dentry_part, dread_part), "chan")
+    dpair = jnp.concatenate(
+        [dentry_sum.astype(jnp.bfloat16), dread_sum.astype(jnp.bfloat16)], axis=1
+    )
+    pair_grad = lax.dot_general(act, dpair, contract_rows, preferred_element_type=jnp.float32)
+    entry_grad = pair_grad[:, :per_state]
+    read_grad = pair_grad[:, per_state:]
+    dact_pair = lax.dot_general(dpair, pair_map, contract_cols, preferred_element_type=jnp.float32)
+    dact_state, ddelta = lax.psum((dact_scan + dact_pair, ddelta_part), "state")
+    ddpre = (ddelta * jax.nn.sigmoid(dpre)).astype(jnp.bfloat16)
+    bias_grad = jnp.sum(ddpre.astype(jnp.float32), axis=0)
+    delta_grad = lax.dot_general(lowrank, ddpre, contract_rows, preferred_element_type=jnp.float32)
+    dlow_part = lax.dot_general(
+        ddpre, delta_weight, contract_cols, preferred_element_type=jnp.float32
+    )
+    dlow = lax.psum(dlow_part, "chan").astype(jnp.bfloat16)
+    rank_grad = lax.dot_general(act, dlow, contract_rows, preferred_element_type=jnp.float32)
+    dact = (
+        dact_state
+        + dmix * skip_weight[None, :]
+        + lax.dot_general(dlow, select_rank, contract_cols, preferred_element_type=jnp.float32)
+    )
+    dconv = dact * maskf * silu_slope(conv)
+    offset_grad = jnp.sum(dconv, axis=0)
+    kernel_rows = []
+    dinner = jnp.zeros((tokens_all, chans), jnp.float32)
+    for index in range(kernel_len):
+        lag = kernel_len - 1 - index
+        masked = dconv * valids[index]
+        kernel_rows.append(jnp.sum(masked * shifted[index], axis=0))
+        dinner = dinner + advanced(masked * conv_kernel[index][None, :], lag)
+    kernel_grad = jnp.stack(kernel_rows, axis=0)
+    dboth = jnp.concatenate([dinner * maskf, dgate], axis=1).astype(jnp.bfloat16)
+    chosen = dboth
+    in_flat_grad = lax.dot_general(
+        lax.all_gather(normed, "chan", axis=0, tiled=True),
+        chosen,
+        contract_rows,
+        preferred_element_type=jnp.float32,
+    )
+    in_grad = in_flat_grad.reshape(width, 2, chans)
+    chosen = dboth
+    dnormed = lax.psum_scatter(
+        lax.dot_general(chosen, in_flat, contract_cols, preferred_element_type=jnp.float32),
+        "chan",
+        scatter_dimension=0,
+        tiled=True,
+    )
+    gain_part = jnp.sum(dnormed * scaled, axis=0)
+    gain_grad = lax.psum(gain_part, "chan")
+    dscaled = dnormed * norm_gain[None, :]
+    input_grad = cotangent + inv_rms * (
+        dscaled - scaled * jnp.mean(dscaled * scaled, axis=1, keepdims=True)
+    )
+    return (
+        result,
+        input_grad,
+        gain_grad,
+        in_grad,
+        kernel_grad,
+        offset_grad,
+        rank_grad,
+        entry_grad,
+        read_grad,
+        delta_grad,
+        bias_grad,
+        decay_grad,
+        skip_grad,
+        outw_acc,
+    )
 
 
 def own_block(states):
@@ -66,19 +277,82 @@
     return lax.dot_general(eye, values, (((1,), (1,)), ((), ())), preferred_element_type=wide)
 
 
-def forward_body(
+def forward_body(parts, order_ref, *refs):
+    sources, refs = refs[: 2 * parts + 2], refs[2 * parts + 2 :]
+    params, (kept_hbm, dpre_hbm, gated_hbm), refs = refs[:5], refs[5:8], refs[8:]
+    carry, step_all, drive_all, small_all, dgated_all, pair_all, fresh_all = refs[:7]
+    kept_all, dpre_all, gated_all, came, left = refs[7:]
+    blocks = small_all.shape[1]
+    chunk = step_all.shape[0]
+    states = carry.shape[0]
+
+    def entering(turn):
+        block = order_ref[turn]
+        rows = pl.ds(pl.multiple_of(turn * chunk, chunk), chunk)
+        found = []
+        for k in range(parts):
+            found.append((sources[k].at[order_ref[blocks + turn]], small_all.at[k, turn]))
+            found.append((sources[parts + k].at[block], dgated_all.at[k, turn]))
+        found.append((sources[2 * parts].at[:, :, block], pair_all.at[:, :, turn]))
+        found.append((sources[2 * parts + 1].at[rows], fresh_all.at[rows]))
+        return [
+            pltpu.make_async_copy(a, b, came.at[turn, i]) for i, (a, b) in enumerate(found)
+        ]
+
+    def leaving(turn):
+        rows = pl.ds(pl.multiple_of(turn * chunk, chunk), chunk)
+        tall = pl.ds(pl.multiple_of(turn * (chunk * states), chunk * states), chunk * states)
+        found = [
+            (kept_all.at[tall], kept_hbm.at[tall]),
+            (dpre_all.at[rows], dpre_hbm.at[rows]),
+            (gated_all.at[:, :, turn], gated_hbm.at[:, :, order_ref[turn]]),
+        ]
+        return [
+            pltpu.make_async_copy(a, b, left.at[turn, i]) for i, (a, b) in enumerate(found)
+        ]
+
+    @pl.loop(0, blocks)
+    def _(turn):
+        for copy in entering(turn):
+            copy.start()
+
+    carry[...] = jnp.zeros_like(carry)
+
+    @pl.loop(0, blocks)
+    def _(turn):
+        for copy in entering(turn):
+            copy.wait()
+        forward_steps(
+            turn,
+            parts,
+            order_ref,
+            small_all,
+            dgated_all,
+            pair_all,
+            fresh_all,
+            *params,
+            kept_all,
+            dpre_all,
+            gated_all,
+            carry,
+            step_all,
+            drive_all,
+        )
+        for copy in leaving(turn):
+            copy.start()
+
+    @pl.loop(0, blocks)
+    def _(turn):
+        for copy in leaving(turn):
+            copy.wait()
+
+
+def forward_steps(
+    turn,
     parts,
     order_ref,
-    *refs,
-):
-    small_refs, dgated_refs, refs = refs[:parts], refs[parts : 2 * parts], refs[2 * parts :]
-    forward_steps(order_ref, small_refs, dgated_refs, *refs)
-
-
-def forward_steps(
-    order_ref,
-    small_refs,
-    dgated_refs,
+    small_all,
+    dgated_all,
     pair_ref,
     fresh_ref,
     weight_ref,
@@ -88,201 +362,323 @@
     spread_ref,
     kept_ref,
     dpre_ref,
-    *rest,
+    gated_ref,
+    carry,
+    step_all,
+    drive_all,
 ):
-    parts = len(small_refs)
-    gated_ref, carry, step_all, drive_all, mixed_all, small_all, dgated_all = rest
-
-    @pl.when(pl.program_id(0) == 0)
-    def _():
-        carry[...] = jnp.zeros_like(carry)
-
     coeff = coeff_ref[...]
     states = coeff.shape[0]
+    chunk = step_all.shape[0]
+    origin = pl.multiple_of(turn * (chunk * states), chunk * states)
     rank = weight_ref.shape[0]
-    length = dpre_ref.shape[0]
-    quarter = length // parts
+    quarter = small_all.shape[2]
     chosen = own_block(states)
     part = order_ref[order_ref.shape[0] - 1]
+    columns = [None] * parts
+    reading = [None] * parts
+
+    def before(j):
+        rows = slice(j * quarter, (j + 1) * quarter)
+        small = small_all[part ^ j, turn]
+        dpre = (
+            jnp.dot(small[:, :rank], weight_ref[...], preferred_element_type=wide) + bias_ref[...]
+        )
+        dpre_ref[pl.ds(turn * chunk + j * quarter, quarter), :] = dpre
+        delta = jax.nn.softplus(dpre)
+        step_all[rows, :] = jnp.where(fresh_ref[pl.ds(turn * chunk + j * quarter, quarter), :].astype(wide) > 0.0, delta, FAR)
+        drive_all[rows, :] = delta * pair_ref[j, 0, turn].astype(wide)
+        pair = small[:, rank:]
+        columns[j] = transposed(pair)
+        reading[j] = jnp.dot(
+            pair, spread_ref[:, GROUP * states :], preferred_element_type=wide
+        )
+
+    def scan(j, state):
+        for group in range(quarter // GROUP):
+            base = j * quarter + group * GROUP
+            kept = []
+            for t in range(base, base + GROUP):
+                here = t - j * quarter
+                decay = jnp.exp2(step_all[t : t + 1, :] * coeff)
+                entry = columns[j][:states, here : here + 1]
+                state = decay * state + drive_all[t : t + 1, :] * entry
+                kept.append(state)
+            rows = pl.ds(origin + base * states, GROUP * states)
+            kept_ref[rows, :] = jnp.concatenate(kept, axis=0).astype(low)
+        return state
+
+    def finish_part(j):
+        found = []
+        for group in range(quarter // GROUP):
+            base = j * quarter + group * GROUP
+            block = kept_ref[pl.ds(origin + base * states, GROUP * states), :]
+            here = reading[j][group * GROUP : (group + 1) * GROUP]
+            weights = jnp.where(chosen, here, 0.0).astype(low)
+            found.append(jnp.dot(weights, block, preferred_element_type=wide))
+        act = pair_ref[j, 0, turn].astype(wide)
+        gate = pair_ref[j, 1, turn].astype(wide)
+        mixed = jnp.concatenate(found, axis=0) + skip_ref[...] * act
+        dgated = dgated_all[part ^ j, turn].astype(wide)
+        gated_ref[j, 0, turn] = (mixed * jax.nn.silu(gate)).astype(low)
+        gated_ref[j, 1, turn] = (dgated * mixed * silu_slope(gate)).astype(low)
+
+    state = carry[...]
+    before(0)
     for j in range(parts):
-        small_all[j] = small_refs[j][0]
-    small = jnp.concatenate([small_all[part ^ j] for j in range(parts)], axis=0)
-    act = jnp.concatenate([pair_ref[j, 0, 0] for j in range(parts)], axis=0).astype(wide)
-    gate = jnp.concatenate([pair_ref[j, 1, 0] for j in range(parts)], axis=0).astype(wide)
-    dpre = jnp.dot(small[:, :rank], weight_ref[...], preferred_element_type=wide) + bias_ref[...]
-    dpre_ref[...] = dpre
-    delta = jax.nn.softplus(dpre)
-    step_all[...] = jnp.where(fresh_ref[...] > 0.0, delta, FAR)
-    drive_all[...] = delta * act
-    pair = small[:, rank:]
-    columns = transposed(pair)
-    reading = jnp.dot(pair, spread_ref[:, GROUP * states :], preferred_element_type=wide)
-    state = carry[...]
-    for group in range(length // GROUP):
-        base = group * GROUP
-        kept = []
-        for t in range(base, base + GROUP):
-            decay = jnp.exp2(step_all[t : t + 1, :] * coeff)
-            state = decay * state + drive_all[t : t + 1, :] * columns[:states, t : t + 1]
-            kept.append(state)
-        kept_ref[base * states : (base + GROUP) * states, :] = jnp.concatenate(
-            kept, axis=0
-        ).astype(low)
+        if j + 1 < parts:
+            before(j + 1)
+        state = scan(j, state)
+        if j:
+            finish_part(j - 1)
+    finish_part(parts - 1)
     carry[...] = state
-    for group in range(length // GROUP):
-        here = slice(group * GROUP, (group + 1) * GROUP)
-        block = kept_ref[group * GROUP * states : (group + 1) * GROUP * states, :]
-        weights = jnp.where(chosen, reading[here], 0.0).astype(low)
-        mixed_all[here, :] = jnp.dot(weights, block, preferred_element_type=wide)
-    mixed = mixed_all[...] + skip_ref[...] * act
-    for j in range(parts):
-        dgated_all[j] = dgated_refs[j][0]
-    dgated = jnp.concatenate([dgated_all[part ^ j] for j in range(parts)], axis=0).astype(wide)
-    gated = (mixed * jax.nn.silu(gate)).astype(low)
-    dgate = (dgated * mixed * silu_slope(gate)).astype(low)
-    for j in range(parts):
-        gated_ref[j, 0, 0] = gated[j * quarter : (j + 1) * quarter]
-        gated_ref[j, 1, 0] = dgate[j * quarter : (j + 1) * quarter]
-
-
-def backward_body(
+
+
+def backward_body(parts, order_ref, *refs):
+    sources, refs = refs[: 2 * parts + 4], refs[2 * parts + 4 :]
+    params, (own_hbm, other_hbm, dscan_hbm), refs = refs[:4], refs[4:7], refs[7:]
+    results, refs = refs[:3], refs[3:]
+    scratch, refs = refs[:11], refs[11:]
+    (small_all, dgated_all, pair_all, fresh_all, dpre_all, kept_all, edge_all) = refs[:7]
+    (own_all, other_all, dscan_all, came, left) = refs[7:]
+    blocks = small_all.shape[1]
+    chunk = scratch[1].shape[0]
+    states = scratch[0].shape[0]
+    for ref in (scratch[0], *results, *scratch[8:10]):
+        ref[...] = jnp.zeros_like(ref)
+
+    def entering(turn):
+        at = blocks - 1 - turn
+        block = order_ref[at]
+        rows = pl.ds(pl.multiple_of(at * chunk, chunk), chunk)
+        tall = pl.ds(pl.multiple_of(at * (chunk * states), chunk * states), chunk * states)
+        found = []
+        for k in range(parts):
+            found.append((sources[k].at[order_ref[blocks + at]], small_all.at[k, at]))
+            found.append((sources[parts + k].at[block], dgated_all.at[k, at]))
+        found.append((sources[2 * parts].at[:, :, block], pair_all.at[:, :, at]))
+        for source, target, here in zip(
+            sources[2 * parts + 1 :], (fresh_all, dpre_all, kept_all), (rows, rows, tall)
+        ):
+            found.append((source.at[here], target.at[here]))
+        ahead = pl.multiple_of(jnp.maximum(at * (chunk * states) - states, 0), states)
+        found.append((sources[-1].at[pl.ds(ahead, states)], edge_all.at[at]))
+        return [
+            pltpu.make_async_copy(a, b, came.at[turn, i]) for i, (a, b) in enumerate(found)
+        ]
+
+    def leaving(turn):
+        at = blocks - 1 - turn
+        block = order_ref[at]
+        place = order_ref[blocks + at]
+        found = [
+            (own_all.at[:, at], own_hbm.at[:, place]),
+            (other_all.at[:, at], other_hbm.at[:, place]),
+            (dscan_all.at[:, at], dscan_hbm.at[:, block]),
+        ]
+        return [
+            pltpu.make_async_copy(a, b, left.at[turn, i]) for i, (a, b) in enumerate(found)
+        ]
+
+    @pl.loop(0, blocks)
+    def _(turn):
+        for copy in entering(turn):
+            copy.start()
+
+    @pl.loop(0, blocks)
+    def _(turn):
+        for copy in entering(turn):
+            copy.wait()
+        backward_steps(
+            turn,
+            parts,
+            blocks,
+            order_ref,
+            small_all,
+            dgated_all,
+            pair_all,
+            fresh_all,
+            dpre_all,
+            kept_all,
+            edge_all,
+            *params,
+            own_all,
+            other_all,
+            dscan_all,
+            *results,
+            *scratch,
+        )
+        for copy in leaving(turn):
+            copy.start()
+
+    @pl.loop(0, blocks)
+    def _(turn):
+        for copy in leaving(turn):
+            copy.wait()
+
+
+def backward_steps(
+    turn,
     parts,
+    blocks,
     order_ref,
-    *refs,
-):
-    small_refs, dgated_refs, refs = refs[:parts], refs[parts : 2 * parts], refs[2 * parts :]
-    backward_steps(order_ref, small_refs, dgated_refs, *refs)
-
-
-def backward_steps(
-    order_ref,
-    small_refs,
-    dgated_refs,
+    small_all,
+    dgated_all,
     pair_ref,
     fresh_ref,
     dpre_ref,
     kept_ref,
-    before_ref,
+    edge_ref,
     weight_ref,
     skip_ref,
     coeff_ref,
     spread_ref,
-    *rest,
+    own_ref,
+    other_ref,
+    dscan_ref,
+    delta_grad_ref,
+    decay_ref,
+    sums_ref,
+    carry,
+    step_all,
+    drive_all,
+    delta_all,
+    dmix_all,
+    lam_all,
+    flow_all,
+    cross_all,
+    next_partial,
+    next_dscan,
+    partial_all,
 ):
-    parts = len(small_refs)
-    own_ref, other_ref, dscan_ref = rest[:3]
-    rest = rest[3:]
-    (delta_grad_ref, decay_ref, sums_ref) = rest[:3]
-    (carry, step_all, drive_all, delta_all, dmix_all, lam_all, flow_all) = rest[3:10]
-    (lam_sum, flow_sum, cross_all, next_partial, next_dscan, small_all) = rest[10:16]
-    (partial_all, dgated_all) = rest[16:]
-    turn = pl.program_id(0)
-
-    @pl.when(turn == 0)
-    def _():
-        carry[...] = jnp.zeros_like(carry)
-        delta_grad_ref[...] = jnp.zeros_like(delta_grad_ref)
-        decay_ref[...] = jnp.zeros_like(decay_ref)
-        sums_ref[...] = jnp.zeros_like(sums_ref)
-        next_partial[...] = jnp.zeros_like(next_partial)
-        next_dscan[...] = jnp.zeros_like(next_dscan)
-
     coeff = coeff_ref[...]
     states = coeff.shape[0]
     rank = weight_ref.shape[0]
-    length = dpre_ref.shape[0]
-    quarter = length // parts
-    spread = spread_ref[...]
+    quarter = small_all.shape[2]
     chosen = own_block(states)
+    ones = jnp.where(chosen, 1.0, 0.0).astype(low)
     across = (((1,), (1,)), ((), ()))
     down = (((0,), (0,)), ((), ()))
     part = order_ref[order_ref.shape[0] - 1]
-    for j in range(parts):
-        small_all[j] = small_refs[j][0]
-    small = jnp.concatenate([small_all[part ^ j] for j in range(parts)], axis=0)
-    act = jnp.concatenate([pair_ref[j, 0, 0] for j in range(parts)], axis=0).astype(wide)
-    gate = jnp.concatenate([pair_ref[j, 1, 0] for j in range(parts)], axis=0).astype(wide)
-    for j in range(parts):
-        dgated_all[j] = dgated_refs[j][0]
-    dgated = jnp.concatenate([dgated_all[part ^ j] for j in range(parts)], axis=0).astype(wide)
-    dpre = dpre_ref[...]
-    delta = jax.nn.softplus(dpre)
-    dmix = dgated * jax.nn.silu(gate)
-    step_all[...] = jnp.where(fresh_ref[...] > 0.0, delta, FAR)
-    drive_all[...] = delta * act
-    delta_all[...] = delta
-    dmix_all[...] = dmix
-    pair = small[:, rank:]
-    columns = transposed(pair)
-    entering = jnp.dot(pair, spread[:, : GROUP * states], preferred_element_type=wide)
-    first = jnp.where(turn == pl.num_programs(0) - 1, 0.0, before_ref[...].astype(wide))
+    chunk = step_all.shape[0]
+    block_turn = blocks - 1 - turn
+    origin = pl.multiple_of(block_turn * (chunk * states), chunk * states)
+    first = jnp.where(block_turn == 0, 0.0, edge_ref[block_turn].astype(wide))
+    columns = [None] * parts
+    entering = [None] * parts
+    after_partial = [next_partial[...]]
+    after_dscan = [next_dscan[...]]
+
+    def before(j):
+        rows = slice(j * quarter, (j + 1) * quarter)
+        small = small_all[part ^ j, block_turn]
+        delta = jax.nn.softplus(dpre_ref[pl.ds(block_turn * chunk + j * quarter, quarter), :])
+        act = pair_ref[j, 0, block_turn].astype(wide)
+        gate = pair_ref[j, 1, block_turn].astype(wide)
+        step_all[rows, :] = jnp.where(fresh_ref[pl.ds(block_turn * chunk + j * quarter, quarter), :].astype(wide) > 0.0, delta, FAR)
+        drive_all[rows, :] = delta * act
+        delta_all[rows, :] = delta
+        dmix_all[rows, :] = dgated_all[part ^ j, block_turn].astype(wide) * jax.nn.silu(gate)
+        pair = small[:, rank:]
+        columns[j] = transposed(pair)
+        entering[j] = jnp.dot(
+            pair, spread_ref[:, : GROUP * states], preferred_element_type=wide
+        )
+
+    def scan(j, pulled, summed):
+        for group in range(quarter // GROUP - 1, -1, -1):
+            base = j * quarter + group * GROUP
+            lams = [None] * GROUP
+            flows = [None] * GROUP
+            rows = slice(base * states, (base + GROUP) * states)
+            block = kept_ref[pl.ds(origin + base * states, GROUP * states), :].astype(wide)
+            if base:
+                edge = kept_ref[pl.ds(origin + (base - 1) * states, states), :].astype(wide)
+            else:
+                edge = first
+            for i in range(GROUP - 1, -1, -1):
+                t = base + i
+                here = t - j * quarter
+                read = columns[j][states:, here : here + 1]
+                lam = read * dmix_all[t : t + 1, :] + pulled
+                pulled = jnp.exp2(step_all[t : t + 1, :] * coeff) * lam
+                flow = pulled * (block[(i - 1) * states : i * states] if i else edge)
+                summed = summed + flow * delta_all[t : t + 1, :]
+                lams[i] = lam
+                flows[i] = flow * coeff
+            lam_all[rows, :] = jnp.concatenate(lams, axis=0).astype(low)
+            flow_all[rows, :] = jnp.concatenate(flows, axis=0).astype(low)
+        return pulled, summed
+
+    def finish_part(j):
+        part_rows = slice(j * quarter, (j + 1) * quarter)
+        lam_found = []
+        flow_found = []
+        for group in range(quarter // GROUP):
+            base = j * quarter + group * GROUP
+            here = slice(base, base + GROUP)
+            rows = slice(base * states, (base + GROUP) * states)
+            lam_block = lam_all[rows, :]
+            entry = entering[j][group * GROUP : (group + 1) * GROUP]
+            weights = jnp.where(chosen, entry, 0.0).astype(low)
+            lam_found.append(jnp.dot(weights, lam_block, preferred_element_type=wide))
+            flow_found.append(jnp.dot(ones, flow_all[rows, :], preferred_element_type=wide))
+            cross = lax.dot_general(
+                drive_all[here, :].astype(low), lam_block, across, preferred_element_type=wide
+            )
+            cross_all[here, : GROUP * states] = jnp.where(chosen, cross, 0.0).astype(low)
+            cross = lax.dot_general(
+                dmix_all[here, :].astype(low),
+                kept_ref[pl.ds(origin + base * states, GROUP * states), :],
+                across,
+                preferred_element_type=wide,
+            )
+            cross_all[here, GROUP * states :] = jnp.where(chosen, cross, 0.0).astype(low)
+        dpair = lax.dot_general(
+            cross_all[part_rows, :], spread_ref[...], across, preferred_element_type=wide
+        ).astype(low)
+        found = jnp.concatenate(lam_found, axis=0)
+        act = pair_ref[j, 0, block_turn].astype(wide)
+        delta = delta_all[part_rows, :]
+        dmix = dmix_all[part_rows, :]
+        ddelta = jnp.concatenate(flow_found, axis=0) * (1.0 / math.log2(math.e)) + found * act
+        ddpre = (ddelta * jax.nn.sigmoid(dpre_ref[pl.ds(block_turn * chunk + j * quarter, quarter), :])).astype(low)
+        small = small_all[part ^ j, block_turn]
+        delta_grad_ref[...] += lax.dot_general(
+            small[:, :rank], ddpre, down, preferred_element_type=wide
+        )
+        dlow = lax.dot_general(
+            ddpre, weight_ref[...], across, preferred_element_type=wide
+        ).astype(low)
+        dscan = (found * delta + dmix * skip_ref[...]).astype(low)
+        sums_ref[0:1, :] += jnp.sum(ddpre.astype(wide), axis=0, keepdims=True)
+        sums_ref[1:2, :] += jnp.sum(dmix * act, axis=0, keepdims=True)
+        after_rows = after_partial[0]
+        partial_all[j, :quarter, :rank] = dlow
+        partial_all[j, :quarter, rank:] = dpair
+        partial_all[j, quarter:, :] = after_rows
+        dscan_ref[j, block_turn, :quarter, :] = dscan
+        dscan_ref[j, block_turn, quarter:, :] = after_dscan[0]
+        after_partial[0] = jnp.concatenate([dlow[:TAIL], dpair[:TAIL]], axis=1)
+        after_dscan[0] = dscan[:TAIL]
+
     pulled = carry[...]
     summed = decay_ref[...]
-    for group in range(length // GROUP - 1, -1, -1):
-        base = group * GROUP
-        lams = [None] * GROUP
-        flows = [None] * GROUP
-        rows = slice(base * states, (base + GROUP) * states)
-        block = kept_ref[rows, :].astype(wide)
-        if group:
-            edge = kept_ref[(base - 1) * states : base * states, :].astype(wide)
-        else:
-            edge = first
-        for i in range(GROUP - 1, -1, -1):
-            t = base + i
-            lam = columns[states:, t : t + 1] * dmix_all[t : t + 1, :] + pulled
-            pulled = jnp.exp2(step_all[t : t + 1, :] * coeff) * lam
-            flow = pulled * (block[(i - 1) * states : i * states] if i else edge)
-            summed = summed + flow * delta_all[t : t + 1, :]
-            lams[i] = lam
-            flows[i] = flow * coeff
-        lam_all[rows, :] = jnp.concatenate(lams, axis=0).astype(low)
-        flow_all[rows, :] = jnp.concatenate(flows, axis=0).astype(low)
+    before(parts - 1)
+    for j in range(parts - 1, -1, -1):
+        if j:
+            before(j - 1)
+        pulled, summed = scan(j, pulled, summed)
+        if j + 1 < parts:
+            finish_part(j + 1)
+    finish_part(0)
     carry[...] = pulled
     decay_ref[...] = summed
-    ones = jnp.where(chosen, 1.0, 0.0).astype(low)
-    for group in range(length // GROUP):
-        here = slice(group * GROUP, (group + 1) * GROUP)
-        rows = slice(group * GROUP * states, (group + 1) * GROUP * states)
-        lam_block = lam_all[rows, :]
-        weights = jnp.where(chosen, entering[here], 0.0).astype(low)
-        lam_sum[here, :] = jnp.dot(weights, lam_block, preferred_element_type=wide)
-        flow_sum[here, :] = jnp.dot(ones, flow_all[rows, :], preferred_element_type=wide)
-        cross = lax.dot_general(
-            drive_all[here, :].astype(low), lam_block, across, preferred_element_type=wide
-        )
-        cross_all[here, : GROUP * states] = jnp.where(chosen, cross, 0.0).astype(low)
-        cross = lax.dot_general(
-            dmix_all[here, :].astype(low), kept_ref[rows, :], across, preferred_element_type=wide
-        )
-        cross_all[here, GROUP * states :] = jnp.where(chosen, cross, 0.0).astype(low)
-    dpair = lax.dot_general(cross_all[...], spread, across, preferred_element_type=wide)
-    scale = 1.0 / math.log2(math.e)
-    found = lam_sum[...]
-    ddelta = flow_sum[...] * scale + found * act
-    ddpre = (ddelta * jax.nn.sigmoid(dpre)).astype(low)
-    delta_grad_ref[...] += lax.dot_general(
-        small[:, :rank], ddpre, down, preferred_element_type=wide
-    )
-    dlow = lax.dot_general(ddpre, weight_ref[...], across, preferred_element_type=wide)
-    dscan = (found * delta + dmix * skip_ref[...]).astype(low)
-    sums_ref[0:1, :] += jnp.sum(ddpre.astype(wide), axis=0, keepdims=True)
-    sums_ref[1:2, :] += jnp.sum(dmix * act, axis=0, keepdims=True)
-    for value, store, after, span in (
-        (dlow.astype(low), partial_all, next_partial, slice(0, rank)),
-        (dpair.astype(low), partial_all, next_partial, slice(rank, rank + 2 * states)),
-        (dscan, dscan_ref, next_dscan, slice(0, dscan.shape[1])),
-    ):
-        longer = jnp.concatenate([value, after[:, span]], axis=0)
-        for j in range(parts):
-            window = longer[j * quarter : (j + 1) * quarter + TAIL]
-            if store is dscan_ref:
-                store[j, 0] = window
-            else:
-                store[j, :, span] = window
-        after[:, span] = value[:TAIL]
+    next_partial[...] = after_partial[0]
+    next_dscan[...] = after_dscan[0]
     for k in range(parts):
-        (other_ref if k % 2 else own_ref)[k // 2, 0] = partial_all[part ^ k]
+        (other_ref if k % 2 else own_ref)[k // 2, block_turn] = partial_all[part ^ k]
 
 
 def forward_scan(order, small, pair, dgated, fresh, weight, bias, skip, coeff, spread):
@@ -291,56 +687,43 @@
     columns = small[0].shape[-1]
     chunk = parts * quarter
     tokens = blocks * chunk
-
-    def whole(values):
-        return pl.BlockSpec(values.shape, lambda t, order: (0, 0))
-
-    row = pl.BlockSpec((chunk, width), lambda t, order: (t, 0))
+    streamed = (*small, *dgated, pair, fresh)
+    params = (weight, bias, skip, coeff, spread)
+    apart = pl.BlockSpec(memory_space=pl.ANY)
+    kept = (tokens * states, width)
+    gated = (parts, 2, blocks, quarter, width)
     return pl.pallas_call(
         functools.partial(forward_body, parts),
         grid_spec=pltpu.PrefetchScalarGridSpec(
             num_scalar_prefetch=1,
-            grid=(blocks,),
-            in_specs=[
-                pl.BlockSpec((1, quarter, columns), lambda t, order: (order[blocks + t], 0, 0))
-                for _ in range(parts)
-            ]
-            + [
-                pl.BlockSpec((1, quarter, width), lambda t, order: (order[t], 0, 0))
-                for _ in range(parts)
-            ]
-            + [
-                pl.BlockSpec(
-                    (parts, 2, 1, quarter, width), lambda t, order: (0, 0, order[t], 0, 0)
-                ),
-                pl.BlockSpec((chunk, 1), lambda t, order: (t, 0)),
-            ]
-            + [whole(v) for v in (weight, bias, skip, coeff, spread)],
-            out_specs=[
-                pl.BlockSpec((chunk * states, width), lambda t, order: (t, 0)),
-                row,
-                pl.BlockSpec(
-                    (parts, 2, 1, quarter, width), lambda t, order: (0, 0, order[t], 0, 0)
-                ),
-            ],
+            grid=(1,),
+            in_specs=[apart] * len(streamed)
+            + [pl.BlockSpec(v.shape, lambda t, order: (0, 0)) for v in params],
+            out_specs=[apart] * 3,
             scratch_shapes=[
                 pltpu.VMEM((states, width), wide),
                 pltpu.VMEM((chunk, width), wide),
                 pltpu.VMEM((chunk, width), wide),
-                pltpu.VMEM((chunk, width), wide),
-                pltpu.VMEM((parts, quarter, columns), low),
-                pltpu.VMEM((parts, quarter, width), low),
+                pltpu.VMEM((parts, blocks, quarter, columns), low),
+                pltpu.VMEM((parts, blocks, quarter, width), low),
+                pltpu.VMEM(gated, low),
+                pltpu.VMEM((tokens, width), low),
+                pltpu.VMEM(kept, low),
+                pltpu.VMEM((tokens, width), wide),
+                pltpu.VMEM(gated, low),
+                pltpu.SemaphoreType.DMA((blocks, len(streamed) + 1)),
+                pltpu.SemaphoreType.DMA((blocks, 3)),
             ],
         ),
         out_shape=[
-            pltpu.HBM((tokens * states, width), low),
+            pltpu.HBM(kept, low),
             pltpu.HBM((tokens, width), wide),
-            pltpu.HBM((parts, 2, blocks, quarter, width), low),
+            pltpu.HBM(gated, low),
         ],
-        compiler_params=pltpu.CompilerParams(vmem_limit_bytes=16 * 1024 * 1024),
-        cost_estimate=spent(14),
+        compiler_params=pltpu.CompilerParams(vmem_limit_bytes=28 * 1024 * 1024),
+        cost_estimate=spent(12),
         name="forward_scan",
-    )(order, *map(in_hbm, (*small, *dgated, pair, fresh, weight, bias, skip, coeff, spread)))
+    )(order, *map(in_hbm, streamed), *params)
 
 
 def backward_scan(
@@ -351,89 +734,49 @@
     rank = weight.shape[0]
     columns = small[0].shape[-1]
     chunk = parts * quarter
-    last = blocks - 1
-
-    def whole(shape):
-        return pl.BlockSpec(shape, lambda t, order: (0, 0))
-
-    row = pl.BlockSpec((chunk, width), lambda t, order: (last - t, 0))
+    tokens = blocks * chunk
+    streamed = (*small, *dgated, pair, fresh, dpre, kept)
+    params = (weight, skip, coeff, spread)
+    apart = pl.BlockSpec(memory_space=pl.ANY)
+    sums = (parts // 2, blocks, quarter + TAIL, columns)
+    dscan = (parts, blocks, quarter + TAIL, width)
+    results = ((rank, width), (states, width), (8, width))
     return pl.pallas_call(
         functools.partial(backward_body, parts),
         grid_spec=pltpu.PrefetchScalarGridSpec(
             num_scalar_prefetch=1,
-            grid=(blocks,),
-            in_specs=[
-                pl.BlockSpec(
-                    (1, quarter, columns), lambda t, order: (order[blocks + last - t], 0, 0)
-                )
-                for _ in range(parts)
-            ]
-            + [
-                pl.BlockSpec((1, quarter, width), lambda t, order: (order[last - t], 0, 0))
-                for _ in range(parts)
-            ]
-            + [
-                pl.BlockSpec(
-                    (parts, 2, 1, quarter, width),
-                    lambda t, order: (0, 0, order[last - t], 0, 0),
-                ),
-                pl.BlockSpec((chunk, 1), lambda t, order: (last - t, 0)),
-                row,
-                pl.BlockSpec((chunk * states, width), lambda t, order: (last - t, 0)),
-                pl.BlockSpec(
-                    (states, width),
-                    lambda t, order: (jnp.maximum((last - t) * chunk - 1, 0), 0),
-                ),
-            ]
-            + [whole(v.shape) for v in (weight, skip, coeff, spread)],
-            out_specs=[
-                pl.BlockSpec(
-                    (parts // 2, 1, quarter + TAIL, columns),
-                    lambda t, order: (0, order[blocks + last - t], 0, 0),
-                )
-                for _ in range(2)
-            ]
-            + [
-                pl.BlockSpec(
-                    (parts, 1, quarter + TAIL, width),
-                    lambda t, order: (0, order[last - t], 0, 0),
-                ),
-                whole((rank, width)),
-                whole((states, width)),
-                whole((8, width)),
-            ],
+            grid=(1,),
+            in_specs=[apart] * len(streamed)
+            + [pl.BlockSpec(v.shape, lambda t, order: (0, 0)) for v in params],
+            out_specs=[apart] * 3 + [pl.BlockSpec(v, lambda t, order: (0, 0)) for v in results],
             scratch_shapes=[pltpu.VMEM((states, width), wide)]
             + [pltpu.VMEM((chunk, width), wide)] * 4
             + [pltpu.VMEM((chunk * states, width), low)] * 2
-            + [pltpu.VMEM((chunk, width), wide)] * 2
             + [
                 pltpu.VMEM((chunk, 2 * GROUP * states), low),
                 pltpu.VMEM((TAIL, columns), low),
                 pltpu.VMEM((TAIL, width), low),
-                pltpu.VMEM((parts, quarter, columns), low),
                 pltpu.VMEM((parts, quarter + TAIL, columns), low),
-                pltpu.VMEM((parts, quarter, width), low),
+                pltpu.VMEM((parts, blocks, quarter, columns), low),
+                pltpu.VMEM((parts, blocks, quarter, width), low),
+                pltpu.VMEM(pair.shape, low),
+                pltpu.VMEM((tokens, width), low),
+                pltpu.VMEM((tokens, width), wide),
+                pltpu.VMEM((tokens * states, width), low),
+                pltpu.VMEM((blocks, states, width), low),
+                pltpu.VMEM(sums, low),
+                pltpu.VMEM(sums, low),
+                pltpu.VMEM(dscan, low),
+                pltpu.SemaphoreType.DMA((blocks, len(streamed) + 1)),
+                pltpu.SemaphoreType.DMA((blocks, 3)),
             ],
         ),
-        out_shape=[
-            pltpu.HBM((parts // 2, blocks, quarter + TAIL, columns), low)
-            for _ in range(2)
-        ]
-        + [
-            pltpu.HBM((parts, blocks, quarter + TAIL, width), low),
-            jax.ShapeDtypeStruct((rank, width), wide),
-            jax.ShapeDtypeStruct((states, width), wide),
-            jax.ShapeDtypeStruct((8, width), wide),
-        ],
-        compiler_params=pltpu.CompilerParams(vmem_limit_bytes=16 * 1024 * 1024),
-        cost_estimate=spent(24),
+        out_shape=[pltpu.HBM(sums, low), pltpu.HBM(sums, low), pltpu.HBM(dscan, low)]
+        + [jax.ShapeDtypeStruct(v, wide) for v in results],
+        compiler_params=pltpu.CompilerParams(vmem_limit_bytes=28 * 1024 * 1024),
+        cost_estimate=spent(19),
         name="backward_scan",
-    )(
-        order,
-        *map(
-            in_hbm, (*small, *dgated, pair, fresh, dpre, kept, kept, weight, skip, coeff, spread)
-        ),
-    )
+    )(order, *map(in_hbm, streamed), *params)
 
 
 def interleave_body(inner_ref, gate_ref, out_ref):
@@ -676,7 +1019,7 @@
     (weight_ref, rows_ref, kept_ref, first_ref, second_ref, own_ref, other_ref) = refs[:7]
     (dgate_ref, gated, product) = refs[7:]
     turn = pl.program_id(0)
-    half = pl.num_programs(0) // 2
+    half = pl.num_programs(0) // 4
     count, quarter, width = pieces_ref.shape[2:]
 
     @pl.when(pl.program_id(0) == 0)
@@ -715,7 +1058,7 @@
     parts, _, count, quarter, width = pieces.shape
     depth = weight.shape[1]
     tile = 512
-    half = depth // tile // 2
+    half = depth // tile // 4
     chans = parts * width
     tall = count * quarter
     return pl.pallas_call(
@@ -744,8 +1087,8 @@
         ),
         out_shape=[
             pltpu.HBM((count // 2, quarter, depth), low),
-            pltpu.HBM((count // 2, quarter, depth // 2), low),
-            pltpu.HBM((count // 2, quarter, depth // 2), low),
+            pltpu.HBM((count // 2, quarter, half * tile), low),
+            pltpu.HBM((count // 2, quarter, depth - half * tile), low),
             pltpu.HBM((parts // 2, width, depth), low),
             pltpu.HBM((parts // 2, width, depth), low),
             pltpu.HBM((tall, chans), low),
@@ -896,23 +1239,16 @@
 
 
 class Moves:
-    def __init__(self, n_chan, n_state):
-        self.n_chan = n_chan
-        self.n_state = n_state
-        self.near = (n_chan, n_state) == (8, 4)
+    def __init__(self):
         self.chan = lax.axis_index("chan").astype(jnp.uint32)
         self.part = lax.axis_index("state").astype(jnp.uint32)
         self.z = self.chan // 2
         self.y = self.chan % 2
-        places = jnp.arange(n_chan, dtype=jnp.uint32)
-        if self.near:
-            planes = (self.z + 4 - places % 4) % 4
-            self.blocks = planes * 2 + (self.y + places // 4) % 2
-            hops = (self.z + 4 - places // 2) % 4
-            self.order = (self.y + places) % 2 * 4 + hops
-        else:
-            self.blocks = places
-            self.order = places
+        places = jnp.arange(8, dtype=jnp.uint32)
+        planes = (self.z + 4 - places % 4) % 4
+        self.blocks = planes * 2 + (self.y + places // 4) % 2
+        hops = (self.z + 4 - places // 2) % 4
+        self.order = (self.y + places) % 2 * 4 + hops
 
     def over_y(self, values):
         return lax.ppermute(values, "chan", [(i, i ^ 1) for i in range(8)])
@@ -941,113 +1277,6 @@
         across = self.over_state(values, 2)
         return values, core, across, self.over_state(across, 1)
 
-    def gather_state(self, values):
-        if not self.near:
-            return lax.all_gather(values, "state", axis=0)
-        return self.in_order(self.pieces_state(values))
-
-    def gather_near(self, values):
-        if not self.near:
-            found = lax.all_gather(values, "state", axis=0)
-            return [
-                lax.dynamic_index_in_dim(found, self.part ^ k, 0, keepdims=False)
-                for k in range(self.n_state)
-            ]
-        return list(self.pieces_state(values))
-
-    def trade_state(self, values):
-        if not self.near:
-            return self.swap_state(values)
-        chosen = [
-            lax.dynamic_index_in_dim(values, self.part ^ k, 0, keepdims=False) for k in range(4)
-        ]
-        moved = [chosen[0]] + [self.over_state(chosen[k], k) for k in (1, 2, 3)]
-        return self.in_order(moved)
-
-    def pieces_chan(self, values):
-        own = self.over_y(values)
-        along = [self.over_z(values, hops) for hops in (1, 2, 3)]
-        own, along[0] = tied(own, along[0])
-        return [values] + along + [own] + [self.over_y(piece) for piece in along]
-
-    def gather_chan(self, values):
-        if not self.near:
-            return lax.all_gather(values, "chan", axis=0)
-        return jnp.stack(self.pieces_chan(values))
-
-    def gather_rows(self, values, cut):
-        if not self.near:
-            found = lax.all_gather(values, "chan", axis=0)
-            return found[:, :cut].reshape(-1, values.shape[1]), found[:, cut:]
-        pieces = self.pieces_chan(values)
-        first = jnp.concatenate([piece[:cut] for piece in pieces], axis=0)
-        return first, jnp.stack([piece[cut:] for piece in pieces])
-
-    def in_axis_order(self, values):
-        if not self.near:
-            return values
-        return jnp.stack(
-            [
-                lax.dynamic_index_in_dim(values, self.order[k], 0, keepdims=False)
-                for k in range(self.n_chan)
-            ]
-        )
-
-    def gather_small(self, values):
-        if not self.near:
-            return lax.all_gather(values, "chan", axis=0)
-        copies = jnp.broadcast_to(values[None], (self.n_chan,) + values.shape)
-        return lax.all_to_all(copies, "chan", 0, 0, tiled=True)
-
-    def sum_small(self, parts):
-        moved = lax.all_to_all(parts, "chan", 0, 0, tiled=True)
-        return jnp.sum(moved.astype(wide), axis=0)
-
-    def joined_planes(self, kept, sent):
-        return kept + self.over_y(sent).astype(wide)
-
-    def summed_planes(self, joined):
-        total = joined[0]
-        for hops in (1, 2, 3):
-            total = total + self.over_z(joined[4 - hops].astype(low), hops).astype(wide)
-        return total
-
-    def sum_planes(self, kept, sent):
-        return self.summed_planes(self.joined_planes(kept, sent))
-
-    def sum_chan(self, parts):
-        if not self.near:
-            return self.sum_small(parts.astype(low))
-        return self.sum_planes(parts[:4], parts[4:].astype(low))
-
-    def sum_row(self, values):
-        if not self.near:
-            return lax.psum(values, "chan")
-        both = values + self.over_y(values)
-        total = both
-        for hops in (1, 2, 3):
-            total = total + self.over_z(both, hops)
-        return total
-
-    def sum_state(self, parts):
-        if not self.near:
-            moved = lax.all_to_all(parts, "state", 0, 0, tiled=True)
-            return jnp.sum(moved.astype(wide), axis=0).astype(low)
-        cut = parts.reshape((2, 2) + parts.shape[1:])
-        core = self.part % 2
-        sent = lax.dynamic_index_in_dim(cut, 1 - core, 1, keepdims=False)
-        kept = lax.dynamic_index_in_dim(cut, core, 1, keepdims=False)
-        chip = (kept.astype(wide) + self.over_state(sent, 1).astype(wide)).astype(low)
-        side = self.part // 2
-        sent = lax.dynamic_index_in_dim(chip, 1 - side, 0, keepdims=False)
-        kept = lax.dynamic_index_in_dim(chip, side, 0, keepdims=False)
-        return (kept.astype(wide) + self.over_state(sent, 2).astype(wide)).astype(low)
-
-    def total_state(self, values):
-        rows, columns = values.shape
-        parts = values.reshape(self.n_state, rows // self.n_state, columns)
-        return self.gather_state(self.sum_state(parts)).reshape(rows, columns)
-
 
 def tied(*values):
     return lax.optimization_barrier(values)
@@ -1056,294 +1285,6 @@
 def after(values, *others):
     token = lax.optimization_barrier((lax.create_token(), others))[0]
     return lax.optimization_barrier((token, values))[1]
-
-
-def shards(
-    n_chan,
-    n_state,
-    hidden_in,
-    norm_gain,
-    in_weight,
-    conv_kernel,
-    conv_offset,
-    select_rank,
-    select_entry,
-    select_read,
-    delta_weight,
-    step_bias,
-    decay_log,
-    skip_weight,
-    out_weight,
-    lengths,
-    pad_mask,
-    cotangent,
-):
-    rows_dev, width = hidden_in.shape
-    tokens = pad_mask.shape[0]
-    chans = in_weight.shape[2]
-    taps = conv_kernel.shape[0]
-    rank = select_rank.shape[1]
-    per_state = select_entry.shape[1]
-    states = per_state * n_state
-    small = rank + 2 * states
-    quarter = rows_dev // n_state
-    own = chans // n_state
-    rows_q = n_chan * quarter
-    part = lax.axis_index("state").astype(jnp.uint32)
-    contract_rows = (((0,), (0,)), ((), ()))
-    contract_cols = (((1,), (1,)), ((), ()))
-    moves = Moves(n_chan, n_state)
-    blocks = moves.blocks
-    order = jnp.concatenate([moves.order, moves.order, part[None]]).astype(jnp.int32)
-
-    def mine(values, axis=0):
-        return lax.dynamic_slice_in_dim(values, part * own, own, axis)
-
-    def in_axis(pieces):
-        stacked = jnp.stack(pieces)
-        return jnp.stack(
-            [
-                lax.dynamic_index_in_dim(stacked, part ^ j, 0, keepdims=False)
-                for j in range(n_state)
-            ]
-        )
-
-    def split_own(values):
-        cut = values.reshape(values.shape[:-1] + (n_state, own))
-        return jnp.moveaxis(cut, -2, 0)
-
-    def join_own(values):
-        moved = jnp.moveaxis(values, 0, -2)
-        return moved.reshape(moved.shape[:-2] + (chans,))
-
-    def chosen_rows(chooser, values):
-        flat = values.reshape(values.shape[0], -1)
-        found = jnp.dot(chooser, flat, precision=lax.Precision.HIGHEST)
-        return found.reshape(values.shape)
-
-    start = part * quarter
-    hidden_q = lax.dynamic_slice_in_dim(hidden_in, start, quarter, 0)
-    ahead = (start + (rows_dev - HALO)) % rows_dev
-    behind = (start + quarter) % rows_dev
-    local = jnp.concatenate(
-        [
-            hidden_q,
-            lax.dynamic_slice_in_dim(hidden_in, ahead, HALO, 0),
-            lax.dynamic_slice_in_dim(hidden_in, behind, HALO, 0),
-        ],
-        axis=0,
-    )
-    inv_all = lax.rsqrt(jnp.mean(local * local, axis=1, keepdims=True) + epsilon)
-    scaled_all = local * inv_all
-    normed_all = (scaled_all * norm_gain[None, :]).astype(low)
-    inv_rms = inv_all[:quarter]
-    scaled = scaled_all[:quarter]
-    normed_q, normed_side = moves.gather_rows(normed_all, quarter)
-    cot_q = lax.dynamic_slice_in_dim(cotangent, start, quarter, 0).astype(low)
-    grad_q = lax.all_gather(cot_q, "chan", axis=0)
-
-    place = positions(lengths, tokens)
-    flags = [pad_mask.astype(wide)]
-    flags += [(place >= lag).astype(wide) for lag in range(1, taps)]
-    flags = jnp.stack(flags)
-    padded = jnp.pad(flags, ((0, 0), (HALO, HALO + rows_dev)))
-    span = quarter + 2 * HALO
-    flags_win = lax.dynamic_slice_in_dim(padded, start, n_chan * rows_dev, 1)
-    flags_win = flags_win.reshape(taps, n_chan, rows_dev)[:, :, :span]
-    chooser = (blocks[:, None] == jnp.arange(n_chan)[None, :]).astype(wide)
-    flags_win = jnp.einsum("kb,fbr->fkr", chooser, flags_win)
-    mask_win = flags_win[0][:, :, None]
-    valid_win = flags_win[1:]
-    one_before = (blocks[:, None] - 1 == blocks[None, :]).astype(wide)
-    one_after = (blocks[:, None] + 1 == blocks[None, :]).astype(wide)
-    itself = jnp.eye(n_chan, dtype=wide)
-    one_before = jnp.where(part == 0, one_before, itself)
-    one_after = jnp.where(part == n_state - 1, one_after, itself)
-
-    def valid_at(lag, first, count):
-        if lag == 0:
-            return 1.0
-        return valid_win[lag - 1][:, first : first + count, None]
-
-    columns = jnp.concatenate([select_entry, select_read], axis=1)
-    columns = moves.gather_state(columns).reshape(n_state, chans, 2, per_state)
-    columns = jnp.transpose(columns, (1, 2, 0, 3)).reshape(chans, 2 * states)
-    select = jnp.concatenate([select_rank, columns], axis=1)
-    decay_own = moves.swap_state(jnp.swapaxes(decay_log.reshape(per_state, n_state, own), 0, 1))
-    coeff = -jnp.exp(decay_own.reshape(states, own))
-
-    in_flat = lax.optimization_barrier(in_weight.reshape(width, 2 * chans))
-    both = jnp.dot(normed_q, in_flat, preferred_element_type=wide)
-    both = both.reshape(n_chan, quarter, 2 * chans)
-    gate_q = both[:, :, chans:].astype(low)
-    sides = jnp.dot(
-        normed_side.reshape(-1, width), in_flat[:, :chans], preferred_element_type=wide
-    ).reshape(n_chan, 2 * HALO, chans)
-    before = chosen_rows(one_before, sides[:, :HALO])
-    after = chosen_rows(one_after, sides[:, HALO:])
-    inner_win = jnp.concatenate([before, both[:, :, :chans], after], axis=1) * mask_win
-
-    reach = quarter + HALO
-    conv_win = conv_offset
-    for index in range(taps):
-        lag = taps - 1 - index
-        shifted = inner_win[:, HALO - lag : HALO - lag + reach]
-        conv_win = conv_win + conv_kernel[index] * shifted * valid_at(lag, HALO, reach)
-    act_win = jax.nn.silu(conv_win[:, :quarter]) * mask_win[:, HALO : HALO + quarter]
-    act_win = act_win.astype(low)
-    act_q = act_win.reshape(rows_q, chans)
-
-    partial = jnp.dot(act_q, select, preferred_element_type=wide)
-    summed = moves.sum_chan(partial.reshape(n_chan, quarter, small)).astype(low)
-    sent = jnp.stack([split_own(act_win), split_own(gate_q)], axis=1)
-    channels = moves.swap_state(sent)
-    summed, channels = tied(summed, channels)
-    picked = moves.gather_near(moves.gather_small(summed))
-
-    if moves.near:
-        grad_q = jnp.concatenate(
-            [lax.dynamic_index_in_dim(grad_q, blocks[k], 0, keepdims=False) for k in range(8)],
-            axis=0,
-        )
-    grad_q = grad_q.reshape(rows_q, width)
-    dgated_q = lax.dot_general(grad_q, out_weight, contract_cols, preferred_element_type=wide)
-    dgated_q = dgated_q.astype(low).reshape(n_chan, quarter, chans)
-    dgated = list(in_axis(list(moves.swap_state(split_own(dgated_q)))))
-
-    weight_own = mine(delta_weight, 1)
-    bias_own = mine(step_bias)[None, :]
-    skip_own = mine(skip_weight)[None, :]
-    fresh = (place > 0).astype(wide)[:, None]
-    spread = spreading(states)
-    coeff_two = coeff * math.log2(math.e)
-    kept, dpre, gated = forward_scan(
-        order, picked, channels, dgated, fresh, weight_own, bias_own, skip_own, coeff_two, spread
-    )
-
-    gated = moves.swap_state(gated)
-    gated_q = join_own(gated[:, 0]).reshape(rows_q, chans)
-    dgate_q = join_own(gated[:, 1]).reshape(rows_q, chans)
-    own_sums, other_sums, dscan, delta_grad_own, decay_total, sums = backward_scan(
-        order,
-        picked,
-        channels,
-        dgated,
-        fresh,
-        dpre,
-        kept,
-        weight_own,
-        skip_own,
-        coeff_two,
-        spread,
-    )
-    partial = [(other_sums if k % 2 else own_sums)[k // 2] for k in range(n_state)]
-    partial = in_axis(partial)
-    decay_grad_own = coeff * decay_total
-    partial, gated_q = tied(partial, gated_q)
-    partial = moves.sum_state(partial)
-
-    branch = jnp.dot(gated_q, out_weight, preferred_element_type=wide)
-    out_part = lax.dot_general(gated_q, grad_q, contract_rows, preferred_element_type=wide)
-    packed = jnp.concatenate([delta_grad_own, decay_grad_own, sums], axis=0)
-    partial, branch, out_part, packed, dscan = tied(
-        partial, branch.astype(low), out_part.astype(low), packed, dscan
-    )
-    dsmall = moves.gather_chan(moves.sum_small(partial).astype(low))[:, :reach]
-    dscan_win = join_own(moves.swap_state(dscan))[:, :reach].astype(wide)
-    gate_part = lax.dot_general(normed_q, dgate_q, contract_rows, preferred_element_type=wide)
-    branch = lax.psum_scatter(
-        moves.in_axis_order(branch.reshape(n_chan, quarter, width)).reshape(rows_q, width),
-        "chan",
-        scatter_dimension=0,
-        tiled=True,
-    )
-    out_grad = moves.total_state(out_part).astype(wide)
-    dsmall, dscan_win, dgate_q, gate_part = tied(
-        dsmall, dscan_win, dgate_q, gate_part.astype(low)
-    )
-
-    dact = dscan_win + lax.dot_general(
-        dsmall.reshape(-1, small), select, contract_cols, preferred_element_type=wide
-    ).reshape(n_chan, reach, chans)
-    dconv = dact * mask_win[:, HALO:] * silu_slope(conv_win)
-    dinner = jnp.zeros((n_chan, quarter, chans), wide)
-    kernel_rows = []
-    for index in range(taps):
-        lag = taps - 1 - index
-        masked = dconv * valid_at(lag, HALO, reach)
-        shifted = inner_win[:, HALO - lag : HALO - lag + quarter]
-        kernel_rows.append(jnp.sum(masked[:, :quarter] * shifted, axis=(0, 1)))
-        dinner = dinner + masked[:, lag : lag + quarter] * conv_kernel[index]
-    kernel_rows.append(jnp.sum(dconv[:, :quarter], axis=(0, 1)))
-    dinner = (dinner * mask_win[:, HALO : HALO + quarter]).astype(low).reshape(rows_q, chans)
-    dboth = jnp.concatenate([dinner, dgate_q], axis=1)
-
-    def backed(rows, weight):
-        return lax.dot_general(rows, weight, contract_cols, preferred_element_type=wide)
-
-    if moves.near:
-        half = width // 2
-        joined = []
-        gains = []
-        for columns in (slice(0, half), slice(half, width)):
-            gain = jnp.zeros((half,), wide)
-            halves = []
-            for rows in (slice(rows_q // 2, rows_q), slice(0, rows_q // 2)):
-                piece = backed(dboth[rows], in_flat[columns])
-                gain = gain + jnp.sum(piece * normed_q[rows, columns].astype(wide), axis=0)
-                halves.append(piece.reshape(4, quarter, half))
-            joined.append(moves.joined_planes(halves[1], halves[0].astype(low)))
-            gains.append(gain)
-        joined[0], gains[0], gains[1], dinner = tied(joined[0], gains[0], gains[1], dinner)
-        dnormed = jnp.concatenate([moves.summed_planes(v) for v in joined], axis=1)
-        gain_part = jnp.concatenate(gains)
-    else:
-        dnormed = backed(dboth, in_flat)
-        gain_part = jnp.sum(dnormed * normed_q.astype(wide), axis=0)
-        dnormed = moves.sum_chan(dnormed.reshape(n_chan, quarter, width))
-    gain_part = moves.sum_row(gain_part)[None]
-    dscaled = dnormed * norm_gain[None, :]
-    change = inv_rms * (dscaled - scaled * jnp.mean(dscaled * scaled, axis=1, keepdims=True))
-    change = moves.gather_state(jnp.concatenate([change, gain_part], axis=0).astype(low))
-    input_grad = cotangent + change[:, :quarter].reshape(rows_dev, width)
-    gain_grad = jnp.sum(change[:, quarter].astype(wide), axis=0) / norm_gain
-
-    result = hidden_in + moves.gather_state(branch).reshape(rows_dev, width)
-    inner_part = lax.dot_general(normed_q, dinner, contract_rows, preferred_element_type=wide)
-    gate_grad = moves.total_state(gate_part)
-    in_grad = interleave(moves.total_state(inner_part.astype(low)), gate_grad)
-
-    dsmall_q = dsmall[:, :quarter].reshape(rows_q, small)
-    select_grad = lax.dot_general(dsmall_q, act_q, contract_rows, preferred_element_type=wide)
-    rest = moves.gather_near(jnp.concatenate([select_grad, jnp.stack(kernel_rows)], axis=0))
-    rest = sum(rest)
-    rank_grad = rest[:rank].T
-    first = rank + part * per_state
-    entry_grad = lax.dynamic_slice_in_dim(rest, first, per_state, 0).T
-    read_grad = lax.dynamic_slice_in_dim(rest, first + states, per_state, 0).T
-    kernel_grad = rest[small : small + taps]
-    offset_grad = rest[small + taps]
-    packed = jnp.swapaxes(moves.gather_state(packed), 0, 1).reshape(-1, chans)
-    delta_grad = packed[:rank]
-    decay_grad = lax.dynamic_slice_in_dim(packed, rank + part * per_state, per_state, 0)
-    bias_grad = packed[rank + states]
-    skip_grad = packed[rank + states + 1]
-    return (
-        result,
-        input_grad,
-        gain_grad,
-        in_grad,
-        kernel_grad,
-        offset_grad,
-        rank_grad,
-        entry_grad,
-        read_grad,
-        delta_grad,
-        bias_grad,
-        decay_grad,
-        skip_grad,
-        out_grad,
-    )
 
 
 def near_shards(
@@ -1380,7 +1321,7 @@
     part = lax.axis_index("state").astype(jnp.uint32)
     contract_rows = (((0,), (0,)), ((), ()))
     contract_cols = (((1,), (1,)), ((), ()))
-    moves = Moves(n_chan, n_state)
+    moves = Moves()
     blocks = moves.blocks
     planes = jnp.arange(4, dtype=jnp.uint32)
     small_order = jnp.stack([(moves.y ^ u) * 4 + planes for u in (0, 1)], axis=1).reshape(-1)
@@ -1492,14 +1433,14 @@
     summed = total_of(joined, along)
     came = moves.over_y(summed)
     dgated = trades(dgated)
-    picked = moves.gather_near(jnp.concatenate([summed, came], axis=0))
+    picked = moves.pieces_state(jnp.concatenate([summed, came], axis=0))
     tie = tied(*picked, *dgated, channels)
     picked, dgated, channels = tie[:4], tie[4:8], tie[8]
 
     weight_own = mine(delta_weight, 1)
     bias_own = mine(step_bias)[None, :]
     skip_own = mine(skip_weight)[None, :]
-    fresh = (place > 0).astype(wide)[:, None]
+    fresh = jnp.broadcast_to((place > 0).astype(low)[:, None], (tokens, own))
     spread = spreading(states)
     coeff_two = coeff * math.log2(math.e)
     kept, dpre, gated = forward_scan(
@@ -1534,8 +1475,6 @@
         own_sums, other_sums, packed, gated, dscan
     )
 
-    half = width // 2
-    first, second = slice(0, half), slice(half, width)
     came = moves.over_state(other_sums, 1)
     branch_kept, sent, second_branch, out_kept, out_sent, dgate_q = emit(
         places, gated, out_weight, grad_q
@@ -1604,10 +1543,10 @@
     out_slant = moves.over_state(out_chip, 1)
     packed_chip = moves.over_state(packed, 2)
     tie = tied(
-        left_sent, dboth, rank_part, out_core, out_slant, packed_chip, *right_sent, *branches
-    )
-    left_sent, dboth, rank_part, out_core, out_slant, packed_chip = tie[:6]
-    right_sent, branches = tie[6:9], tie[9:]
+        left_sent, dboth, rank_part, out_core, out_slant, packed_chip, branches[0], *right_sent
+    )
+    left_sent, dboth, rank_part, out_core, out_slant, packed_chip, branches[0] = tie[:7]
+    right_sent = tie[7:]
 
     left_came = moves.over_y(left_sent)
     right_along = [moves.over_z(right_sent[hops - 1], hops) for hops in (1, 2, 3)]
@@ -1713,9 +1652,10 @@
 
 def solution(mesh):
     sizes = dict(mesh.shape)
-    program = near_shards if (sizes["chan"], sizes["state"]) == (8, 4) else shards
+    near = (sizes["chan"], sizes["state"]) == (8, 4)
+    program = functools.partial(near_shards, 8, 4) if near else shards
     return jax.shard_map(
-        functools.partial(program, sizes["chan"], sizes["state"]),
+        program,
         mesh=mesh,
         in_specs=(
             P("chan", None),

time: 356 us -> 350 us (0.983)
  starting transfers between devices: 88 us -> 97.1 us
  waiting for transfers between devices: 102 us -> 96.2 us
  Pallas kernels: 84.3 us -> 80.1 us
    ppermute x21, starting transfers between devices: 39.2 us -> 50.7 us  [over_z(): lax.ppermute(values, 'chan', [(i, (i + 2 * hops) % 8) for i in range(8)])]
    ppermute x21, waiting for transfers between devices: 24.8 us -> 15.9 us  [over_z(): lax.ppermute(values, 'chan', [(i, (i + 2 * hops) % 8) for i in range(8)])]
    unnamed x121 -> x107, local copies, waits for them, and re-layouts: 12.6 us -> 12.7 us
  transfers between devices with their start and end apart: 72 -> 72, of which waited for: 25 -> 22; matrix products, arithmetic and copies ran while one was open for 14% -> 13% of each run, Pallas kernels for 18% -> 17%
where the time goes in v1:
time: 350 us; the launch traced here: 349 us
  starting transfers between devices  97.1 us (28%)
  waiting for transfers between devices  96.2 us (27%)
  Pallas kernels  80.1 us (23%)
  other arithmetic  25 us (7%)
  local copies, waits for them, and re-layouts  23.7 us (7%)
  between operations  14.8 us (4%)
  matrix products  12.3 us (4%)
    ppermute x21, starting transfers between devices, over_z(): lax.ppermute(values, 'chan', [(i, (i + 2 * hops) % 8) for i in range(8)])  50.7 us
    ppermute x13, waiting for transfers between devices, over_y(): return lax.ppermute(values, 'chan', [(i, i ^ 1) for i in range(8)])  38.8 us
    ppermute x29, waiting for transfers between devices, over_state(): return lax.ppermute(values, 'state', [(i, i ^ bits) for i in range(4)])  33.5 us
    pallas_call x1, Pallas kernels, backward_scan(): pl.pallas_call(functools.partial(backward_body, parts), grid_spec=pltpu.P...  21.4 us
    ppermute x29, starting transfers between devices, over_state(): return lax.ppermute(values, 'state', [(i, i ^ bits) for i in range(4)])  18.5 us
    ppermute x21, waiting for transfers between devices, over_z(): lax.ppermute(values, 'chan', [(i, (i + 2 * hops) % 8) for i in range(8)])  15.9 us
    pallas_call x1, Pallas kernels, forward_scan(): pl.pallas_call(functools.partial(forward_body, parts), grid_spec=pltpu.Pr...  14.1 us
    all_to_all x4, starting transfers between devices, swap_state(): return lax.all_to_all(values, 'state', 0, 0, tiled=True)  13.8 us
  transfers between devices with their start and end apart: 72, of which 22 were waited for; matrix products, arithmetic and copies ran while one was open for 13% of the time, Pallas kernels for 17%

profile of v1, /device:TPU:0, one launch (start us, length us, event | category | flops | bytes accessed | tf_op | source)
XLA Modules:
  0.0 349.1 jit_solution(18119251708829770132)
XLA Ops:
  19.8 3.3 all-to-all-start
  26.2 5.4 %copy.67 = bf16[256,8,2,512]{3,1,2,0:T(8,128)(2,1)} copy(bf16[256,8,2,512]{3,2,1,0:T(2,128)(2,1)} %bitcast.164) | data formatting | bytes 8388608
  31.7 5.6 %collective-permute-done.2.refs_2_ = bf16[72,2048]{1,0:T(8,128)(2,1)S(1)} collective-permute-done((bf16[72,2048]{1,0:T(8,128)(2,1)S(1)}, bf16[72,2048]{1,0:T(8,128)(2,1)S(1)}, u32[]{:S(2)}, u32[]{:S(2)}) %collective-permute-start.2) | collective-permute-done | bytes 294944 | tf_op jit(solution)/shard_map/ppermute | solution.py:1257
  44.9 6.1 %collective-permute-done.6.refs_5_ = bf16[72,2048]{1,0:T(8,128)(2,1)S(1)} collective-permute-done((bf16[72,2048]{1,0:T(8,128)(2,1)S(1)}, bf16[72,2048]{1,0:T(8,128)(2,1)S(1)}, u32[]{:S(2)}, u32[]{:S(2)}) %collective-permute-start.6) | collective-permute-done | bytes 294944 | tf_op jit(solution)/shard_map/ppermute | solution.py:1254
  51.1 9.1 %collective-permute-done.7.refs_6_ = bf16[72,2048]{1,0:T(8,128)(2,1)S(1)} collective-permute-done((bf16[72,2048]{1,0:T(8,128)(2,1)S(1)}, bf16[72,2048]{1,0:T(8,128)(2,1)S(1)}, u32[]{:S(2)}, u32[]{:S(2)}) %collective-permute-start.7) | collective-permute-done | bytes 294944 | tf_op jit(solution)/shard_map/ppermute | solution.py:1254
  60.9 4.5 %collective-permute-done.8.refs_7_ = bf16[72,2048]{1,0:T(8,128)(2,1)S(1)} collective-permute-done((bf16[72,2048]{1,0:T(8,128)(2,1)}, bf16[72,2048]{1,0:T(8,128)(2,1)S(1)}, u32[]{:S(2)}, u32[]{:S(2)}) %collective-permute-start.8) | collective-permute-done | bytes 294944 | tf_op jit(solution)/shard_map/ppermute | solution.py:1254
  68.1 9.9 %project.1 = (bf16[512,2048]{1,0:T(8,128)(2,1)}, f32[8,80,512]{2,1,0:T(8,128)}, bf16[4,2,8,64,128]{4,3,2,1,0:T(8,128)(2,1)}, f32[4,64,160]{2,1,0:T(8,128)S(1)}, bf16[4,64,160]{2,1,0:T(8,128)(2,1)S(1)}) custom-call(s32[20]{0:T(128)S(1)} %pad_add_fusion.1.place_ref, bf16[72,2048]{1,0:T(8,128)(2,1)} %copy-done.22, bf16[72,2048]{1,0:T(8,128)(2,1)} %copy-done.28, ...), custom_call_target="tpu_custom_call" | custom-call | bytes 28800000 | tf_op jit(solution)/shard_map/project/pallas_call | solution.py:922
  78.6 8.0 %collective-permute-done.10 = bf16[4,64,160]{2,1,0:T(8,128)(2,1)S(1)} collective-permute-done((bf16[4,64,160]{2,1,0:T(8,128)(2,1)S(1)}, bf16[4,64,160]{2,1,0:T(8,128)(2,1)S(1)}, u32[]{:S(2)}, u32[]{:S(2)}) %collective-permute-start.10) | collective-permute-done | bytes 81952 | tf_op jit(solution)/shard_map/ppermute | solution.py:1254
  86.6 3.5 %collective-permute-start.11 = (bf16[4,64,160]{2,1,0:T(8,128)(2,1)S(1)}, bf16[4,64,160]{2,1,0:T(8,128)(2,1)}, u32[]{:S(2)}, u32[]{:S(2)}) collective-permute-start(bf16[4,64,160]{2,1,0:T(8,128)(2,1)S(1)} %add_convert_fusion.7), channel_id=1, source_target_pairs={{0,8},{4,12},{8,16},{12,20},{16,24},{20,28},{24,0},{28,4},{1,9},{5... | collective-permute-start | bytes 245768 | tf_op jit(solution)/shard_map/ppermute | solution.py:1257
  92.8 3.5 %all-to-all-start.1 = ((bf16[4,2,8,64,128]{4,3,2,1,0:T(8,128)(2,1)}), bf16[4,2,8,64,128]{4,3,2,1,0:T(8,128)(2,1)S(1)}, u32[]{:S(2)}, u32[]{:S(2)}) async-start(bf16[4,2,8,64,128]{4,3,2,1,0:T(8,128)(2,1)} %get-tuple-element.180), calls=%async_computation.1 | async-start | bytes 2097152 | tf_op jit(solution)/shard_map/all_to_all | solution.py:1263
  98.4 5.7 %pull.1 = (bf16[512,2048]{1,0:T(8,128)(2,1)}, bf16[8,64,128]{2,1,0:T(8,128)(2,1)}, bf16[8,64,128]{2,1,0:T(8,128)(2,1)}, bf16[8,64,128]{2,1,0:T(8,128)(2,1)}, bf16[8,64,128]{2,1,0:T(8,128)(2,1)}) custom-call(s32[9]{0:T(128)S(1)} %add_convert_fusion.8.order_ref, bf16[8,64,2048]{2,1,0:T(8,128)(2,1)} %bitcast.165, bf16[512,2048]{1,0:T(8,128)(2,1)} %refs_1_.1), custom_call_target="tpu_custom_call" | custom-call | bytes 21600000 | tf_op jit(solution)/shard_map/pull/pallas_call | solution.py:995
  105.8 4.5 %collective-permute-done.14 = bf16[4,64,160]{2,1,0:T(8,128)(2,1)S(1)} collective-permute-done((bf16[4,64,160]{2,1,0:T(8,128)(2,1)S(1)}, bf16[4,64,160]{2,1,0:T(8,128)(2,1)S(1)}, u32[]{:S(2)}, u32[]{:S(2)}) %collective-permute-start.14) | collective-permute-done | bytes 81952 | tf_op jit(solution)/shard_map/ppermute | solution.py:1254
  114.8 4.8 %collective-permute-done.16.refs_2_ = bf16[8,64,160]{2,1,0:T(8,128)(2,1)} collective-permute-done((bf16[8,64,160]{2,1,0:T(8,128)(2,1)}, bf16[8,64,160]{2,1,0:T(8,128)(2,1)}, u32[]{:S(2)}, u32[]{:S(2)}) %collective-permute-start.16) | collective-permute-done | bytes 163872 | tf_op jit(solution)/shard_map/ppermute | solution.py:1260
  123.5 14.1 %forward_scan.1 = (bf16[32768,128]{1,0:T(8,128)(2,1)}, f32[2048,128]{1,0:T(8,128)}, bf16[4,2,8,64,128]{4,3,2,1,0:T(8,128)(2,1)}) custom-call(s32[17]{0:T(128)S(1)} %add_convert_fusion.9.order_ref, bf16[8,64,160]{2,1,0:T(8,128)(2,1)} %pad_maximum_fusion.2.refs_0_, bf16[8,64,160]{2,1,0:T(8,128)(2,1)} %collective-permute-done.15.refs_1_, ...), custom_call_target="tpu_custom_call" | custom-call | bytes 43200000 | tf_op jit(solution)/shard_map/forward_scan/pallas_call | solution.py:695
  137.6 3.5 %all-to-all-start.2 = ((bf16[4,2,8,64,128]{4,3,2,1,0:T(8,128)(2,1)}), bf16[4,2,8,64,128]{4,3,2,1,0:T(8,128)(2,1)S(1)}, u32[]{:S(2)}, u32[]{:S(2)}) async-start(bf16[4,2,8,64,128]{4,3,2,1,0:T(8,128)(2,1)} %get-tuple-element.198), calls=%async_computation.2 | async-start | bytes 2097152 | tf_op jit(solution)/shard_map/all_to_all | solution.py:1263
  141.4 21.4 %backward_scan.1 = (bf16[2,8,80,160]{3,2,1,0:T(8,128)(2,1)}, bf16[2,8,80,160]{3,2,1,0:T(8,128)(2,1)}, bf16[4,8,80,128]{3,2,1,0:T(8,128)(2,1)}, f32[128,128]{1,0:...) custom-call(s32[17]{0:T(128)S(1)} %add_convert_fusion.9.order_ref, ...), custom_call_target="tpu_custom_call" | custom-call | bytes 68400000 | tf_op jit(solution)/shard_map/backward_scan/pallas_call | solution.py:744
  164.4 7.9 %emit.1 = (bf16[4,64,2048]{2,1,0:T(8,128)(2,1)}, bf16[4,64,512]{2,1,0:T(8,128)(2,1)}, bf16[4,64,1536]{2,1,0:T(8,128)(2,1)}, bf16[2,128,2048]{2,1,0:T(8,128)(2,1)...) custom-call(s32[9]{0:T(128)S(1)} %add_convert_fusion.8.order_ref, bf16[4,2,8,64,128]{4,3,2,1,0:T(8,128)(2,1)} %copy-done.21, ...), custom_call_target="tpu_custom_call" | custom-call | bytes 21600000 | tf_op jit(solution)/shard_map/emit/pallas_call | solution.py:1064
  172.3 4.4 %fusion.46 = (bf16[2048,512]{1,0:T(8,128)(2,1)}, f32[2048]{0:T(1024)S(1)}) fusion(bf16[2048,1024]{1,0:T(8,128)(2,1)S(1)} %bitcast.159, bf16[512,2048]{1,0:T(8,128)(2,1)} %get-tuple-element.209, bf16[512,512]{1,0:T(8,128)(2,1)} %get-tuple-element.210.refs_8_), kind=kOutput, calls=%fused_computation.175 | convolution fusion | flops 1077934080 | bytes 6823936 | tf_op jit(solution)/shard_map/dot_general | solution.py:1489
  181.6 7.9 %collective-permute-done.22 = bf16[8,80,160]{2,1,0:T(8,128)(2,1)S(1)} collective-permute-done((bf16[8,80,160]{2,1,0:T(8,128)(2,1)S(1)}, bf16[8,80,160]{2,1,0:T(8,128)(2,1)S(1)}, u32[]{:S(2)}, u32[]{:S(2)}) %collective-permute-start.22) | collective-permute-done | bytes 204832 | tf_op jit(solution)/shard_map/ppermute | solution.py:1260
  192.0 3.7 %collective-permute-done.24 = bf16[4,80,160]{2,1,0:T(8,128)(2,1)S(1)} collective-permute-done((bf16[4,80,160]{2,1,0:T(8,128)(2,1)S(1)}, bf16[4,80,160]{2,1,0:T(8,128)(2,1)S(1)}, u32[]{:S(2)}, u32[]{:S(2)}) %collective-permute-start.24) | collective-permute-done | bytes 102432 | tf_op jit(solution)/shard_map/ppermute | solution.py:1254
  198.4 3.5 all-to-all-start.3
  201.9 3.7 %collective-permute-start.27 = (bf16[4,80,160]{2,1,0:T(8,128)(2,1)S(1)}, bf16[4,80,160]{2,1,0:T(8,128)(2,1)S(1)}, u32[]{:S(2)}, u32[]{:S(2)}) collective-permute-start(bf16[4,80,160]{2,1,0:T(8,128)(2,1)S(1)} %add_convert_fusion.4), channel_id=1, source_target_pairs={{0,8},{4,12},{8,16},{12,20},{16,24},{20,28},{24,0},{28,4},{1,9},{5... | collective-permute-start | bytes 307208 | tf_op jit(solution)/shard_map/ppermute | solution.py:1257
  212.9 4.5 %collective-permute-done.28 = bf16[4,80,160]{2,1,0:T(8,128)(2,1)S(1)} collective-permute-done((bf16[4,80,160]{2,1,0:T(8,128)(2,1)S(1)}, bf16[4,80,160]{2,1,0:T(8,128)(2,1)S(1)}, u32[]{:S(2)}, u32[]{:S(2)}) %collective-permute-start.28) | collective-permute-done | bytes 102432 | tf_op jit(solution)/shard_map/ppermute | solution.py:1257
  217.4 3.6 %collective-permute-done.31 = bf16[128,2048]{1,0:T(8,128)(2,1)} collective-permute-done((bf16[128,2048]{1,0:T(8,128)(2,1)}, bf16[128,2048]{1,0:T(8,128)(2,1)}, u32[]{:S(2)}, u32[]{:S(2)}) %collective-permute-start.31) | collective-permute-done | bytes 524320 | tf_op jit(solution)/shard_map/ppermute | solution.py:1260
  234.4 6.8 %turn_back.1 = (bf16[512,1024]{1,0:T(8,128)(2,1)S(1)}, bf16[512,128]{1,0:T(8,128)(2,1)}, f32[40,512]{1,0:T(8,128)S(1)}) custom-call(s32[9]{0:T(128)S(1)} %add_convert_fusion.8.order_ref, bf16[4,80,160]{2,1,0:T(8,128)(2,1)} %add_convert_fusion.3.refs_0_, bf16[4,80,160]{2,1,0:T(8,128)(2,1)} %collective-permute-done.32.refs_1_, ...), custom_call_target="tpu_custom_call" | custom-call | bytes 19800000 | tf_op jit(solution)/shard_map/turn_back/pallas_call | solution.py:1192
  246.4 4.8 %collective-permute-start.39 = (bf16[2,64,640]{2,1,0:T(8,128)(2,1)S(1)}, bf16[2,64,640]{2,1,0:T(8,128)(2,1)S(1)}, u32[]{:S(2)}, u32[]{:S(2)}) collective-permute-start(bf16[2,64,640]{2,1,0:T(8,128)(2,1)S(1)} %get-tuple-element.236), channel_id=1, source_target_pairs={{0,8},{4,12},{8,16},{12,20},{16,24},{20,28},{24,0},{28,4},{1,9},{5... | collective-permute-start | bytes 491528 | tf_op jit(solution)/shard_map/ppermute | solution.py:1257
  254.7 10.2 %collective-permute-start.44 = (bf16[2,64,640]{2,1,0:T(8,128)(2,1)}, bf16[2,64,640]{2,1,0:T(8,128)(2,1)}, u32[]{:S(2)}, u32[]{:S(2)}) collective-permute-start(bf16[2,64,640]{2,1,0:T(8,128)(2,1)} %get-tuple-element.245), channel_id=1, source_target_pairs={{0,24},{4,28},{8,0},{12,4},{16,8},{20,12},{24,16},{28,20},{1,25},{... | collective-permute-start | bytes 491528 | tf_op jit(solution)/shard_map/ppermute | solution.py:1257
  267.3 4.3 %placed.3 = f32[512,2048]{1,0:T(8,128)} custom-call(s32[4]{0:T(128)S(1)} %xor_convert_fusion.order_ref, bf16[128,2048]{1,0:T(8,128)(2,1)S(1)} %fusion.5.refs_0_, bf16[128,2048]{1,0:T(8,128)(2,1)} %collective-permute-done.33.refs_1_, bf16[128,2048]{1,0:T(8,128)(2,1)} %collective-permute-done.34.refs_2_, bf16[128,2048]{1,0:T(8,128)(2,1)S(1)} %collective-permute-done.35.refs_3_), custom_call_target="tpu_custom_call" | custom-call | bytes 9000000 | tf_op jit(solution)/shard_map/placed/pallas_call | solution.py:818
  277.9 3.3 collective-permute-start.50
  287.7 5.8 %collective-permute-done.49 = bf16[64,1408]{1,0:T(8,128)(2,1)S(1)} collective-permute-done((bf16[64,1408]{1,0:T(8,128)(2,1)S(1)}, bf16[64,1408]{1,0:T(8,128)(2,1)S(1)}, u32[]{:S(2)}, u32[]{:S(2)}) %collective-permute-start.49) | collective-permute-done | bytes 180256 | tf_op jit(solution)/shard_map/ppermute | solution.py:1257
  299.1 11.8 %collective-permute-done.53 = f32[44,512]{1,0:T(8,128)S(1)} collective-permute-done((f32[44,512]{1,0:T(8,128)S(1)}, f32[44,512]{1,0:T(8,128)S(1)}, u32[]{:S(2)}, u32[]{:S(2)}) %collective-permute-start.53) | collective-permute-done | bytes 90144 | tf_op jit(solution)/shard_map/ppermute | solution.py:1260
  337.4 5.1 %interleave.1 = f32[2048,2,512]{2,1,0:T(2,128)} custom-call(bf16[2048,512]{1,0:T(8,128)(2,1)S(1)} %copy-done.7, bf16[2048,512]{1,0:T(8,128)(2,1)S(1)} %copy-done.6), custom_call_target="tpu_custom_call" | custom-call | bytes 18000000 | tf_op jit(solution)/shard_map/interleave/pallas_call | solution.py:791
  (337 shorter events, 130.2 us)
Async XLA Ops:
  11.2 20.4 %collective-permute-start = (bf16[72,2048]{1,0:T(8,128)(2,1)S(1)}, bf16[72,2048]{1,0:T(8,128)(2,1)S(1)}, u32[]{:S(2)}, u32[]{:S(2)}) collective-permute-start(bf16[72,2048]{1,0:T(8,128)(2,1)S(1)} %get-tuple-element.294.refs_0_), channel_id=1, source_target_pairs={{0,4},{4,0},{8,12},{12,8},{16,20},{20,16},{24,28},{28,24},{1,5},{5... | collective-permute-start | bytes 884744 | tf_op jit(solution)/shard_map/ppermute | solution.py:1254
  14.2 17.5 %collective-permute-start.1 = (bf16[72,2048]{1,0:T(8,128)(2,1)S(1)}, bf16[72,2048]{1,0:T(8,128)(2,1)S(1)}, u32[]{:S(2)}, u32[]{:S(2)}) collective-permute-start(bf16[72,2048]{1,0:T(8,128)(2,1)S(1)} %get-tuple-element.294.refs_0_), channel_id=1, source_target_pairs={{0,8},{4,12},{8,16},{12,20},{16,24},{20,28},{24,0},{28,4},{1,9},{5... | collective-permute-start | bytes 884744 | tf_op jit(solution)/shard_map/ppermute | solution.py:1257
  15.7 21.5 %collective-permute-start.2 = (bf16[72,2048]{1,0:T(8,128)(2,1)S(1)}, bf16[72,2048]{1,0:T(8,128)(2,1)S(1)}, u32[]{:S(2)}, u32[]{:S(2)}) collective-permute-start(bf16[72,2048]{1,0:T(8,128)(2,1)S(1)} %get-tuple-element.294.refs_0_), channel_id=1, source_target_pairs={{0,16},{4,20},{8,24},{12,28},{16,0},{20,4},{24,8},{28,12},{1,17},{... | collective-permute-start | bytes 884744 | tf_op jit(solution)/shard_map/ppermute | solution.py:1257
  18.3 18.9 %collective-permute-start.3 = (bf16[72,2048]{1,0:T(8,128)(2,1)S(1)}, bf16[72,2048]{1,0:T(8,128)(2,1)}, u32[]{:S(2)}, u32[]{:S(2)}) collective-permute-start(bf16[72,2048]{1,0:T(8,128)(2,1)S(1)} %get-tuple-element.294.refs_0_), channel_id=1, source_target_pairs={{0,24},{4,28},{8,0},{12,4},{16,8},{20,12},{24,16},{28,20},{1,25},{... | collective-permute-start | bytes 884744 | tf_op jit(solution)/shard_map/ppermute | solution.py:1257
  23.0 75.4 %all-gather.9.cloned.1.call-start = ((), (), s32[]{:S(2)}) async-start(), calls=%async_computation.10 | async-start | bytes 2359296 | tf_op jit(solution)/shard_map/all_gather | solution.py:1393
  41.7 18.5 %collective-permute-start.7 = (bf16[72,2048]{1,0:T(8,128)(2,1)S(1)}, bf16[72,2048]{1,0:T(8,128)(2,1)S(1)}, u32[]{:S(2)}, u32[]{:S(2)}) collective-permute-start(bf16[72,2048]{1,0:T(8,128)(2,1)S(1)} %collective-permute-done.2.refs_2_), channel_id=1, source_target_pairs={{0,4},{4,0},{8,12},{12,8},{16,20},{20,16},{24,28},{28,24},{1,5},{5... | collective-permute-start | bytes 884744 | tf_op jit(solution)/shard_map/ppermute | solution.py:1254
  43.2 22.3 %collective-permute-start.8 = (bf16[72,2048]{1,0:T(8,128)(2,1)}, bf16[72,2048]{1,0:T(8,128)(2,1)S(1)}, u32[]{:S(2)}, u32[]{:S(2)}) collective-permute-start(bf16[72,2048]{1,0:T(8,128)(2,1)} %collective-permute-done.3.refs_3_), channel_id=1, source_target_pairs={{0,4},{4,0},{8,12},{12,8},{16,20},{20,16},{24,28},{28,24},{1,5},{5... | collective-permute-start | bytes 884744 | tf_op jit(solution)/shard_map/ppermute | solution.py:1254
  86.6 17.6 %collective-permute-start.11 = (bf16[4,64,160]{2,1,0:T(8,128)(2,1)S(1)}, bf16[4,64,160]{2,1,0:T(8,128)(2,1)}, u32[]{:S(2)}, u32[]{:S(2)}) collective-permute-start(bf16[4,64,160]{2,1,0:T(8,128)(2,1)S(1)} %add_convert_fusion.7), channel_id=1, source_target_pairs={{0,8},{4,12},{8,16},{12,20},{16,24},{20,28},{24,0},{28,4},{1,9},{5... | collective-permute-start | bytes 245768 | tf_op jit(solution)/shard_map/ppermute | solution.py:1257
  90.1 14.1 %collective-permute-start.12 = (bf16[4,64,160]{2,1,0:T(8,128)(2,1)S(1)}, bf16[4,64,160]{2,1,0:T(8,128)(2,1)}, u32[]{:S(2)}, u32[]{:S(2)}) collective-permute-start(bf16[4,64,160]{2,1,0:T(8,128)(2,1)S(1)} %add_convert_fusion.7), channel_id=1, source_target_pairs={{0,16},{4,20},{8,24},{12,28},{16,0},{20,4},{24,8},{28,12},{1,17},{... | collective-permute-start | bytes 245768 | tf_op jit(solution)/shard_map/ppermute | solution.py:1257
  92.8 26.8 %all-to-all-start.1 = ((bf16[4,2,8,64,128]{4,3,2,1,0:T(8,128)(2,1)}), bf16[4,2,8,64,128]{4,3,2,1,0:T(8,128)(2,1)S(1)}, u32[]{:S(2)}, u32[]{:S(2)}) async-start(bf16[4,2,8,64,128]{4,3,2,1,0:T(8,128)(2,1)} %get-tuple-element.180), calls=%async_computation.1 | async-start | bytes 2097152 | tf_op jit(solution)/shard_map/all_to_all | solution.py:1263
  137.6 25.8 %all-to-all-start.2 = ((bf16[4,2,8,64,128]{4,3,2,1,0:T(8,128)(2,1)}), bf16[4,2,8,64,128]{4,3,2,1,0:T(8,128)(2,1)S(1)}, u32[]{:S(2)}, u32[]{:S(2)}) async-start(bf16[4,2,8,64,128]{4,3,2,1,0:T(8,128)(2,1)} %get-tuple-element.198), calls=%async_computation.2 | async-start | bytes 2097152 | tf_op jit(solution)/shard_map/all_to_all | solution.py:1263
  141.1 86.8 %reduce-scatter.3.cloned.1.call-start = ((), (), s32[]{:S(2)}) async-start(), calls=%async_computation.6 | async-start | bytes 2621440 | tf_op jit(solution)/shard_map/reduce_scatter | solution.py:1491
  195.7 25.3 %collective-permute-start.30 = (bf16[4,64,1536]{2,1,0:T(8,128)(2,1)}, bf16[4,64,1536]{2,1,0:T(8,128)(2,1)}, u32[]{:S(2)}, u32[]{:S(2)}) collective-permute-start(bf16[4,64,1536]{2,1,0:T(8,128)(2,1)} %get-tuple-element.217), channel_id=1, source_target_pairs={{0,4},{4,0},{8,12},{12,8},{16,20},{20,16},{24,28},{28,24},{1,5},{5... | collective-permute-start | bytes 2359304 | tf_op jit(solution)/shard_map/ppermute | solution.py:1254
  196.8 24.2 %collective-permute-start.31 = (bf16[128,2048]{1,0:T(8,128)(2,1)}, bf16[128,2048]{1,0:T(8,128)(2,1)}, u32[]{:S(2)}, u32[]{:S(2)}) collective-permute-start(bf16[128,2048]{1,0:T(8,128)(2,1)} %slice_bitcast_fusion.1), channel_id=1, source_target_pairs={{0,2},{1,3},{2,0},{3,1},{4,6},{5,7},{6,4},{7,5},{8,10},{9,11},{10,... | collective-permute-start | bytes 1572872 | tf_op jit(solution)/shard_map/ppermute | solution.py:1260
  198.4 29.6 %all-to-all-start.3 = ((bf16[4,8,80,128]{3,2,1,0:T(8,128)(2,1)}), bf16[4,8,80,128]{3,2,1,0:T(8,128)(2,1)S(1)}, u32[]{:S(2)}, u32[]{:S(2)}) async-start(bf16[4,8,80,128]{3,2,1,0:T(8,128)(2,1)} %get-tuple-element.223), calls=%async_computation.3 | async-start | bytes 1310720 | tf_op jit(solution)/shard_map/all_to_all | solution.py:1263
  201.8 72.9 %all-gather.5.cloned.1.call-start = ((), (), s32[]{:S(2)}) async-start(), calls=%async_computation.7 | async-start | bytes 2621440 | tf_op jit(solution)/shard_map/all_gather | solution.py:1518
  211.0 32.1 %collective-permute-start.36 = (bf16[152,128]{1,0:T(8,128)(2,1)}, bf16[152,128]{1,0:T(8,128)(2,1)}, u32[]{:S(2)}, u32[]{:S(2)}) collective-permute-start(bf16[152,128]{1,0:T(8,128)(2,1)} %pad_maximum_fusion.7), channel_id=1, source_target_pairs={{0,2},{1,3},{2,0},{3,1},{4,6},{5,7},{6,4},{7,5},{8,10},{9,11},{10,... | collective-permute-start | bytes 116744 | tf_op jit(solution)/shard_map/ppermute | solution.py:1260
  224.6 19.7 %collective-permute-start.34 = (bf16[128,2048]{1,0:T(8,128)(2,1)S(1)}, bf16[128,2048]{1,0:T(8,128)(2,1)}, u32[]{:S(2)}, u32[]{:S(2)}) collective-permute-start(bf16[128,2048]{1,0:T(8,128)(2,1)S(1)} %fusion.5.refs_0_), channel_id=1, source_target_pairs={{0,2},{1,3},{2,0},{3,1},{4,6},{5,7},{6,4},{7,5},{8,10},{9,11},{10,... | collective-permute-start | bytes 1572872 | tf_op jit(solution)/shard_map/ppermute | solution.py:1260
  225.2 20.9 %collective-permute-start.33 = (bf16[128,2048]{1,0:T(8,128)(2,1)S(1)}, bf16[128,2048]{1,0:T(8,128)(2,1)}, u32[]{:S(2)}, u32[]{:S(2)}) collective-permute-start(bf16[128,2048]{1,0:T(8,128)(2,1)S(1)} %fusion.5.refs_0_), channel_id=1, source_target_pairs={{0,1},{1,0},{2,3},{3,2},{4,5},{5,4},{6,7},{7,6},{8,9},{9,8},{10,11... | collective-permute-start | bytes 1572872 | tf_op jit(solution)/shard_map/ppermute | solution.py:1260
  228.0 83.6 %reduce-scatter.5.cloned.1.call-start = ((), (), s32[]{:S(2)}) async-start(), calls=%async_computation.8 | async-start | bytes 2621440 | tf_op jit(solution)/shard_map/reduce_scatter | solution.py:1576
  230.3 15.9 %collective-permute-start.37 = (bf16[64,2048]{1,0:T(8,128)(2,1)S(1)}, bf16[64,2048]{1,0:T(8,128)(2,1)S(1)}, u32[]{:S(2)}, u32[]{:S(2)}) collective-permute-start(bf16[64,2048]{1,0:T(8,128)(2,1)S(1)} %get-tuple-element.304), channel_id=1, source_target_pairs={{0,8},{4,12},{8,16},{12,20},{16,24},{20,28},{24,0},{28,4},{1,9},{5... | collective-permute-start | bytes 786440 | tf_op jit(solution)/shard_map/ppermute | solution.py:1257
  231.7 23.0 %collective-permute-start.40 = (bf16[64,2048]{1,0:T(8,128)(2,1)S(1)}, bf16[64,2048]{1,0:T(8,128)(2,1)S(1)}, u32[]{:S(2)}, u32[]{:S(2)}) collective-permute-start(bf16[64,2048]{1,0:T(8,128)(2,1)S(1)} %get-tuple-element.302), channel_id=1, source_target_pairs={{0,16},{4,20},{8,24},{12,28},{16,0},{20,4},{24,8},{28,12},{1,17},{... | collective-permute-start | bytes 786440 | tf_op jit(solution)/shard_map/ppermute | solution.py:1257
  243.1 21.8 %collective-permute-start.41 = (bf16[64,2048]{1,0:T(8,128)(2,1)S(1)}, bf16[64,2048]{1,0:T(8,128)(2,1)S(1)}, u32[]{:S(2)}, u32[]{:S(2)}) collective-permute-start(bf16[64,2048]{1,0:T(8,128)(2,1)S(1)} %get-tuple-element.303), channel_id=1, source_target_pairs={{0,24},{4,28},{8,0},{12,4},{16,8},{20,12},{24,16},{28,20},{1,25},{... | collective-permute-start | bytes 786440 | tf_op jit(solution)/shard_map/ppermute | solution.py:1257
  246.4 25.2 %collective-permute-start.39 = (bf16[2,64,640]{2,1,0:T(8,128)(2,1)S(1)}, bf16[2,64,640]{2,1,0:T(8,128)(2,1)S(1)}, u32[]{:S(2)}, u32[]{:S(2)}) collective-permute-start(bf16[2,64,640]{2,1,0:T(8,128)(2,1)S(1)} %get-tuple-element.236), channel_id=1, source_target_pairs={{0,8},{4,12},{8,16},{12,20},{16,24},{20,28},{24,0},{28,4},{1,9},{5... | collective-permute-start | bytes 491528 | tf_op jit(solution)/shard_map/ppermute | solution.py:1257
  251.2 23.6 %collective-permute-start.38 = (bf16[4,64,1408]{2,1,0:T(8,128)(2,1)}, bf16[4,64,1408]{2,1,0:T(8,128)(2,1)}, u32[]{:S(2)}, u32[]{:S(2)}) collective-permute-start(bf16[4,64,1408]{2,1,0:T(8,128)(2,1)} %bitcast.22), channel_id=1, source_target_pairs={{0,4},{4,0},{8,12},{12,8},{16,20},{20,16},{24,28},{28,24},{1,5},{5... | collective-permute-start | bytes 2162696 | tf_op jit(solution)/shard_map/ppermute | solution.py:1254
  252.7 22.1 %collective-permute-start.43 = (bf16[2,64,640]{2,1,0:T(8,128)(2,1)}, bf16[2,64,640]{2,1,0:T(8,128)(2,1)}, u32[]{:S(2)}, u32[]{:S(2)}) collective-permute-start(bf16[2,64,640]{2,1,0:T(8,128)(2,1)} %get-tuple-element.244), channel_id=1, source_target_pairs={{0,16},{4,20},{8,24},{12,28},{16,0},{20,4},{24,8},{28,12},{1,17},{... | collective-permute-start | bytes 491528 | tf_op jit(solution)/shard_map/ppermute | solution.py:1257
  254.7 20.1 %collective-permute-start.44 = (bf16[2,64,640]{2,1,0:T(8,128)(2,1)}, bf16[2,64,640]{2,1,0:T(8,128)(2,1)}, u32[]{:S(2)}, u32[]{:S(2)}) collective-permute-start(bf16[2,64,640]{2,1,0:T(8,128)(2,1)} %get-tuple-element.245), channel_id=1, source_target_pairs={{0,24},{4,28},{8,0},{12,4},{16,8},{20,12},{24,16},{28,20},{1,25},{... | collective-permute-start | bytes 491528 | tf_op jit(solution)/shard_map/ppermute | solution.py:1257
  275.4 60.4 %all-gather.7.cloned.1.call-start = ((), (), s32[]{:S(2)}) async-start(), calls=%async_computation.9 | async-start | bytes 2621440 | tf_op jit(solution)/shard_map/all_gather | solution.py:1616
  277.4 16.1 %collective-permute-start.49 = (bf16[64,1408]{1,0:T(8,128)(2,1)S(1)}, bf16[64,1408]{1,0:T(8,128)(2,1)S(1)}, u32[]{:S(2)}, u32[]{:S(2)}) collective-permute-start(bf16[64,1408]{1,0:T(8,128)(2,1)S(1)} %get-tuple-element.306), channel_id=1, source_target_pairs={{0,16},{4,20},{8,24},{12,28},{16,0},{20,4},{24,8},{28,12},{1,17},{... | collective-permute-start | bytes 540680 | tf_op jit(solution)/shard_map/ppermute | solution.py:1257
  277.9 15.6 %collective-permute-start.50 = (bf16[64,1408]{1,0:T(8,128)(2,1)S(1)}, bf16[64,1408]{1,0:T(8,128)(2,1)S(1)}, u32[]{:S(2)}, u32[]{:S(2)}) collective-permute-start(bf16[64,1408]{1,0:T(8,128)(2,1)S(1)} %get-tuple-element.305), channel_id=1, source_target_pairs={{0,24},{4,28},{8,0},{12,4},{16,8},{20,12},{24,16},{28,20},{1,25},{... | collective-permute-start | bytes 540680 | tf_op jit(solution)/shard_map/ppermute | solution.py:1257
  294.0 16.9 %collective-permute-start.51 = (bf16[64,2048]{1,0:T(8,128)(2,1)S(1)}, bf16[64,2048]{1,0:T(8,128)(2,1)S(1)}, u32[]{:S(2)}, u32[]{:S(2)}) collective-permute-start(bf16[64,2048]{1,0:T(8,128)(2,1)S(1)} %multiply_convert_fusion.1.refs_0_), channel_id=1, source_target_pairs={{0,2},{1,3},{2,0},{3,1},{4,6},{5,7},{6,4},{7,5},{8,10},{9,11},{10,... | collective-permute-start | bytes 786440 | tf_op jit(solution)/shard_map/ppermute | solution.py:1260
  294.7 16.9 %collective-permute-start.52 = (bf16[64,2048]{1,0:T(8,128)(2,1)S(1)}, bf16[64,2048]{1,0:T(8,128)(2,1)S(1)}, u32[]{:S(2)}, u32[]{:S(2)}) collective-permute-start(bf16[64,2048]{1,0:T(8,128)(2,1)S(1)} %multiply_convert_fusion.1.refs_0_), channel_id=1, source_target_pairs={{0,1},{1,0},{2,3},{3,2},{4,5},{5,4},{6,7},{7,6},{8,9},{9,8},{10,11... | collective-permute-start | bytes 786440 | tf_op jit(solution)/shard_map/ppermute | solution.py:1260
  (91 other events, 823.5 us)
Sparse Core Ops, SparseCore 0:
  37.4 60.9 all-gather.8
  176.8 43.3 reduce-scatter.2
  228.1 23.8 all-gather.4
  275.5 35.9 reduce-scatter.4
  312.9 22.8 all-gather.6

commit v2 on v1

--- a/solution.py
+++ b/solution.py
@@ -779,25 +779,45 @@
     )(order, *map(in_hbm, streamed), *params)
 
 
-def interleave_body(inner_ref, gate_ref, out_ref):
-    out_ref[:, 0, :] = inner_ref[...].astype(wide)
-    out_ref[:, 1, :] = gate_ref[...].astype(wide)
-
-
-def interleave(inner, gate):
-    rows, width = inner.shape
+def interleave_body(parts, order_ref, *refs):
+    values, out_ref = refs[: 2 * parts], refs[2 * parts]
+    width, block = values[0].shape
+    places = [lax.broadcasted_iota(jnp.int32, (block, block), axis) for axis in (0, 1)]
+    same = jnp.where(places[0] == places[1], 1.0, 0.0).astype(low)
+    for part in range(parts):
+
+        @pl.when(order_ref[0] == part)
+        def _(part=part):
+            for half in range(2):
+                for k in range(parts):
+                    out_ref[:, half, (part ^ k) * width : ((part ^ k) + 1) * width] = (
+                        lax.dot_general(
+                            same,
+                            values[half * parts + k][...],
+                            (((1,), (1,)), ((), ())),
+                            preferred_element_type=wide,
+                        )
+                    )
+
+
+def interleave(order, inner, gate):
+    parts = len(inner)
+    width, depth = inner[0].shape
     block = 256
-    spec = pl.BlockSpec((block, width), lambda t: (t, 0))
     return pl.pallas_call(
-        interleave_body,
-        grid=(rows // block,),
-        in_specs=[spec, spec],
-        out_specs=pl.BlockSpec((block, 2, width), lambda t: (t, 0, 0)),
-        out_shape=jax.ShapeDtypeStruct((rows, 2, width), wide),
+        functools.partial(interleave_body, parts),
+        grid_spec=pltpu.PrefetchScalarGridSpec(
+            num_scalar_prefetch=1,
+            grid=(depth // block,),
+            in_specs=[pl.BlockSpec((width, block), lambda t, order: (0, t))] * parts
+            + [pl.BlockSpec((None, width, block), lambda t, order: (1, 0, t))] * parts,
+            out_specs=pl.BlockSpec((block, 2, parts * width), lambda t, order: (t, 0, 0)),
+        ),
+        out_shape=jax.ShapeDtypeStruct((depth, 2, parts * width), wide),
         compiler_params=pltpu.CompilerParams(vmem_limit_bytes=16 * 1024 * 1024),
         cost_estimate=spent(5),
         name="interleave",
-    )(inner, gate)
+    )(order, *inner, *gate)
 
 
 def placed_body(parts, order_ref, *refs):
@@ -813,14 +833,18 @@
 
 def placed(order, values, base=None):
     parts = len(values)
-    rows, width = values[0].shape
+    rows, width = values[0].shape[-2:]
     flat = pl.BlockSpec((rows, width), lambda p, order: (p, 0))
+    if values[0].ndim == 3:
+        piece = pl.BlockSpec((None, rows, width), lambda p, order: (0, 0, 0))
+    else:
+        piece = pl.BlockSpec((rows, width), lambda p, order: (0, 0))
     return pl.pallas_call(
         functools.partial(placed_body, parts),
         grid_spec=pltpu.PrefetchScalarGridSpec(
             num_scalar_prefetch=1,
             grid=(parts,),
-            in_specs=[pl.BlockSpec((rows, width), lambda p, order: (0, 0))] * parts
+            in_specs=[piece] * parts
             + ([] if base is None else [flat]),
             out_specs=flat,
         ),
@@ -1013,13 +1037,20 @@
     )(order, in_hbm(rows), in_hbm(weight))
 
 
+def spread_parts(part, product, own_ref, other_ref):
+    parts = 2 * own_ref.shape[0]
+    width = product.shape[0] // parts
+    for p in range(parts):
+        here = pl.ds(pl.multiple_of((part ^ p) * width, width), width)
+        yield (other_ref if p % 2 else own_ref), p // 2, here
+
+
 def emit_body(order_ref, *refs):
     pieces_ref, refs = refs[0], refs[1:]
     parts = pieces_ref.shape[0]
-    (weight_ref, rows_ref, kept_ref, first_ref, second_ref, own_ref, other_ref) = refs[:7]
-    (dgate_ref, gated, product) = refs[7:]
-    turn = pl.program_id(0)
-    half = pl.num_programs(0) // 4
+    (weight_ref, rows_ref, normed_ref, turned_ref) = refs[:4]
+    (kept_ref, sent_ref, own_ref, other_ref, dgate_ref, gain_ref) = refs[4:10]
+    (gated, product, second) = refs[10:]
     count, quarter, width = pieces_ref.shape[2:]
 
     @pl.when(pl.program_id(0) == 0)
@@ -1033,34 +1064,31 @@
 
     values = gated[...]
     branch = jnp.dot(values, weight_ref[...], preferred_element_type=wide).astype(low)
-    for k in range(count // 2):
-        kept_ref[k] = branch[k * quarter : (k + 1) * quarter]
-    other = branch[count // 2 * quarter :].reshape(count // 2, quarter, branch.shape[1])
-
-    @pl.when(turn < half)
-    def _():
-        first_ref[...] = other
-
-    @pl.when(turn >= half)
-    def _():
-        second_ref[...] = other
-
+    kept_ref[...] = branch[: count // 2 * quarter].reshape(kept_ref.shape)
+    sent_ref[...] = branch[count // 2 * quarter :].reshape(sent_ref.shape)
+    down = (((0,), (0,)), ((), ()))
     product[...] = lax.dot_general(
-        values, rows_ref[...], (((0,), (0,)), ((), ())), preferred_element_type=wide
+        values, rows_ref[...], down, preferred_element_type=wide
     ).astype(low)
-    part = order_ref[count]
-    for p in range(parts):
-        here = pl.ds(pl.multiple_of((part ^ p) * width, width), width)
-        (other_ref if p % 2 else own_ref)[p // 2] = product[here, :]
-
-
-def emit(order, pieces, weight, rows):
+    found = lax.dot_general(
+        dgate_ref[...], normed_ref[...], down, preferred_element_type=wide
+    )
+    gain_ref[...] = jnp.sum(found * turned_ref[...].astype(wide), axis=0, keepdims=True)
+    second[...] = found.astype(low)
+    for ref, p, here in spread_parts(order_ref[count], product, own_ref, other_ref):
+        ref[p, 0] = product[here, :]
+        ref[p, 1] = second[here, :]
+
+
+def emit(order, pieces, weight, rows, normed, turned):
     parts, _, count, quarter, width = pieces.shape
     depth = weight.shape[1]
     tile = 512
-    half = depth // tile // 4
     chans = parts * width
     tall = count * quarter
+    blocks = pl.BlockSpec((count // 2, quarter, tile), lambda t, order: (0, 0, t))
+    grads = pl.BlockSpec((parts // 2, 2, width, tile), lambda t, order: (0, 0, 0, t))
+    columns = pl.BlockSpec((tall, tile), lambda t, order: (0, t))
     return pl.pallas_call(
         emit_body,
         grid_spec=pltpu.PrefetchScalarGridSpec(
@@ -1069,34 +1097,76 @@
             in_specs=[
                 pl.BlockSpec(pieces.shape, lambda t, order: (0, 0, 0, 0, 0)),
                 pl.BlockSpec((chans, tile), lambda t, order: (0, t)),
-                pl.BlockSpec((tall, tile), lambda t, order: (0, t)),
+                columns,
+                columns,
+                pl.BlockSpec((chans, tile), lambda t, order: (1, t)),
             ],
             out_specs=[
-                pl.BlockSpec((count // 2, quarter, tile), lambda t, order: (0, 0, t)),
-                pl.BlockSpec(
-                    (count // 2, quarter, tile), lambda t, order: (0, 0, jnp.minimum(t, half - 1))
-                ),
-                pl.BlockSpec(
-                    (count // 2, quarter, tile), lambda t, order: (0, 0, jnp.maximum(t - half, 0))
-                ),
-                pl.BlockSpec((parts // 2, width, tile), lambda t, order: (0, 0, t)),
-                pl.BlockSpec((parts // 2, width, tile), lambda t, order: (0, 0, t)),
+                blocks,
+                blocks,
+                grads,
+                grads,
                 pl.BlockSpec((tall, chans), lambda t, order: (0, 0)),
+                pl.BlockSpec((1, tile), lambda t, order: (0, t)),
             ],
-            scratch_shapes=[pltpu.VMEM((tall, chans), low), pltpu.VMEM((chans, tile), low)],
+            scratch_shapes=[
+                pltpu.VMEM((tall, chans), low),
+                pltpu.VMEM((chans, tile), low),
+                pltpu.VMEM((chans, tile), low),
+            ],
         ),
         out_shape=[
             pltpu.HBM((count // 2, quarter, depth), low),
-            pltpu.HBM((count // 2, quarter, half * tile), low),
-            pltpu.HBM((count // 2, quarter, depth - half * tile), low),
+            pltpu.HBM((count // 2, quarter, depth), low),
+            pltpu.HBM((parts // 2, 2, width, depth), low),
+            pltpu.HBM((parts // 2, 2, width, depth), low),
+            pltpu.HBM((tall, chans), low),
+            jax.ShapeDtypeStruct((1, depth), wide),
+        ],
+        compiler_params=pltpu.CompilerParams(vmem_limit_bytes=24 * 1024 * 1024),
+        cost_estimate=spent(6),
+        name="emit",
+    )(order, *map(in_hbm, (pieces, weight, rows, normed, turned)))
+
+
+def weigh_body(order_ref, rows_ref, normed_ref, turned_ref, own_ref, other_ref, gain_ref, product):
+    found = lax.dot_general(
+        rows_ref[...], normed_ref[...], (((0,), (0,)), ((), ())), preferred_element_type=wide
+    )
+    gain_ref[...] = jnp.sum(found * turned_ref[...].astype(wide), axis=0, keepdims=True)
+    product[...] = found.astype(low)
+    for ref, p, here in spread_parts(order_ref[8], product, own_ref, other_ref):
+        ref[p] = product[here, :]
+
+
+def weigh(order, rows, normed, turned, parts):
+    tall, depth = normed.shape
+    chans = rows.shape[1] // 2
+    width = chans // parts
+    tile = 512
+    grads = pl.BlockSpec((parts // 2, width, tile), lambda t, order: (0, 0, t))
+    return pl.pallas_call(
+        weigh_body,
+        grid_spec=pltpu.PrefetchScalarGridSpec(
+            num_scalar_prefetch=1,
+            grid=(depth // tile,),
+            in_specs=[
+                pl.BlockSpec((tall, chans), lambda t, order: (0, 0)),
+                pl.BlockSpec((tall, tile), lambda t, order: (0, t)),
+                pl.BlockSpec((chans, tile), lambda t, order: (0, t)),
+            ],
+            out_specs=[grads, grads, pl.BlockSpec((1, tile), lambda t, order: (0, t))],
+            scratch_shapes=[pltpu.VMEM((chans, tile), low)],
+        ),
+        out_shape=[
             pltpu.HBM((parts // 2, width, depth), low),
             pltpu.HBM((parts // 2, width, depth), low),
-            pltpu.HBM((tall, chans), low),
+            jax.ShapeDtypeStruct((1, depth), wide),
         ],
-        compiler_params=pltpu.CompilerParams(vmem_limit_bytes=20 * 1024 * 1024),
-        cost_estimate=spent(6),
-        name="emit",
-    )(order, in_hbm(pieces), in_hbm(weight), in_hbm(rows))
+        compiler_params=pltpu.CompilerParams(vmem_limit_bytes=16 * 1024 * 1024),
+        cost_estimate=spent(4),
+        name="weigh",
+    )(order, rows, in_hbm(normed), in_hbm(turned))
 
 
 def turn_body(order_ref, *refs):
@@ -1387,13 +1457,14 @@
     columns_chip = moves.over_state(columns, 2)
     decay_own = moves.swap_state(decay_cut)
     in_flat = in_weight.reshape(width, 2 * chans)
-    across, along[0], along[1], along[2], columns_core, columns_chip, decay_own, in_flat, cot_q = tied(
-        across, *along, columns_core, columns_chip, decay_own, in_flat, cot_q
-    )
+    tie = tied(across, *along, columns_core, columns_chip, decay_own, in_flat, cot_q)
+    across, along, columns_core, columns_chip = tie[0], list(tie[1:4]), *tie[4:6]
+    decay_own, in_flat, cot_q = tie[6:]
     grads = lax.all_gather(cot_q, "chan", axis=0)
     over = [moves.over_y(piece) for piece in along]
     columns_slant = moves.over_state(columns_chip, 1)
-    over[0], over[1], over[2], columns_slant = tied(*over, columns_slant)
+    turned = in_flat.T
+    over[0], over[1], over[2], columns_slant, turned = tied(*over, columns_slant, turned)
     pieces = [normed_all] + along + [across] + over
 
     place = positions(lengths, tokens)
@@ -1471,51 +1542,38 @@
     )
     decay_grad_own = coeff * decay_total
     packed = jnp.concatenate([delta_grad_own, decay_grad_own, sums], axis=0).astype(low)
+
     own_sums, other_sums, packed, gated, dscan = tied(
         own_sums, other_sums, packed, gated, dscan
     )
-
     came = moves.over_state(other_sums, 1)
-    branch_kept, sent, second_branch, out_kept, out_sent, dgate_q = emit(
-        places, gated, out_weight, grad_q
-    )
-    came, sent, second_branch, out_sent, dgate_q = tied(
-        came, sent, second_branch, out_sent, dgate_q
-    )
+    dscan = moves.swap_state(dscan)
+    came, own_sums, packed, gated = tied(came, own_sums, packed, gated)
 
     chip = added(own_sums, came)
     came = moves.over_state(chip[1], 2)
-    branch_came = moves.over_y(sent)
-    gate_part = lax.dot_general(normed_q, dgate_q, contract_rows, preferred_element_type=wide)
-    gain = jnp.sum(gate_part * in_flat[:, chans:].astype(wide), axis=1)
-    gate_part = lax.psum_scatter(gate_part.astype(low), "state", scatter_dimension=0, tiled=True)
-    out_came = moves.over_state(out_sent, 1)
-    came, gain, out_came = tied(came, gain, out_came)
+    branch_kept, sent, parts_kept, parts_sent, dgate_q, gain = emit(
+        places, gated, out_weight, grad_q, normed_q, turned
+    )
+    came, sent, parts_sent = tied(came, sent, parts_sent)
 
     joined = added(chip[0], came)
     came = moves.over_y(joined[4:])
-    dscan = moves.swap_state(dscan)
-    out_part = added(out_kept, out_came)
-    out_came = moves.over_state(out_part[1], 2)
-    packed_core = moves.over_state(packed, 1)
-    came, second_branch, packed_core, branch_came = tied(
-        came, second_branch, packed_core, branch_came
-    )
+    parts_came = moves.over_state(parts_sent, 1)
+    came, parts_came, sent = tied(came, parts_came, sent)
 
     joined = added(joined[:4], came)
     along = [moves.over_z(joined, hops) for hops in (1, 2, 3)]
-    second_came = moves.over_y(second_branch)
-    along[0], along[1], along[2], second_came, out_came = tied(*along, second_came, out_came)
+    branch_came = moves.over_y(sent)
+    parts_sum = added(parts_kept, parts_came)
+    parts_came = moves.over_state(parts_sum[1], 2)
+    along[0], along[1], along[2], branch_came, dscan = tied(*along, branch_came, dscan)
 
     partial = total_of(joined, along)
     came = moves.over_y(partial)
-    branch_came = jnp.concatenate([branch_came, second_came], axis=2)
     branch = added(branch_kept, branch_came)
     branches = [moves.over_z(branch[4 - hops], hops) for hops in (1, 2, 3)]
-    out_part = added(out_part[0], out_came)
-    out_chip = moves.over_state(out_part, 2)
-    came, partial, dscan, gate_part = tied(came, partial, dscan, gate_part)
-    gate_grad = lax.all_gather(gate_part, "state", axis=0, tiled=True)
+    came, partial = tied(came, partial)
 
     dboth, rank_part, rows_part = turn_back(
         places,
@@ -1539,41 +1597,26 @@
     left_sent = backed(dboth[other], in_flat[left]).astype(low).reshape(4, quarter, edge)
     right_all = backed(dboth, in_flat[right]).reshape(2, 4, quarter, width - edge)
     right_sent = [right_all[:, 4 - hops].astype(low) for hops in (1, 2, 3)]
-    out_core = moves.over_state(out_part, 1)
-    out_slant = moves.over_state(out_chip, 1)
-    packed_chip = moves.over_state(packed, 2)
-    tie = tied(
-        left_sent, dboth, rank_part, out_core, out_slant, packed_chip, branches[0], *right_sent
-    )
-    left_sent, dboth, rank_part, out_core, out_slant, packed_chip, branches[0] = tie[:7]
-    right_sent = tie[7:]
+    inner_kept, inner_sent, inner_gain = weigh(places, dboth, normed_q, turned, n_state)
+    inner_came = moves.over_state(inner_sent, 1)
+    gain = (gain + inner_gain).reshape(-1, chans)
+    gain = jnp.concatenate([rows_part, gain], axis=0)
+    small = jnp.concatenate([packed, rank_part], axis=0)
+    tie = tied(left_sent, dboth, small, parts_came, inner_came, gain, *branches, *right_sent)
+    left_sent, dboth, small, parts_came, inner_came, gain = tie[:6]
+    branches, right_sent = tie[6:9], tie[9:]
 
     left_came = moves.over_y(left_sent)
     right_along = [moves.over_z(right_sent[hops - 1], hops) for hops in (1, 2, 3)]
-    rank_core = moves.over_state(rank_part, 1)
-    left_kept = backed(dboth[same], in_flat[left]).reshape(4, quarter, edge)
-    inner_part = lax.dot_general(
-        normed_q,
-        after(dboth, right_along[0])[:, :chans],
-        contract_rows,
-        preferred_element_type=wide,
-    )
-    gain = gain + jnp.sum(inner_part * in_flat[:, :chans].astype(wide), axis=1)
-    gain = jnp.concatenate([rows_part, gain.reshape(-1, chans)], axis=0)
+    parts_own = added(parts_sum[0], parts_came)
+    parts_chip = moves.over_state(parts_own, 2)
+    gain_came = moves.over_state(gain, 1)
+    left_kept = backed(after(dboth, right_along[0])[same], in_flat[left])
+    left_kept = left_kept.reshape(4, quarter, edge)
     branch = total_of(branch[0], branches)
-    tie = tied(
-        left_came,
-        left_kept,
-        inner_part.astype(low),
-        gain,
-        branch,
-        gate_grad,
-        rank_core,
-        *right_along,
-    )
-    left_came, left_kept, inner_part, gain, branch, gate_grad, rank_core = tie[:7]
-    right_along = tie[7:]
-    inner_part = lax.psum_scatter(inner_part, "state", scatter_dimension=0, tiled=True)
+    tie = tied(left_came, left_kept, gain, gain_came, branch, parts_chip, *right_along)
+    left_came, left_kept, gain, gain_came, branch, parts_chip = tie[:6]
+    right_along = tie[6:]
 
     joined = left_kept + left_came.astype(wide)
     left_sum = joined[0]
@@ -1582,12 +1625,14 @@
     for piece in right_along:
         right_sum = right_sum + piece.astype(wide)
     right_came = moves.over_y(right_sum[1].astype(low))
-    gain_came = moves.over_state(gain, 1)
-    out_grad = placed(ranks, (out_part, out_core, out_chip, out_slant))
-    packed_slant = moves.over_state(packed_chip, 1)
-    tie = tied(right_came, gain_came, out_grad, packed_slant, *left_along)
-    right_came, gain_came, out_grad, packed_slant = tie[:4]
-    left_along = tie[4:]
+    inner_sum = added(inner_kept, inner_came)
+    inner_came = moves.over_state(inner_sum[1], 2)
+    gain = gain + gain_came
+    gain_came = moves.over_state(gain, 2)
+    small_core = moves.over_state(small, 1)
+    tie = tied(right_came, gain, gain_came, inner_came, small_core, *left_along)
+    right_came, gain, gain_came, inner_came, small_core = tie[:5]
+    left_along = tie[5:]
 
     for piece in left_along:
         left_sum = left_sum + piece.astype(wide)
@@ -1598,45 +1643,69 @@
     change = change.astype(low)
     change_chip = moves.over_state(change, 2)
     change_core = moves.over_state(change, 1)
+    inner_own = added(inner_sum[0], inner_came)
+    inner_chip = moves.over_state(inner_own, 2)
     gain = gain + gain_came
-    gain_came = moves.over_state(gain, 2)
-    rank_sum = added(rank_part, rank_core)
-    rank_chip = moves.over_state(rank_sum, 2)
-    packed = moves.in_order((packed, packed_core, packed_chip, packed_slant))
+    gain_came = moves.over_y(gain[8 + 2 * states :].reshape(width))
+    inner_core = moves.over_state(inner_own, 1)
+    parts_core = moves.over_state(parts_own, 1)
+    parts_slant = moves.over_state(parts_chip, 1)
+    out_grad = placed(ranks, (parts_own, parts_core, parts_chip, parts_slant))
+    place_at = 8 + part * per_state
+    smalls = (
+        gain[:taps],
+        gain[taps],
+        lax.dynamic_slice_in_dim(gain, place_at, per_state, 0).T,
+        lax.dynamic_slice_in_dim(gain, place_at + states, per_state, 0).T,
+    )
+    tie = tied(
+        change_chip,
+        change_core,
+        gain,
+        gain_came,
+        inner_chip,
+        inner_core,
+        parts_core,
+        parts_slant,
+        out_grad,
+        *smalls,
+    )
+    change_chip, change_core, gain, gain_came, inner_chip, inner_core = tie[:6]
+    parts_core, parts_slant, out_grad = tie[6:9]
+    smalls = tie[9:]
+
+    inner_slant = moves.over_state(inner_chip, 1)
+    branch_chip = moves.over_state(branch, 2)
+    branch_core = moves.over_state(branch, 1)
+    change_slant = moves.over_state(change_chip, 1)
+    fixed = packed.shape[0]
+    rank_sum = added(small[fixed:], small_core[fixed:])
+    small_sum = jnp.concatenate([small[:fixed], rank_sum], axis=0)
+    small_chip = moves.over_state(small_sum, 2)
+    gain = gain[8 + 2 * states :].reshape(width) + gain_came
+    in_grad = interleave(
+        ranks,
+        (inner_own, inner_core, inner_chip, inner_slant),
+        (parts_own, parts_core, parts_chip, parts_slant),
+    )
+    tie = tied(branch_chip, branch_core, change_slant, small_chip, gain, in_grad)
+    branch_chip, branch_core, change_slant, small_chip, gain, in_grad = tie
+
+    branch_slant = moves.over_state(branch_chip, 1)
+    packed_slant = moves.over_state(small_chip[:fixed], 1)
+    gains = [gain] + [moves.over_z(gain, hops) for hops in (1, 2, 3)]
+    rank_grad = rank_sum.astype(wide) + small_chip[fixed:].astype(wide)
+    packed = moves.in_order((packed, small_core[:fixed], small_chip[:fixed], packed_slant))
     packed = jnp.swapaxes(packed, 0, 1).reshape(-1, chans).astype(wide)
-    packs = (
+    smalls = (
+        *smalls[:2],
+        rank_grad,
+        *smalls[2:],
         packed[:rank],
         packed[rank + states],
         lax.dynamic_slice_in_dim(packed, rank + part * per_state, per_state, 0),
         packed[rank + states + 1],
     )
-    tie = tied(change_chip, change_core, gain_came, rank_chip, inner_part, *packs)
-    change_chip, change_core, gain_came, rank_chip, inner_part = tie[:5]
-    packs = tie[5:]
-    inner_grad = lax.all_gather(inner_part, "state", axis=0, tiled=True)
-
-    change_slant = moves.over_state(change_chip, 1)
-    branch_chip = moves.over_state(branch, 2)
-    branch_core = moves.over_state(branch, 1)
-    gain = gain + gain_came
-    gain_came = moves.over_y(gain[8 + 2 * states :].reshape(width))
-    rank_grad = rank_sum.astype(wide) + rank_chip.astype(wide)
-    place_at = 8 + part * per_state
-    smalls = (
-        gain[:taps],
-        gain[taps],
-        rank_grad,
-        lax.dynamic_slice_in_dim(gain, place_at, per_state, 0).T,
-        lax.dynamic_slice_in_dim(gain, place_at + states, per_state, 0).T,
-        *packs,
-    )
-    tie = tied(change_slant, branch_chip, branch_core, gain_came, gain, *smalls)
-    change_slant, branch_chip, branch_core, gain_came, gain = tie[:5]
-    smalls = tie[5:]
-
-    branch_slant = moves.over_state(branch_chip, 1)
-    gain = gain[8 + 2 * states :].reshape(width) + gain_came
-    gains = [gain] + [moves.over_z(gain, hops) for hops in (1, 2, 3)]
     input_grad = placed(ranks, (change, change_core, change_chip, change_slant), cotangent)
     result = placed(ranks, (branch, branch_core, branch_chip, branch_slant), hidden_in)
     gains = jnp.stack(gains)
@@ -1646,7 +1715,6 @@
             gains, (moves.z + 4 - plane_at) % 4, 0, keepdims=False
         )
     gain_grad = gain_grad / norm_gain
-    in_grad = interleave(inner_grad, gate_grad)
     return (result, input_grad, gain_grad, in_grad, *smalls, out_grad)
 
 

time: 350 us -> 345 us (0.986)
  starting transfers between devices: 97.1 us -> 81.2 us
  Pallas kernels: 80.1 us -> 89.1 us
  local copies, waits for them, and re-layouts: 23.7 us -> 29.8 us
  matrix products: 12.3 us -> 6.86 us
    ppermute x21, starting transfers between devices: 50.7 us -> 36.9 us  [over_z(): lax.ppermute(values, 'chan', [(i, (i + 2 * hops) % 8) for i in range(8)])]
    ppermute x13 -> x12, waiting for transfers between devices: 38.8 us -> 51 us  [over_y(): return lax.ppermute(values, 'chan', [(i, i ^ 1) for i in range(8)])]
    pallas_call x1 -> x2, Pallas kernels: 5.09 us -> 14.7 us  [the longest x1 8.97 us: interleave(): pl.pallas_call(functools.partial(interleave_body, parts), grid_spec=pltpu...]
    dot_general x2 -> x0, matrix products: 7.03 us -> none  [the longest x1 4.36 us: near_shards(): lax.dot_general(normed_q, dgate_q, contract_rows, preferred_element_type=...]
    ppermute x21, waiting for transfers between devices: 15.9 us -> 9.38 us  [over_z(): lax.ppermute(values, 'chan', [(i, (i + 2 * hops) % 8) for i in range(8)])]
    optimization_barrier x0 -> x1, local copies, waits for them, and re-layouts: none -> 6.41 us  [tied(): return lax.optimization_barrier(values)]
    all_gather x1, waiting for transfers between devices: 2.16 us -> 6.98 us  [near_shards(): grads = lax.all_gather(cot_q, 'chan', axis=0)]
    convert_element_type x8 -> x10, other arithmetic: 6.79 us -> 9.65 us  [added(): return (kept.astype(wide) + came.astype(wide)).astype(low)]
  transfers between devices with their start and end apart: 72 -> 70, of which waited for: 22 -> 22; matrix products, arithmetic and copies ran while one was open for 13% -> 15% of each run, Pallas kernels for 17% -> 21%
where the time goes in v2:
time: 345 us; the launch traced here: 343 us
  waiting for transfers between devices  99.2 us (29%)
  Pallas kernels  89.1 us (26%)
  starting transfers between devices  81.2 us (24%)
  local copies, waits for them, and re-layouts  29.8 us (9%)
  other arithmetic  22.2 us (6%)
  between operations  15 us (4%)
  matrix products  6.86 us (2%)
    ppermute x12, waiting for transfers between devices, over_y(): return lax.ppermute(values, 'chan', [(i, i ^ 1) for i in range(8)])  51 us
    ppermute x21, starting transfers between devices, over_z(): lax.ppermute(values, 'chan', [(i, (i + 2 * hops) % 8) for i in range(8)])  36.9 us
    ppermute x32, waiting for transfers between devices, over_state(): return lax.ppermute(values, 'state', [(i, i ^ bits) for i in range(4)])  31.8 us
    pallas_call x1, Pallas kernels, backward_scan(): pl.pallas_call(functools.partial(backward_body, parts), grid_spec=pltpu.P...  21.5 us
    ppermute x32, starting transfers between devices, over_state(): return lax.ppermute(values, 'state', [(i, i ^ bits) for i in range(4)])  17.5 us
    pallas_call x1, Pallas kernels, forward_scan(): pl.pallas_call(functools.partial(forward_body, parts), grid_spec=pltpu.Pr...  14.1 us
    all_to_all x4, starting transfers between devices, swap_state(): return lax.all_to_all(values, 'state', 0, 0, tiled=True)  14 us
    ppermute x12, starting transfers between devices, over_y(): return lax.ppermute(values, 'chan', [(i, i ^ 1) for i in range(8)])  12.9 us
  transfers between devices with their start and end apart: 70, of which 22 were waited for; matrix products, arithmetic and copies ran while one was open for 15% of the time, Pallas kernels for 21%

profile of v2, /device:TPU:0, one launch (start us, length us, event | category | flops | bytes accessed | tf_op | source)
XLA Modules:
  0.0 343.4 jit_solution(16193810238339387392)
XLA Ops:
  19.8 3.3 all-to-all-start
  26.2 11.1 %copy.48 = bf16[2048,2,512]{0,2,1:T(8,128)(2,1)} copy(bf16[2048,2,512]{2,1,0:T(2,128)(2,1)} %param.22) | data formatting | bytes 8388608 | tf_op args[2]
  44.0 6.4 %copy.52.refs_8_ = bf16[2048,1024]{1,0:T(8,128)(2,1)} copy(bf16[2048,1024]{0,1:T(8,128)(2,1)} %bitcast.162) | data formatting | bytes 8388608 | tf_op jit(solution)/shard_map/optimization_barrier | solution.py:1352
  51.2 9.2 %collective-permute-done.7.refs_6_ = bf16[72,2048]{1,0:T(8,128)(2,1)} collective-permute-done((bf16[72,2048]{1,0:T(8,128)(2,1)S(1)}, bf16[72,2048]{1,0:T(8,128)(2,1)}, u32[]{:S(2)}, u32[]{:S(2)}) %collective-permute-start.7) | collective-permute-done | bytes 294944 | tf_op jit(solution)/shard_map/ppermute | solution.py:1324
  60.4 5.2 %collective-permute-done.8.refs_7_ = bf16[72,2048]{1,0:T(8,128)(2,1)} collective-permute-done((bf16[72,2048]{1,0:T(8,128)(2,1)}, bf16[72,2048]{1,0:T(8,128)(2,1)}, u32[]{:S(2)}, u32[]{:S(2)}) %collective-permute-start.8) | collective-permute-done | bytes 294944 | tf_op jit(solution)/shard_map/ppermute | solution.py:1324
  67.6 9.9 %project.1 = (bf16[512,2048]{1,0:T(8,128)(2,1)}, f32[8,80,512]{2,1,0:T(8,128)}, bf16[4,2,8,64,128]{4,3,2,1,0:T(8,128)(2,1)}, f32[4,64,160]{2,1,0:T(8,128)S(1)}, bf16[4,64,160]{2,1,0:T(8,128)(2,1)S(1)}) custom-call(s32[20]{0:T(128)S(1)} %pad_add_fusion.1.place_ref, bf16[72,2048]{1,0:T(8,128)(2,1)} %copy-done.19, bf16[72,2048]{1,0:T(8,128)(2,1)} %copy-done.23, ...), custom_call_target="tpu_custom_call" | custom-call | bytes 28800000 | tf_op jit(solution)/shard_map/project/pallas_call | solution.py:946
  78.0 8.0 %collective-permute-done.10 = bf16[4,64,160]{2,1,0:T(8,128)(2,1)S(1)} collective-permute-done((bf16[4,64,160]{2,1,0:T(8,128)(2,1)S(1)}, bf16[4,64,160]{2,1,0:T(8,128)(2,1)S(1)}, u32[]{:S(2)}, u32[]{:S(2)}) %collective-permute-start.10) | collective-permute-done | bytes 81952 | tf_op jit(solution)/shard_map/ppermute | solution.py:1324
  86.0 3.5 %collective-permute-start.11 = (bf16[4,64,160]{2,1,0:T(8,128)(2,1)S(1)}, bf16[4,64,160]{2,1,0:T(8,128)(2,1)}, u32[]{:S(2)}, u32[]{:S(2)}) collective-permute-start(bf16[4,64,160]{2,1,0:T(8,128)(2,1)S(1)} %add_convert_fusion.8), channel_id=1, source_target_pairs={{0,8},{4,12},{8,16},{12,20},{16,24},{20,28},{24,0},{28,4},{1,9},{5... | collective-permute-start | bytes 245768 | tf_op jit(solution)/shard_map/ppermute | solution.py:1327
  92.8 3.5 %all-to-all-start.1 = ((bf16[4,2,8,64,128]{4,3,2,1,0:T(8,128)(2,1)}), bf16[4,2,8,64,128]{4,3,2,1,0:T(8,128)(2,1)S(1)}, u32[]{:S(2)}, u32[]{:S(2)}) async-start(bf16[4,2,8,64,128]{4,3,2,1,0:T(8,128)(2,1)} %get-tuple-element.178), calls=%async_computation.1 | async-start | bytes 2097152 | tf_op jit(solution)/shard_map/all_to_all | solution.py:1333
  96.3 7.0 %all-gather.3.cloned.1.call-done = bf16[512,2048]{1,0:T(8,128)(2,1)} async-done(((bf16[64,2048]{1,0:T(8,128)(2,1)}), bf16[512,2048]{1,0:T(8,128)(2,1)}) %all-gather.3.cloned.1.call-update) | async-done | bytes 2097168 | tf_op jit(solution)/shard_map/all_gather | solution.py:1463
  103.3 5.7 %pull.1 = (bf16[512,2048]{1,0:T(8,128)(2,1)}, bf16[8,64,128]{2,1,0:T(8,128)(2,1)}, bf16[8,64,128]{2,1,0:T(8,128)(2,1)}, bf16[8,64,128]{2,1,0:T(8,128)(2,1)}, bf16[8,64,128]{2,1,0:T(8,128)(2,1)}) custom-call(s32[9]{0:T(128)S(1)} %add_convert_fusion.9.order_ref, bf16[8,64,2048]{2,1,0:T(8,128)(2,1)} %bitcast.168, bf16[512,2048]{1,0:T(8,128)(2,1)} %refs_1_.1), custom_call_target="tpu_custom_call" | custom-call | bytes 21600000 | tf_op jit(solution)/shard_map/pull/pallas_call | solution.py:1019
  110.9 4.2 %collective-permute-done.14 = bf16[4,64,160]{2,1,0:T(8,128)(2,1)S(1)} collective-permute-done((bf16[4,64,160]{2,1,0:T(8,128)(2,1)S(1)}, bf16[4,64,160]{2,1,0:T(8,128)(2,1)S(1)}, u32[]{:S(2)}, u32[]{:S(2)}) %collective-permute-start.14) | collective-permute-done | bytes 81952 | tf_op jit(solution)/shard_map/ppermute | solution.py:1324
  119.5 4.9 %collective-permute-done.16.refs_2_ = bf16[8,64,160]{2,1,0:T(8,128)(2,1)} collective-permute-done((bf16[8,64,160]{2,1,0:T(8,128)(2,1)}, bf16[8,64,160]{2,1,0:T(8,128)(2,1)}, u32[]{:S(2)}, u32[]{:S(2)}) %collective-permute-start.16) | collective-permute-done | bytes 163872 | tf_op jit(solution)/shard_map/ppermute | solution.py:1330
  128.3 14.1 %forward_scan.1 = (bf16[32768,128]{1,0:T(8,128)(2,1)}, f32[2048,128]{1,0:T(8,128)}, bf16[4,2,8,64,128]{4,3,2,1,0:T(8,128)(2,1)}) custom-call(s32[17]{0:T(128)S(1)} %add_convert_fusion.10.order_ref, bf16[8,64,160]{2,1,0:T(8,128)(2,1)} %pad_maximum_fusion.2.refs_0_, bf16[8,64,160]{2,1,0:T(8,128)(2,1)} %collective-permute-done.15.refs_1_, ...), custom_call_target="tpu_custom_call" | custom-call | bytes 43200000 | tf_op jit(solution)/shard_map/forward_scan/pallas_call | solution.py:695
  142.4 3.7 %all-to-all-start.2 = ((bf16[4,2,8,64,128]{4,3,2,1,0:T(8,128)(2,1)}), bf16[4,2,8,64,128]{4,3,2,1,0:T(8,128)(2,1)S(1)}, u32[]{:S(2)}, u32[]{:S(2)}) async-start(bf16[4,2,8,64,128]{4,3,2,1,0:T(8,128)(2,1)} %get-tuple-element.196), calls=%async_computation.2 | async-start | bytes 2097152 | tf_op jit(solution)/shard_map/all_to_all | solution.py:1333
  146.1 21.5 %backward_scan.1 = (bf16[2,8,80,160]{3,2,1,0:T(8,128)(2,1)}, bf16[2,8,80,160]{3,2,1,0:T(8,128)(2,1)}, bf16[4,8,80,128]{3,2,1,0:T(8,128)(2,1)}, f32[128,128]{1,0:...) custom-call(s32[17]{0:T(128)S(1)} %add_convert_fusion.10.order_ref, ...), custom_call_target="tpu_custom_call" | custom-call | bytes 68400000 | tf_op jit(solution)/shard_map/backward_scan/pallas_call | solution.py:744
  173.3 9.4 %emit.1 = (bf16[4,64,2048]{2,1,0:T(8,128)(2,1)}, bf16[4,64,2048]{2,1,0:T(8,128)(2,1)}, bf16[2,2,128,2048]{3,2,1,0:T(8,128)(2,1)}, bf16[2,2,128,2048]{3,2,1,0:T(8...) custom-call(s32[9]{0:T(128)S(1)} %add_convert_fusion.9.order_ref, bf16[4,2,8,64,128]{4,3,2,1,0:T(8,128)(2,1)} %copy-done.18, ...), custom_call_target="tpu_custom_call" | custom-call | bytes 21600000 | tf_op jit(solution)/shard_map/emit/pallas_call | solution.py:1092
  183.8 3.5 %all-to-all-start.3 = ((bf16[4,8,80,128]{3,2,1,0:T(8,128)(2,1)}), bf16[4,8,80,128]{3,2,1,0:T(8,128)(2,1)S(1)}, u32[]{:S(2)}, u32[]{:S(2)}) async-start(bf16[4,8,80,128]{3,2,1,0:T(8,128)(2,1)} %get-tuple-element.215), calls=%async_computation.3 | async-start | bytes 1310720 | tf_op jit(solution)/shard_map/all_to_all | solution.py:1333
  191.1 3.5 %collective-permute-start.27 = (bf16[4,80,160]{2,1,0:T(8,128)(2,1)S(1)}, bf16[4,80,160]{2,1,0:T(8,128)(2,1)}, u32[]{:S(2)}, u32[]{:S(2)}) collective-permute-start(bf16[4,80,160]{2,1,0:T(8,128)(2,1)S(1)} %add_convert_fusion.5), channel_id=1, source_target_pairs={{0,24},{4,28},{8,0},{12,4},{16,8},{20,12},{24,16},{28,20},{1,25},{... | collective-permute-start | bytes 307208 | tf_op jit(solution)/shard_map/ppermute | solution.py:1327
  195.2 3.0 add_convert_fusion
  200.5 5.1 %collective-permute-done.26 = bf16[4,80,160]{2,1,0:T(8,128)(2,1)S(1)} collective-permute-done((bf16[4,80,160]{2,1,0:T(8,128)(2,1)S(1)}, bf16[4,80,160]{2,1,0:T(8,128)(2,1)S(1)}, u32[]{:S(2)}, u32[]{:S(2)}) %collective-permute-start.26) | collective-permute-done | bytes 102432 | tf_op jit(solution)/shard_map/ppermute | solution.py:1327
  205.6 13.5 %collective-permute-done.28 = bf16[4,64,2048]{2,1,0:T(8,128)(2,1)} collective-permute-done((bf16[4,64,2048]{2,1,0:T(8,128)(2,1)}, bf16[4,64,2048]{2,1,0:T(8,128)(2,1)}, u32[]{:S(2)}, u32[]{:S(2)}) %collective-permute-start.28) | collective-permute-done | bytes 1048608 | tf_op jit(solution)/shard_map/ppermute | solution.py:1324
  228.6 5.9 %turn_back.1 = (bf16[512,1024]{1,0:T(8,128)(2,1)S(1)}, bf16[512,128]{1,0:T(8,128)(2,1)}, f32[40,512]{1,0:T(8,128)S(1)}) custom-call(s32[9]{0:T(128)S(1)} %add_convert_fusion.9.order_ref, bf16[4,80,160]{2,1,0:T(8,128)(2,1)S(1)} %add_convert_fusion.4.refs_0_, bf16[4,80,160]{2,1,0:T(8,128)(2,1)S(1)} %collective-permute-done.29.refs_1_, ...), custom_call_target="tpu_custom_call" | custom-call | bytes 19800000 | tf_op jit(solution)/shard_map/turn_back/pallas_call | solution.py:1262
  234.5 5.7 %weigh.1 = (bf16[2,128,2048]{2,1,0:T(8,128)(2,1)}, bf16[2,128,2048]{2,1,0:T(8,128)(2,1)}, f32[1,2048]{1,0:T(1,128)S(1)}) custom-call(s32[9]{0:T(128)S(1)} %add_convert_fusion.9.order_ref, bf16[512,1024]{1,0:T(8,128)(2,1)S(1)} %get-tuple-element.239.rows_ref, bf16[512,2048]{1,0:T(8,128)(2,1)} %get-tuple-element.206.refs_3_.normed_ref, ...), custom_call_target="tpu_custom_call" | custom-call | bytes 14400000 | tf_op jit(solution)/shard_map/weigh/pallas_call | solution.py:1148
  260.2 3.7 %collective-permute-done.39 = bf16[2,64,640]{2,1,0:T(8,128)(2,1)S(1)} collective-permute-done((bf16[2,64,640]{2,1,0:T(8,128)(2,1)S(1)}, bf16[2,64,640]{2,1,0:T(8,128)(2,1)S(1)}, u32[]{:S(2)}, u32[]{:S(2)}) %collective-permute-start.39) | collective-permute-done | bytes 163872 | tf_op jit(solution)/shard_map/ppermute | solution.py:1327
  263.9 4.5 %collective-permute-done.35 = bf16[4,64,1408]{2,1,0:T(8,128)(2,1)S(1)} collective-permute-done((bf16[4,64,1408]{2,1,0:T(8,128)(2,1)S(1)}, bf16[4,64,1408]{2,1,0:T(8,128)(2,1)S(1)}, u32[]{:S(2)}, u32[]{:S(2)}) %collective-permute-start.35) | collective-permute-done | bytes 720928 | tf_op jit(solution)/shard_map/ppermute | solution.py:1324
  268.4 5.5 %collective-permute-done.38.refs_2_.refs_6_ = bf16[2,128,2048]{2,1,0:T(8,128)(2,1)S(1)} collective-permute-done((bf16[2,128,2048]{2,1,0:T(8,128)(2,1)S(1)}, bf16[2,128,2048]{2,1,0:T(8,128)(2,1)S(1)}, u32[]{:S(2)}, u32[]{:S(2)}) %collective-permute-start.38) | collective-permute-done | bytes 1048608 | tf_op jit(solution)/shard_map/ppermute | solution.py:1330
  280.6 4.5 %collective-permute-done.45 = bf16[128,2048]{1,0:T(8,128)(2,1)S(1)} collective-permute-done((bf16[128,2048]{1,0:T(8,128)(2,1)S(1)}, bf16[128,2048]{1,0:T(8,128)(2,1)S(1)}, u32[]{:S(2)}, u32[]{:S(2)}) %collective-permute-start.45) | collective-permute-done | bytes 524320 | tf_op jit(solution)/shard_map/ppermute | solution.py:1330
  286.6 3.0 collective-permute-done.43
  299.5 11.2 %collective-permute-done.50.refs_2_ = bf16[64,2048]{1,0:T(8,128)(2,1)S(1)} collective-permute-done((bf16[64,2048]{1,0:T(8,128)(2,1)S(1)}, bf16[64,2048]{1,0:T(8,128)(2,1)S(1)}, u32[]{:S(2)}, u32[]{:S(2)}) %collective-permute-start.50) | collective-permute-done | bytes 262176 | tf_op jit(solution)/shard_map/ppermute | solution.py:1330
  313.0 9.0 %interleave.1 = f32[2048,2,512]{2,1,0:T(2,128)} custom-call(s32[4]{0:T(128)S(1)} %xor_convert_fusion.order_ref, bf16[128,2048]{1,0:T(8,128)(2,1)S(1)} %fusion.6.refs_0_, bf16[128,2048]{1,0:T(8,128)(2,1)S(1)} %collective-permute-done.54.refs_1_, bf16[128,2048]{1,0:T(8,128)(2,1)S(1)} %collective-permute-done.53.refs_2_, ...), custom_call_target="tpu_custom_call" | custom-call | bytes 18000000 | tf_op jit(solution)/shard_map/interleave/pallas_call | solution.py:807
  322.0 3.1 collective-permute-start.61
  (298 shorter events, 113.1 us)
Async XLA Ops:
  11.2 26.1 %collective-permute-start = (bf16[72,2048]{1,0:T(8,128)(2,1)S(1)}, bf16[72,2048]{1,0:T(8,128)(2,1)S(1)}, u32[]{:S(2)}, u32[]{:S(2)}) collective-permute-start(bf16[72,2048]{1,0:T(8,128)(2,1)S(1)} %get-tuple-element.290.refs_0_), channel_id=1, source_target_pairs={{0,4},{4,0},{8,12},{12,8},{16,20},{20,16},{24,28},{28,24},{1,5},{5... | collective-permute-start | bytes 884744 | tf_op jit(solution)/shard_map/ppermute | solution.py:1324
  14.2 23.2 %collective-permute-start.1 = (bf16[72,2048]{1,0:T(8,128)(2,1)S(1)}, bf16[72,2048]{1,0:T(8,128)(2,1)S(1)}, u32[]{:S(2)}, u32[]{:S(2)}) collective-permute-start(bf16[72,2048]{1,0:T(8,128)(2,1)S(1)} %get-tuple-element.290.refs_0_), channel_id=1, source_target_pairs={{0,8},{4,12},{8,16},{12,20},{16,24},{20,28},{24,0},{28,4},{1,9},{5... | collective-permute-start | bytes 884744 | tf_op jit(solution)/shard_map/ppermute | solution.py:1327
  15.8 21.6 %collective-permute-start.2 = (bf16[72,2048]{1,0:T(8,128)(2,1)S(1)}, bf16[72,2048]{1,0:T(8,128)(2,1)S(1)}, u32[]{:S(2)}, u32[]{:S(2)}) collective-permute-start(bf16[72,2048]{1,0:T(8,128)(2,1)S(1)} %get-tuple-element.290.refs_0_), channel_id=1, source_target_pairs={{0,16},{4,20},{8,24},{12,28},{16,0},{20,4},{24,8},{28,12},{1,17},{... | collective-permute-start | bytes 884744 | tf_op jit(solution)/shard_map/ppermute | solution.py:1327
  18.3 19.1 %collective-permute-start.3 = (bf16[72,2048]{1,0:T(8,128)(2,1)S(1)}, bf16[72,2048]{1,0:T(8,128)(2,1)}, u32[]{:S(2)}, u32[]{:S(2)}) collective-permute-start(bf16[72,2048]{1,0:T(8,128)(2,1)S(1)} %get-tuple-element.290.refs_0_), channel_id=1, source_target_pairs={{0,24},{4,28},{8,0},{12,4},{16,8},{20,12},{24,16},{28,20},{1,25},{... | collective-permute-start | bytes 884744 | tf_op jit(solution)/shard_map/ppermute | solution.py:1327
  19.8 17.5 %all-to-all-start = ((f32[4,4,128]{2,1,0:T(4,128)}), f32[4,4,128]{2,1,0:T(4,128)S(1)}, u32[]{:S(2)}, u32[]{:S(2)}) async-start(f32[4,4,128]{2,1,0:T(4,128)} %bitcast.2), calls=%async_computation | async-start | bytes 16384 | tf_op jit(solution)/shard_map/all_to_all | solution.py:1333
  23.1 80.2 %all-gather.3.cloned.1.call-start = ((), (), s32[]{:S(2)}) async-start(), calls=%async_computation.4 | async-start | bytes 2359296 | tf_op jit(solution)/shard_map/all_gather | solution.py:1463
  23.5 13.9 %collective-permute-start.5 = (bf16[512,8]{0,1:T(8,128)(2,1)S(1)}, bf16[512,8]{0,1:T(8,128)(2,1)S(1)}, u32[]{:S(2)}, u32[]{:S(2)}) collective-permute-start(bf16[512,8]{0,1:T(8,128)(2,1)S(1)} %pad_maximum_fusion.14), channel_id=1, source_target_pairs={{0,2},{1,3},{2,0},{3,1},{4,6},{5,7},{6,4},{7,5},{8,10},{9,11},{10,... | collective-permute-start | bytes 24584 | tf_op jit(solution)/shard_map/ppermute | solution.py:1330
  41.8 18.6 %collective-permute-start.7 = (bf16[72,2048]{1,0:T(8,128)(2,1)S(1)}, bf16[72,2048]{1,0:T(8,128)(2,1)}, u32[]{:S(2)}, u32[]{:S(2)}) collective-permute-start(bf16[72,2048]{1,0:T(8,128)(2,1)S(1)} %collective-permute-done.2.refs_2_), channel_id=1, source_target_pairs={{0,4},{4,0},{8,12},{12,8},{16,20},{20,16},{24,28},{28,24},{1,5},{5... | collective-permute-start | bytes 884744 | tf_op jit(solution)/shard_map/ppermute | solution.py:1324
  43.3 22.3 %collective-permute-start.8 = (bf16[72,2048]{1,0:T(8,128)(2,1)}, bf16[72,2048]{1,0:T(8,128)(2,1)}, u32[]{:S(2)}, u32[]{:S(2)}) collective-permute-start(bf16[72,2048]{1,0:T(8,128)(2,1)} %collective-permute-done.3.refs_3_), channel_id=1, source_target_pairs={{0,4},{4,0},{8,12},{12,8},{16,20},{20,16},{24,28},{28,24},{1,5},{5... | collective-permute-start | bytes 884744 | tf_op jit(solution)/shard_map/ppermute | solution.py:1324
  86.0 22.9 %collective-permute-start.11 = (bf16[4,64,160]{2,1,0:T(8,128)(2,1)S(1)}, bf16[4,64,160]{2,1,0:T(8,128)(2,1)}, u32[]{:S(2)}, u32[]{:S(2)}) collective-permute-start(bf16[4,64,160]{2,1,0:T(8,128)(2,1)S(1)} %add_convert_fusion.8), channel_id=1, source_target_pairs={{0,8},{4,12},{8,16},{12,20},{16,24},{20,28},{24,0},{28,4},{1,9},{5... | collective-permute-start | bytes 245768 | tf_op jit(solution)/shard_map/ppermute | solution.py:1327
  89.5 19.5 %collective-permute-start.12 = (bf16[4,64,160]{2,1,0:T(8,128)(2,1)S(1)}, bf16[4,64,160]{2,1,0:T(8,128)(2,1)}, u32[]{:S(2)}, u32[]{:S(2)}) collective-permute-start(bf16[4,64,160]{2,1,0:T(8,128)(2,1)S(1)} %add_convert_fusion.8), channel_id=1, source_target_pairs={{0,16},{4,20},{8,24},{12,28},{16,0},{20,4},{24,8},{28,12},{1,17},{... | collective-permute-start | bytes 245768 | tf_op jit(solution)/shard_map/ppermute | solution.py:1327
  91.3 17.7 %collective-permute-start.13 = (bf16[4,64,160]{2,1,0:T(8,128)(2,1)S(1)}, bf16[4,64,160]{2,1,0:T(8,128)(2,1)}, u32[]{:S(2)}, u32[]{:S(2)}) collective-permute-start(bf16[4,64,160]{2,1,0:T(8,128)(2,1)S(1)} %add_convert_fusion.8), channel_id=1, source_target_pairs={{0,24},{4,28},{8,0},{12,4},{16,8},{20,12},{24,16},{28,20},{1,25},{... | collective-permute-start | bytes 245768 | tf_op jit(solution)/shard_map/ppermute | solution.py:1327
  92.8 31.6 %all-to-all-start.1 = ((bf16[4,2,8,64,128]{4,3,2,1,0:T(8,128)(2,1)}), bf16[4,2,8,64,128]{4,3,2,1,0:T(8,128)(2,1)S(1)}, u32[]{:S(2)}, u32[]{:S(2)}) async-start(bf16[4,2,8,64,128]{4,3,2,1,0:T(8,128)(2,1)} %get-tuple-element.178), calls=%async_computation.1 | async-start | bytes 2097152 | tf_op jit(solution)/shard_map/all_to_all | solution.py:1333
  142.4 25.3 %all-to-all-start.2 = ((bf16[4,2,8,64,128]{4,3,2,1,0:T(8,128)(2,1)}), bf16[4,2,8,64,128]{4,3,2,1,0:T(8,128)(2,1)S(1)}, u32[]{:S(2)}, u32[]{:S(2)}) async-start(bf16[4,2,8,64,128]{4,3,2,1,0:T(8,128)(2,1)} %get-tuple-element.196), calls=%async_computation.2 | async-start | bytes 2097152 | tf_op jit(solution)/shard_map/all_to_all | solution.py:1333
  183.8 16.7 %all-to-all-start.3 = ((bf16[4,8,80,128]{3,2,1,0:T(8,128)(2,1)}), bf16[4,8,80,128]{3,2,1,0:T(8,128)(2,1)S(1)}, u32[]{:S(2)}, u32[]{:S(2)}) async-start(bf16[4,8,80,128]{3,2,1,0:T(8,128)(2,1)} %get-tuple-element.215), calls=%async_computation.3 | async-start | bytes 1310720 | tf_op jit(solution)/shard_map/all_to_all | solution.py:1333
  190.8 14.8 %collective-permute-start.26 = (bf16[4,80,160]{2,1,0:T(8,128)(2,1)S(1)}, bf16[4,80,160]{2,1,0:T(8,128)(2,1)S(1)}, u32[]{:S(2)}, u32[]{:S(2)}) collective-permute-start(bf16[4,80,160]{2,1,0:T(8,128)(2,1)S(1)} %add_convert_fusion.5), channel_id=1, source_target_pairs={{0,16},{4,20},{8,24},{12,28},{16,0},{20,4},{24,8},{28,12},{1,17},{... | collective-permute-start | bytes 307208 | tf_op jit(solution)/shard_map/ppermute | solution.py:1327
  191.1 14.5 %collective-permute-start.27 = (bf16[4,80,160]{2,1,0:T(8,128)(2,1)S(1)}, bf16[4,80,160]{2,1,0:T(8,128)(2,1)}, u32[]{:S(2)}, u32[]{:S(2)}) collective-permute-start(bf16[4,80,160]{2,1,0:T(8,128)(2,1)S(1)} %add_convert_fusion.5), channel_id=1, source_target_pairs={{0,24},{4,28},{8,0},{12,4},{16,8},{20,12},{24,16},{28,20},{1,25},{... | collective-permute-start | bytes 307208 | tf_op jit(solution)/shard_map/ppermute | solution.py:1327
  194.6 24.5 %collective-permute-start.28 = (bf16[4,64,2048]{2,1,0:T(8,128)(2,1)}, bf16[4,64,2048]{2,1,0:T(8,128)(2,1)}, u32[]{:S(2)}, u32[]{:S(2)}) collective-permute-start(bf16[4,64,2048]{2,1,0:T(8,128)(2,1)} %get-tuple-element.214), channel_id=1, source_target_pairs={{0,4},{4,0},{8,12},{12,8},{16,20},{20,16},{24,28},{28,24},{1,5},{5... | collective-permute-start | bytes 3145736 | tf_op jit(solution)/shard_map/ppermute | solution.py:1324
  199.9 46.2 %collective-permute-start.30 = (bf16[2,128,2048]{2,1,0:T(8,128)(2,1)}, bf16[2,128,2048]{2,1,0:T(8,128)(2,1)}, u32[]{:S(2)}, u32[]{:S(2)}) collective-permute-start(bf16[2,128,2048]{2,1,0:T(8,128)(2,1)} %slice_bitcast_fusion.1), channel_id=1, source_target_pairs={{0,2},{1,3},{2,0},{3,1},{4,6},{5,7},{6,4},{7,5},{8,10},{9,11},{10,... | collective-permute-start | bytes 3145736 | tf_op jit(solution)/shard_map/ppermute | solution.py:1330
  223.9 22.2 %collective-permute-start.32 = (bf16[64,2048]{1,0:T(8,128)(2,1)}, bf16[64,2048]{1,0:T(8,128)(2,1)}, u32[]{:S(2)}, u32[]{:S(2)}) collective-permute-start(bf16[64,2048]{1,0:T(8,128)(2,1)} %get-tuple-element.296), channel_id=1, source_target_pairs={{0,8},{4,12},{8,16},{12,20},{16,24},{20,28},{24,0},{28,4},{1,9},{5... | collective-permute-start | bytes 786440 | tf_op jit(solution)/shard_map/ppermute | solution.py:1327
  224.5 21.6 %collective-permute-start.33 = (bf16[64,2048]{1,0:T(8,128)(2,1)}, bf16[64,2048]{1,0:T(8,128)(2,1)}, u32[]{:S(2)}, u32[]{:S(2)}) collective-permute-start(bf16[64,2048]{1,0:T(8,128)(2,1)} %get-tuple-element.295), channel_id=1, source_target_pairs={{0,16},{4,20},{8,24},{12,28},{16,0},{20,4},{24,8},{28,12},{1,17},{... | collective-permute-start | bytes 786440 | tf_op jit(solution)/shard_map/ppermute | solution.py:1327
  225.7 20.5 %collective-permute-start.34 = (bf16[64,2048]{1,0:T(8,128)(2,1)}, bf16[64,2048]{1,0:T(8,128)(2,1)}, u32[]{:S(2)}, u32[]{:S(2)}) collective-permute-start(bf16[64,2048]{1,0:T(8,128)(2,1)} %get-tuple-element.294), channel_id=1, source_target_pairs={{0,24},{4,28},{8,0},{12,4},{16,8},{20,12},{24,16},{28,20},{1,25},{... | collective-permute-start | bytes 786440 | tf_op jit(solution)/shard_map/ppermute | solution.py:1327
  247.9 26.0 %collective-permute-start.38 = (bf16[2,128,2048]{2,1,0:T(8,128)(2,1)S(1)}, bf16[2,128,2048]{2,1,0:T(8,128)(2,1)S(1)}, u32[]{:S(2)}, u32[]{:S(2)}) collective-permute-start(bf16[2,128,2048]{2,1,0:T(8,128)(2,1)S(1)} %fusion.3.refs_0_.refs_4_), channel_id=1, source_target_pairs={{0,2},{1,3},{2,0},{3,1},{4,6},{5,7},{6,4},{7,5},{8,10},{9,11},{10,... | collective-permute-start | bytes 3145736 | tf_op jit(solution)/shard_map/ppermute | solution.py:1330
  251.6 16.8 %collective-permute-start.35 = (bf16[4,64,1408]{2,1,0:T(8,128)(2,1)S(1)}, bf16[4,64,1408]{2,1,0:T(8,128)(2,1)S(1)}, u32[]{:S(2)}, u32[]{:S(2)}) collective-permute-start(bf16[4,64,1408]{2,1,0:T(8,128)(2,1)S(1)} %bitcast.192), channel_id=1, source_target_pairs={{0,4},{4,0},{8,12},{12,8},{16,20},{20,16},{24,28},{28,24},{1,5},{5... | collective-permute-start | bytes 2162696 | tf_op jit(solution)/shard_map/ppermute | solution.py:1324
  258.9 26.2 %collective-permute-start.45 = (bf16[128,2048]{1,0:T(8,128)(2,1)S(1)}, bf16[128,2048]{1,0:T(8,128)(2,1)S(1)}, u32[]{:S(2)}, u32[]{:S(2)}) collective-permute-start(bf16[128,2048]{1,0:T(8,128)(2,1)S(1)} %slice_bitcast_fusion.3), channel_id=1, source_target_pairs={{0,2},{1,3},{2,0},{3,1},{4,6},{5,7},{6,4},{7,5},{8,10},{9,11},{10,... | collective-permute-start | bytes 1572872 | tf_op jit(solution)/shard_map/ppermute | solution.py:1330
  263.9 15.7 %collective-permute-start.46 = (bf16[664,128]{1,0:T(8,128)(2,1)S(1)}, bf16[664,128]{1,0:T(8,128)(2,1)S(1)}, u32[]{:S(2)}, u32[]{:S(2)}) collective-permute-start(bf16[664,128]{1,0:T(8,128)(2,1)S(1)} %pad_maximum_fusion.3), channel_id=1, source_target_pairs={{0,1},{1,0},{2,3},{3,2},{4,5},{5,4},{6,7},{7,6},{8,9},{9,8},{10,11... | collective-permute-start | bytes 509960 | tf_op jit(solution)/shard_map/ppermute | solution.py:1330
  274.1 16.0 %collective-permute-start.47 = (bf16[64,1408]{1,0:T(8,128)(2,1)S(1)}, bf16[64,1408]{1,0:T(8,128)(2,1)S(1)}, u32[]{:S(2)}, u32[]{:S(2)}) collective-permute-start(bf16[64,1408]{1,0:T(8,128)(2,1)S(1)} %get-tuple-element.299), channel_id=1, source_target_pairs={{0,8},{4,12},{8,16},{12,20},{16,24},{20,28},{24,0},{28,4},{1,9},{5... | collective-permute-start | bytes 540680 | tf_op jit(solution)/shard_map/ppermute | solution.py:1327
  290.2 20.5 %collective-permute-start.53 = (bf16[128,2048]{1,0:T(8,128)(2,1)S(1)}, bf16[128,2048]{1,0:T(8,128)(2,1)S(1)}, u32[]{:S(2)}, u32[]{:S(2)}) collective-permute-start(bf16[128,2048]{1,0:T(8,128)(2,1)S(1)} %fusion.6.refs_0_), channel_id=1, source_target_pairs={{0,2},{1,3},{2,0},{3,1},{4,6},{5,7},{6,4},{7,5},{8,10},{9,11},{10,... | collective-permute-start | bytes 1572872 | tf_op jit(solution)/shard_map/ppermute | solution.py:1330
  291.0 19.7 %collective-permute-start.54 = (bf16[128,2048]{1,0:T(8,128)(2,1)S(1)}, bf16[128,2048]{1,0:T(8,128)(2,1)S(1)}, u32[]{:S(2)}, u32[]{:S(2)}) collective-permute-start(bf16[128,2048]{1,0:T(8,128)(2,1)S(1)} %fusion.6.refs_0_), channel_id=1, source_target_pairs={{0,1},{1,0},{2,3},{3,2},{4,5},{5,4},{6,7},{7,6},{8,9},{9,8},{10,11... | collective-permute-start | bytes 1572872 | tf_op jit(solution)/shard_map/ppermute | solution.py:1330
  291.5 19.2 %collective-permute-start.50 = (bf16[64,2048]{1,0:T(8,128)(2,1)S(1)}, bf16[64,2048]{1,0:T(8,128)(2,1)S(1)}, u32[]{:S(2)}, u32[]{:S(2)}) collective-permute-start(bf16[64,2048]{1,0:T(8,128)(2,1)S(1)} %multiply_convert_fusion.1.refs_0_), channel_id=1, source_target_pairs={{0,2},{1,3},{2,0},{3,1},{4,6},{5,7},{6,4},{7,5},{8,10},{9,11},{10,... | collective-permute-start | bytes 786440 | tf_op jit(solution)/shard_map/ppermute | solution.py:1330
  292.9 17.8 %collective-permute-start.51 = (bf16[64,2048]{1,0:T(8,128)(2,1)S(1)}, bf16[64,2048]{1,0:T(8,128)(2,1)S(1)}, u32[]{:S(2)}, u32[]{:S(2)}) collective-permute-start(bf16[64,2048]{1,0:T(8,128)(2,1)S(1)} %multiply_convert_fusion.1.refs_0_), channel_id=1, source_target_pairs={{0,1},{1,0},{2,3},{3,2},{4,5},{5,4},{6,7},{7,6},{8,9},{9,8},{10,11... | collective-permute-start | bytes 786440 | tf_op jit(solution)/shard_map/ppermute | solution.py:1330
  298.9 23.0 %collective-permute-start.41 = (bf16[64,2048]{1,0:T(8,128)(2,1)S(1)}, bf16[64,2048]{1,0:T(8,128)(2,1)S(1)}, u32[]{:S(2)}, u32[]{:S(2)}) collective-permute-start(bf16[64,2048]{1,0:T(8,128)(2,1)S(1)} %fusion.10.refs_0_), channel_id=1, source_target_pairs={{0,2},{1,3},{2,0},{3,1},{4,6},{5,7},{6,4},{7,5},{8,10},{9,11},{10,... | collective-permute-start | bytes 786440 | tf_op jit(solution)/shard_map/ppermute | solution.py:1330
  (70 other events, 587.2 us)
Sparse Core Ops, SparseCore 0:
  37.6 65.6 all-gather.2

commit v3 on v2

--- a/solution.py
+++ b/solution.py
@@ -782,8 +782,7 @@
 def interleave_body(parts, order_ref, *refs):
     values, out_ref = refs[: 2 * parts], refs[2 * parts]
     width, block = values[0].shape
-    places = [lax.broadcasted_iota(jnp.int32, (block, block), axis) for axis in (0, 1)]
-    same = jnp.where(places[0] == places[1], 1.0, 0.0).astype(low)
+    same = diagonal(block)
     for part in range(parts):
 
         @pl.when(order_ref[0] == part)
@@ -855,14 +854,19 @@
     )(order, *values, *(() if base is None else (base,)))
 
 
+def diagonal(size):
+    places = [lax.broadcasted_iota(jnp.int32, (size, size), axis) for axis in (0, 1)]
+    return jnp.where(places[0] == places[1], 1.0, 0.0).astype(low)
+
+
 def project_body(
     place_ref,
     *refs,
 ):
     pieces, refs = refs[:8], refs[8:]
     (weight_ref, flags_ref, taps_ref, offset_ref, select_ref) = refs[:5]
-    (normed_ref, inner_ref, channels_ref, kept_ref, sent_ref) = refs[5:10]
-    (sides, edges, window, total, acts) = refs[10:]
+    (normed_ref, inner_ref, channels_ref, kept_ref, sent_ref, turned_ref) = refs[5:11]
+    (sides, edges, window, total, acts) = refs[11:]
     turn = pl.program_id(0)
     quarter = channels_ref.shape[3]
     width = channels_ref.shape[4]
@@ -881,6 +885,13 @@
         total[...] = jnp.zeros_like(total)
 
     main = jnp.dot(normed_ref[...], weight_ref[...], preferred_element_type=wide)
+    tile = weight_ref.shape[1]
+    same = diagonal(tile)
+    for k in range(weight_ref.shape[0] // tile):
+        here = slice(k * tile, (k + 1) * tile)
+        turned_ref[:, here] = lax.dot_general(
+            same, weight_ref[here, :], (((1,), (1,)), ((), ())), preferred_element_type=wide
+        ).astype(low)
 
     @pl.when(turn < inner_turns)
     def _():
@@ -965,6 +976,7 @@
                 ),
                 whole((count // 2, quarter, small)),
                 whole((count // 2, quarter, small)),
+                pl.BlockSpec((tile, depth), lambda t, place: (t, 0)),
             ],
             scratch_shapes=[
                 pltpu.VMEM((count * 8, depth), wide),
@@ -980,6 +992,7 @@
             jax.ShapeDtypeStruct((parts, 2, count, quarter, width), low),
             jax.ShapeDtypeStruct((count // 2, quarter, small), wide),
             jax.ShapeDtypeStruct((count // 2, quarter, small), low),
+            pltpu.HBM((2 * chans, depth), low),
         ],
         compiler_params=pltpu.CompilerParams(vmem_limit_bytes=28 * 1024 * 1024),
         cost_estimate=spent(8),
@@ -1463,8 +1476,7 @@
     grads = lax.all_gather(cot_q, "chan", axis=0)
     over = [moves.over_y(piece) for piece in along]
     columns_slant = moves.over_state(columns_chip, 1)
-    turned = in_flat.T
-    over[0], over[1], over[2], columns_slant, turned = tied(*over, columns_slant, turned)
+    over[0], over[1], over[2], columns_slant = tied(*over, columns_slant)
     pieces = [normed_all] + along + [across] + over
 
     place = positions(lengths, tokens)
@@ -1491,7 +1503,7 @@
     select = jnp.concatenate([select_rank, columns], axis=1)
     coeff = -jnp.exp(decay_own.reshape(states, own))
 
-    normed_q, inner_all, sent, kept, other = project(
+    normed_q, inner_all, sent, kept, other, turned = project(
         neighbours, pieces, in_flat, flags_rows, conv_kernel, conv_offset[None, :], select, n_state
     )
     reach = quarter + HALO
@@ -1573,7 +1585,10 @@
     came = moves.over_y(partial)
     branch = added(branch_kept, branch_came)
     branches = [moves.over_z(branch[4 - hops], hops) for hops in (1, 2, 3)]
-    came, partial = tied(came, partial)
+    came, partial, parts_came = tied(came, partial, parts_came)
+    parts_own = added(parts_sum[0], parts_came)
+    came, partial, parts_own = tied(came, partial, parts_own)
+    parts_chip = moves.over_state(parts_own, 2)
 
     dboth, rank_part, rows_part = turn_back(
         places,
@@ -1602,14 +1617,12 @@
     gain = (gain + inner_gain).reshape(-1, chans)
     gain = jnp.concatenate([rows_part, gain], axis=0)
     small = jnp.concatenate([packed, rank_part], axis=0)
-    tie = tied(left_sent, dboth, small, parts_came, inner_came, gain, *branches, *right_sent)
-    left_sent, dboth, small, parts_came, inner_came, gain = tie[:6]
-    branches, right_sent = tie[6:9], tie[9:]
+    tie = tied(left_sent, dboth, small, inner_came, gain, *branches, *right_sent)
+    left_sent, dboth, small, inner_came, gain = tie[:5]
+    branches, right_sent = tie[5:8], tie[8:]
 
     left_came = moves.over_y(left_sent)
     right_along = [moves.over_z(right_sent[hops - 1], hops) for hops in (1, 2, 3)]
-    parts_own = added(parts_sum[0], parts_came)
-    parts_chip = moves.over_state(parts_own, 2)
     gain_came = moves.over_state(gain, 1)
     left_kept = backed(after(dboth, right_along[0])[same], in_flat[left])
     left_kept = left_kept.reshape(4, quarter, edge)

time: 345 us -> 337 us (0.977)
  local copies, waits for them, and re-layouts: 29.8 us -> 17.6 us
  other arithmetic: 22.2 us -> 26 us
    ppermute x32, waiting for transfers between devices: 31.8 us -> 38.9 us  [over_state(): return lax.ppermute(values, 'state', [(i, i ^ bits) for i in range(4)])]
    all_gather x1, waiting for transfers between devices: 6.98 us -> 0.02 us  [near_shards(): grads = lax.all_gather(cot_q, 'chan', axis=0)]
    optimization_barrier x1 -> x0, local copies, waits for them, and re-layouts: 6.41 us -> none  [tied(): return lax.optimization_barrier(values)]
    unnamed x69 -> x83, local copies, waits for them, and re-layouts: 11.8 us -> 6.15 us
    ppermute x21, starting transfers between devices: 36.9 us -> 33.4 us  [over_z(): lax.ppermute(values, 'chan', [(i, (i + 2 * hops) % 8) for i in range(8)])]
  transfers between devices with their start and end apart: 70 -> 70, of which waited for: 22 -> 20; matrix products, arithmetic and copies ran while one was open for 15% -> 13% of each run, Pallas kernels for 21% -> 22%
where the time goes in v3:
time: 337 us; the launch traced here: 336 us
  waiting for transfers between devices  101 us (30%)
  Pallas kernels  90.8 us (27%)
  starting transfers between devices  78.7 us (23%)
  other arithmetic  26 us (8%)
  local copies, waits for them, and re-layouts  17.6 us (5%)
  between operations  15 us (4%)
  matrix products  6.85 us (2%)
    ppermute x12, waiting for transfers between devices, over_y(): return lax.ppermute(values, 'chan', [(i, i ^ 1) for i in range(8)])  51.9 us
    ppermute x32, waiting for transfers between devices, over_state(): return lax.ppermute(values, 'state', [(i, i ^ bits) for i in range(4)])  38.9 us
    ppermute x21, starting transfers between devices, over_z(): lax.ppermute(values, 'chan', [(i, (i + 2 * hops) % 8) for i in range(8)])  33.4 us
    pallas_call x1, Pallas kernels, backward_scan(): pl.pallas_call(functools.partial(backward_body, parts), grid_spec=pltpu.P...  21.5 us
    ppermute x32, starting transfers between devices, over_state(): return lax.ppermute(values, 'state', [(i, i ^ bits) for i in range(4)])  17.8 us
    all_to_all x4, starting transfers between devices, swap_state(): return lax.all_to_all(values, 'state', 0, 0, tiled=True)  14.5 us
    pallas_call x1, Pallas kernels, forward_scan(): pl.pallas_call(functools.partial(forward_body, parts), grid_spec=pltpu.Pr...  14.1 us
    ppermute x12, starting transfers between devices, over_y(): return lax.ppermute(values, 'chan', [(i, i ^ 1) for i in range(8)])  13 us
  transfers between devices with their start and end apart: 70, of which 20 were waited for; matrix products, arithmetic and copies ran while one was open for 13% of the time, Pallas kernels for 22%

profile of v3, /device:TPU:0, one launch (start us, length us, event | category | flops | bytes accessed | tf_op | source)
XLA Modules:
  0.0 335.6 jit_solution(8888353792321733915)
XLA Ops:
  11.2 3.0 collective-permute-start
  20.3 3.8 %all-to-all-start = ((f32[4,4,128]{2,1,0:T(4,128)}), f32[4,4,128]{2,1,0:T(4,128)}, u32[]{:S(2)}, u32[]{:S(2)}) async-start(f32[4,4,128]{2,1,0:T(4,128)} %bitcast.2), calls=%async_computation | async-start | bytes 16384 | tf_op jit(solution)/shard_map/all_to_all | solution.py:1346
  27.8 5.4 %copy.53 = bf16[256,8,2,512]{3,1,2,0:T(8,128)(2,1)} copy(bf16[256,8,2,512]{3,2,1,0:T(2,128)(2,1)} %bitcast.166) | data formatting | bytes 8388608
  33.9 3.4 %collective-permute-done.2.refs_2_ = bf16[72,2048]{1,0:T(8,128)(2,1)S(1)} collective-permute-done((bf16[72,2048]{1,0:T(8,128)(2,1)S(1)}, bf16[72,2048]{1,0:T(8,128)(2,1)S(1)}, u32[]{:S(2)}, u32[]{:S(2)}) %collective-permute-start.2) | collective-permute-done | bytes 294944 | tf_op jit(solution)/shard_map/ppermute | solution.py:1340
  46.0 5.9 %collective-permute-done.6.refs_5_ = bf16[72,2048]{1,0:T(8,128)(2,1)S(1)} collective-permute-done((bf16[72,2048]{1,0:T(8,128)(2,1)S(1)}, bf16[72,2048]{1,0:T(8,128)(2,1)S(1)}, u32[]{:S(2)}, u32[]{:S(2)}) %collective-permute-start.6) | collective-permute-done | bytes 294944 | tf_op jit(solution)/shard_map/ppermute | solution.py:1337
  51.9 9.1 %collective-permute-done.7.refs_6_ = bf16[72,2048]{1,0:T(8,128)(2,1)S(1)} collective-permute-done((bf16[72,2048]{1,0:T(8,128)(2,1)S(1)}, bf16[72,2048]{1,0:T(8,128)(2,1)S(1)}, u32[]{:S(2)}, u32[]{:S(2)}) %collective-permute-start.7) | collective-permute-done | bytes 294944 | tf_op jit(solution)/shard_map/ppermute | solution.py:1337
  61.0 5.3 %collective-permute-done.8.refs_7_ = bf16[72,2048]{1,0:T(8,128)(2,1)S(1)} collective-permute-done((bf16[72,2048]{1,0:T(8,128)(2,1)}, bf16[72,2048]{1,0:T(8,128)(2,1)S(1)}, u32[]{:S(2)}, u32[]{:S(2)}) %collective-permute-start.8) | collective-permute-done | bytes 294944 | tf_op jit(solution)/shard_map/ppermute | solution.py:1337
  68.0 11.5 %project.1 = (bf16[512,2048]{1,0:T(8,128)(2,1)}, f32[8,80,512]{2,1,0:T(8,128)}, bf16[4,2,8,64,128]{4,3,2,1,0:T(8,128)(2,1)}, f32[4,64,160]{2,1,0:T(8,128)S(1)}, ...) custom-call(s32[20]{0:T(128)S(1)} %pad_add_fusion.1.place_ref, bf16[72,2048]{1,0:T(8,128)(2,1)} %copy-done.21, ...), custom_call_target="tpu_custom_call" | custom-call | bytes 28800000 | tf_op jit(solution)/shard_map/project/pallas_call | solution.py:957
  80.1 7.2 %collective-permute-done.10 = bf16[4,64,160]{2,1,0:T(8,128)(2,1)S(1)} collective-permute-done((bf16[4,64,160]{2,1,0:T(8,128)(2,1)S(1)}, bf16[4,64,160]{2,1,0:T(8,128)(2,1)S(1)}, u32[]{:S(2)}, u32[]{:S(2)}) %collective-permute-start.10) | collective-permute-done | bytes 81952 | tf_op jit(solution)/shard_map/ppermute | solution.py:1337
  87.3 4.2 %collective-permute-start.11 = (bf16[4,64,160]{2,1,0:T(8,128)(2,1)S(1)}, bf16[4,64,160]{2,1,0:T(8,128)(2,1)}, u32[]{:S(2)}, u32[]{:S(2)}) collective-permute-start(bf16[4,64,160]{2,1,0:T(8,128)(2,1)S(1)} %add_convert_fusion.8), channel_id=1, source_target_pairs={{0,8},{4,12},{8,16},{12,20},{16,24},{20,28},{24,0},{28,4},{1,9},{5... | collective-permute-start | bytes 245768 | tf_op jit(solution)/shard_map/ppermute | solution.py:1340
  94.0 3.5 %all-to-all-start.1 = ((bf16[4,2,8,64,128]{4,3,2,1,0:T(8,128)(2,1)}), bf16[4,2,8,64,128]{4,3,2,1,0:T(8,128)(2,1)S(1)}, u32[]{:S(2)}, u32[]{:S(2)}) async-start(bf16[4,2,8,64,128]{4,3,2,1,0:T(8,128)(2,1)} %get-tuple-element.181), calls=%async_computation.1 | async-start | bytes 2097152 | tf_op jit(solution)/shard_map/all_to_all | solution.py:1346
  97.6 5.7 %pull.1 = (bf16[512,2048]{1,0:T(8,128)(2,1)}, bf16[8,64,128]{2,1,0:T(8,128)(2,1)}, bf16[8,64,128]{2,1,0:T(8,128)(2,1)}, bf16[8,64,128]{2,1,0:T(8,128)(2,1)}, bf16[8,64,128]{2,1,0:T(8,128)(2,1)}) custom-call(s32[9]{0:T(128)S(1)} %add_convert_fusion.9.order_ref, bf16[8,64,2048]{2,1,0:T(8,128)(2,1)} %bitcast.167, bf16[512,2048]{1,0:T(8,128)(2,1)} %refs_1_.1), custom_call_target="tpu_custom_call" | custom-call | bytes 21600000 | tf_op jit(solution)/shard_map/pull/pallas_call | solution.py:1032
  105.1 5.3 %collective-permute-done.14 = bf16[4,64,160]{2,1,0:T(8,128)(2,1)S(1)} collective-permute-done((bf16[4,64,160]{2,1,0:T(8,128)(2,1)S(1)}, bf16[4,64,160]{2,1,0:T(8,128)(2,1)S(1)}, u32[]{:S(2)}, u32[]{:S(2)}) %collective-permute-start.14) | collective-permute-done | bytes 81952 | tf_op jit(solution)/shard_map/ppermute | solution.py:1337
  115.6 5.0 %collective-permute-done.16.refs_2_ = bf16[8,64,160]{2,1,0:T(8,128)(2,1)} collective-permute-done((bf16[8,64,160]{2,1,0:T(8,128)(2,1)}, bf16[8,64,160]{2,1,0:T(8,128)(2,1)}, u32[]{:S(2)}, u32[]{:S(2)}) %collective-permute-start.16) | collective-permute-done | bytes 163872 | tf_op jit(solution)/shard_map/ppermute | solution.py:1343
  124.9 14.1 %forward_scan.1 = (bf16[32768,128]{1,0:T(8,128)(2,1)}, f32[2048,128]{1,0:T(8,128)}, bf16[4,2,8,64,128]{4,3,2,1,0:T(8,128)(2,1)}) custom-call(s32[17]{0:T(128)S(1)} %add_convert_fusion.10.order_ref, bf16[8,64,160]{2,1,0:T(8,128)(2,1)} %pad_maximum_fusion.2.refs_0_, bf16[8,64,160]{2,1,0:T(8,128)(2,1)} %collective-permute-done.15.refs_1_, ...), custom_call_target="tpu_custom_call" | custom-call | bytes 43200000 | tf_op jit(solution)/shard_map/forward_scan/pallas_call | solution.py:695
  139.0 3.7 %all-to-all-start.2 = ((bf16[4,2,8,64,128]{4,3,2,1,0:T(8,128)(2,1)}), bf16[4,2,8,64,128]{4,3,2,1,0:T(8,128)(2,1)S(1)}, u32[]{:S(2)}, u32[]{:S(2)}) async-start(bf16[4,2,8,64,128]{4,3,2,1,0:T(8,128)(2,1)} %get-tuple-element.199), calls=%async_computation.2 | async-start | bytes 2097152 | tf_op jit(solution)/shard_map/all_to_all | solution.py:1346
  142.7 21.5 %backward_scan.1 = (bf16[2,8,80,160]{3,2,1,0:T(8,128)(2,1)}, bf16[2,8,80,160]{3,2,1,0:T(8,128)(2,1)}, bf16[4,8,80,128]{3,2,1,0:T(8,128)(2,1)}, f32[128,128]{1,0:...) custom-call(s32[17]{0:T(128)S(1)} %add_convert_fusion.10.order_ref, ...), custom_call_target="tpu_custom_call" | custom-call | bytes 68400000 | tf_op jit(solution)/shard_map/backward_scan/pallas_call | solution.py:744
  169.9 9.5 %emit.1 = (bf16[4,64,2048]{2,1,0:T(8,128)(2,1)}, bf16[4,64,2048]{2,1,0:T(8,128)(2,1)}, bf16[2,2,128,2048]{3,2,1,0:T(8,128)(2,1)}, bf16[2,2,128,2048]{3,2,1,0:T(8...) custom-call(s32[9]{0:T(128)S(1)} %add_convert_fusion.9.order_ref, bf16[4,2,8,64,128]{4,3,2,1,0:T(8,128)(2,1)} %copy-done.20, ...), custom_call_target="tpu_custom_call" | custom-call | bytes 21600000 | tf_op jit(solution)/shard_map/emit/pallas_call | solution.py:1105
  180.2 3.5 %all-to-all-start.3 = ((bf16[4,8,80,128]{3,2,1,0:T(8,128)(2,1)}), bf16[4,8,80,128]{3,2,1,0:T(8,128)(2,1)S(1)}, u32[]{:S(2)}, u32[]{:S(2)}) async-start(bf16[4,8,80,128]{3,2,1,0:T(8,128)(2,1)} %get-tuple-element.218), calls=%async_computation.3 | async-start | bytes 1310720 | tf_op jit(solution)/shard_map/all_to_all | solution.py:1346
  192.0 3.0 add_convert_fusion
  197.3 4.9 %collective-permute-done.26 = bf16[4,80,160]{2,1,0:T(8,128)(2,1)S(1)} collective-permute-done((bf16[4,80,160]{2,1,0:T(8,128)(2,1)S(1)}, bf16[4,80,160]{2,1,0:T(8,128)(2,1)S(1)}, u32[]{:S(2)}, u32[]{:S(2)}) %collective-permute-start.26) | collective-permute-done | bytes 102432 | tf_op jit(solution)/shard_map/ppermute | solution.py:1340
  202.2 13.5 %collective-permute-done.28 = bf16[4,64,2048]{2,1,0:T(8,128)(2,1)} collective-permute-done((bf16[4,64,2048]{2,1,0:T(8,128)(2,1)}, bf16[4,64,2048]{2,1,0:T(8,128)(2,1)}, u32[]{:S(2)}, u32[]{:S(2)}) %collective-permute-start.28) | collective-permute-done | bytes 1048608 | tf_op jit(solution)/shard_map/ppermute | solution.py:1337
  222.2 2.9 collective-permute-start.34
  226.7 5.9 %turn_back.1 = (bf16[512,1024]{1,0:T(8,128)(2,1)S(1)}, bf16[512,128]{1,0:T(8,128)(2,1)}, f32[40,512]{1,0:T(8,128)S(1)}) custom-call(s32[9]{0:T(128)S(1)} %add_convert_fusion.9.order_ref, bf16[4,80,160]{2,1,0:T(8,128)(2,1)S(1)} %add_convert_fusion.4.refs_0_, bf16[4,80,160]{2,1,0:T(8,128)(2,1)S(1)} %collective-permute-done.29.refs_1_, ...), custom_call_target="tpu_custom_call" | custom-call | bytes 19800000 | tf_op jit(solution)/shard_map/turn_back/pallas_call | solution.py:1275
  232.6 5.7 %weigh.1 = (bf16[2,128,2048]{2,1,0:T(8,128)(2,1)}, bf16[2,128,2048]{2,1,0:T(8,128)(2,1)}, f32[1,2048]{1,0:T(1,128)S(1)}) custom-call(s32[9]{0:T(128)S(1)} %add_convert_fusion.9.order_ref, bf16[512,1024]{1,0:T(8,128)(2,1)S(1)} %get-tuple-element.245.rows_ref, bf16[512,2048]{1,0:T(8,128)(2,1)} %get-tuple-element.209.refs_3_.normed_ref, ...), custom_call_target="tpu_custom_call" | custom-call | bytes 14400000 | tf_op jit(solution)/shard_map/weigh/pallas_call | solution.py:1161
  242.2 2.9 convolution_convert_fusion
  255.2 8.8 %collective-permute-done.38.refs_2_.refs_6_ = bf16[2,128,2048]{2,1,0:T(8,128)(2,1)S(1)} collective-permute-done((bf16[2,128,2048]{2,1,0:T(8,128)(2,1)S(1)}, bf16[2,128,2048]{2,1,0:T(8,128)(2,1)S(1)}, u32[]{:S(2)}, u32[]{:S(2)}) %collective-permute-start.38) | collective-permute-done | bytes 1048608 | tf_op jit(solution)/shard_map/ppermute | solution.py:1343
  270.7 7.9 %collective-permute-done.45 = bf16[128,2048]{1,0:T(8,128)(2,1)S(1)} collective-permute-done((bf16[128,2048]{1,0:T(8,128)(2,1)S(1)}, bf16[128,2048]{1,0:T(8,128)(2,1)S(1)}, u32[]{:S(2)}, u32[]{:S(2)}) %collective-permute-start.45) | collective-permute-done | bytes 524320 | tf_op jit(solution)/shard_map/ppermute | solution.py:1343
  280.1 2.9 collective-permute-done.43
  289.5 3.0 placed.3
  293.2 10.9 %collective-permute-done.50.refs_2_ = bf16[64,2048]{1,0:T(8,128)(2,1)S(1)} collective-permute-done((bf16[64,2048]{1,0:T(8,128)(2,1)S(1)}, bf16[64,2048]{1,0:T(8,128)(2,1)S(1)}, u32[]{:S(2)}, u32[]{:S(2)}) %collective-permute-start.50) | collective-permute-done | bytes 262176 | tf_op jit(solution)/shard_map/ppermute | solution.py:1343
  306.4 9.0 %interleave.1 = f32[2048,2,512]{2,1,0:T(2,128)} custom-call(s32[4]{0:T(128)S(1)} %xor_convert_fusion.order_ref, bf16[128,2048]{1,0:T(8,128)(2,1)S(1)} %fusion.6.refs_0_, bf16[128,2048]{1,0:T(8,128)(2,1)S(1)} %collective-permute-done.54.refs_1_, bf16[128,2048]{1,0:T(8,128)(2,1)S(1)} %collective-permute-done.53.refs_2_, ...), custom_call_target="tpu_custom_call" | custom-call | bytes 18000000 | tf_op jit(solution)/shard_map/interleave/pallas_call | solution.py:806
  (311 shorter events, 108.8 us)
Async XLA Ops:
  11.2 22.7 %collective-permute-start = (bf16[72,2048]{1,0:T(8,128)(2,1)S(1)}, bf16[72,2048]{1,0:T(8,128)(2,1)S(1)}, u32[]{:S(2)}, u32[]{:S(2)}) collective-permute-start(bf16[72,2048]{1,0:T(8,128)(2,1)S(1)} %get-tuple-element.296.refs_0_), channel_id=1, source_target_pairs={{0,4},{4,0},{8,12},{12,8},{16,20},{20,16},{24,28},{28,24},{1,5},{5... | collective-permute-start | bytes 884744 | tf_op jit(solution)/shard_map/ppermute | solution.py:1337
  14.2 19.7 %collective-permute-start.1 = (bf16[72,2048]{1,0:T(8,128)(2,1)S(1)}, bf16[72,2048]{1,0:T(8,128)(2,1)S(1)}, u32[]{:S(2)}, u32[]{:S(2)}) collective-permute-start(bf16[72,2048]{1,0:T(8,128)(2,1)S(1)} %get-tuple-element.296.refs_0_), channel_id=1, source_target_pairs={{0,8},{4,12},{8,16},{12,20},{16,24},{20,28},{24,0},{28,4},{1,9},{5... | collective-permute-start | bytes 884744 | tf_op jit(solution)/shard_map/ppermute | solution.py:1340
  15.8 21.5 %collective-permute-start.2 = (bf16[72,2048]{1,0:T(8,128)(2,1)S(1)}, bf16[72,2048]{1,0:T(8,128)(2,1)S(1)}, u32[]{:S(2)}, u32[]{:S(2)}) collective-permute-start(bf16[72,2048]{1,0:T(8,128)(2,1)S(1)} %get-tuple-element.296.refs_0_), channel_id=1, source_target_pairs={{0,16},{4,20},{8,24},{12,28},{16,0},{20,4},{24,8},{28,12},{1,17},{... | collective-permute-start | bytes 884744 | tf_op jit(solution)/shard_map/ppermute | solution.py:1340
  18.4 18.9 %collective-permute-start.3 = (bf16[72,2048]{1,0:T(8,128)(2,1)S(1)}, bf16[72,2048]{1,0:T(8,128)(2,1)}, u32[]{:S(2)}, u32[]{:S(2)}) collective-permute-start(bf16[72,2048]{1,0:T(8,128)(2,1)S(1)} %get-tuple-element.296.refs_0_), channel_id=1, source_target_pairs={{0,24},{4,28},{8,0},{12,4},{16,8},{20,12},{24,16},{28,20},{1,25},{... | collective-permute-start | bytes 884744 | tf_op jit(solution)/shard_map/ppermute | solution.py:1340
  20.3 13.6 %all-to-all-start = ((f32[4,4,128]{2,1,0:T(4,128)}), f32[4,4,128]{2,1,0:T(4,128)}, u32[]{:S(2)}, u32[]{:S(2)}) async-start(f32[4,4,128]{2,1,0:T(4,128)} %bitcast.2), calls=%async_computation | async-start | bytes 16384 | tf_op jit(solution)/shard_map/all_to_all | solution.py:1346
  24.1 73.5 %all-gather.3.cloned.1.call-start = ((), (), s32[]{:S(2)}) async-start(), calls=%async_computation.4 | async-start | bytes 2359296 | tf_op jit(solution)/shard_map/all_gather | solution.py:1476
  42.5 18.5 %collective-permute-start.7 = (bf16[72,2048]{1,0:T(8,128)(2,1)S(1)}, bf16[72,2048]{1,0:T(8,128)(2,1)S(1)}, u32[]{:S(2)}, u32[]{:S(2)}) collective-permute-start(bf16[72,2048]{1,0:T(8,128)(2,1)S(1)} %collective-permute-done.2.refs_2_), channel_id=1, source_target_pairs={{0,4},{4,0},{8,12},{12,8},{16,20},{20,16},{24,28},{28,24},{1,5},{5... | collective-permute-start | bytes 884744 | tf_op jit(solution)/shard_map/ppermute | solution.py:1337
  44.0 22.3 %collective-permute-start.8 = (bf16[72,2048]{1,0:T(8,128)(2,1)}, bf16[72,2048]{1,0:T(8,128)(2,1)S(1)}, u32[]{:S(2)}, u32[]{:S(2)}) collective-permute-start(bf16[72,2048]{1,0:T(8,128)(2,1)} %collective-permute-done.3.refs_3_), channel_id=1, source_target_pairs={{0,4},{4,0},{8,12},{12,8},{16,20},{20,16},{24,28},{28,24},{1,5},{5... | collective-permute-start | bytes 884744 | tf_op jit(solution)/shard_map/ppermute | solution.py:1337
  87.3 16.0 %collective-permute-start.11 = (bf16[4,64,160]{2,1,0:T(8,128)(2,1)S(1)}, bf16[4,64,160]{2,1,0:T(8,128)(2,1)}, u32[]{:S(2)}, u32[]{:S(2)}) collective-permute-start(bf16[4,64,160]{2,1,0:T(8,128)(2,1)S(1)} %add_convert_fusion.8), channel_id=1, source_target_pairs={{0,8},{4,12},{8,16},{12,20},{16,24},{20,28},{24,0},{28,4},{1,9},{5... | collective-permute-start | bytes 245768 | tf_op jit(solution)/shard_map/ppermute | solution.py:1340
  94.0 26.6 %all-to-all-start.1 = ((bf16[4,2,8,64,128]{4,3,2,1,0:T(8,128)(2,1)}), bf16[4,2,8,64,128]{4,3,2,1,0:T(8,128)(2,1)S(1)}, u32[]{:S(2)}, u32[]{:S(2)}) async-start(bf16[4,2,8,64,128]{4,3,2,1,0:T(8,128)(2,1)} %get-tuple-element.181), calls=%async_computation.1 | async-start | bytes 2097152 | tf_op jit(solution)/shard_map/all_to_all | solution.py:1346
  139.0 25.3 %all-to-all-start.2 = ((bf16[4,2,8,64,128]{4,3,2,1,0:T(8,128)(2,1)}), bf16[4,2,8,64,128]{4,3,2,1,0:T(8,128)(2,1)S(1)}, u32[]{:S(2)}, u32[]{:S(2)}) async-start(bf16[4,2,8,64,128]{4,3,2,1,0:T(8,128)(2,1)} %get-tuple-element.199), calls=%async_computation.2 | async-start | bytes 2097152 | tf_op jit(solution)/shard_map/all_to_all | solution.py:1346
  180.2 17.0 %all-to-all-start.3 = ((bf16[4,8,80,128]{3,2,1,0:T(8,128)(2,1)}), bf16[4,8,80,128]{3,2,1,0:T(8,128)(2,1)S(1)}, u32[]{:S(2)}, u32[]{:S(2)}) async-start(bf16[4,8,80,128]{3,2,1,0:T(8,128)(2,1)} %get-tuple-element.218), calls=%async_computation.3 | async-start | bytes 1310720 | tf_op jit(solution)/shard_map/all_to_all | solution.py:1346
  188.1 14.1 %collective-permute-start.26 = (bf16[4,80,160]{2,1,0:T(8,128)(2,1)S(1)}, bf16[4,80,160]{2,1,0:T(8,128)(2,1)S(1)}, u32[]{:S(2)}, u32[]{:S(2)}) collective-permute-start(bf16[4,80,160]{2,1,0:T(8,128)(2,1)S(1)} %add_convert_fusion.5), channel_id=1, source_target_pairs={{0,16},{4,20},{8,24},{12,28},{16,0},{20,4},{24,8},{28,12},{1,17},{... | collective-permute-start | bytes 307208 | tf_op jit(solution)/shard_map/ppermute | solution.py:1340
  191.4 24.3 %collective-permute-start.28 = (bf16[4,64,2048]{2,1,0:T(8,128)(2,1)}, bf16[4,64,2048]{2,1,0:T(8,128)(2,1)}, u32[]{:S(2)}, u32[]{:S(2)}) collective-permute-start(bf16[4,64,2048]{2,1,0:T(8,128)(2,1)} %get-tuple-element.217), channel_id=1, source_target_pairs={{0,4},{4,0},{8,12},{12,8},{16,20},{20,16},{24,28},{28,24},{1,5},{5... | collective-permute-start | bytes 3145736 | tf_op jit(solution)/shard_map/ppermute | solution.py:1337
  196.7 28.3 %collective-permute-start.30 = (bf16[2,128,2048]{2,1,0:T(8,128)(2,1)}, bf16[2,128,2048]{2,1,0:T(8,128)(2,1)}, u32[]{:S(2)}, u32[]{:S(2)}) collective-permute-start(bf16[2,128,2048]{2,1,0:T(8,128)(2,1)} %slice_bitcast_fusion.1), channel_id=1, source_target_pairs={{0,2},{1,3},{2,0},{3,1},{4,6},{5,7},{6,4},{7,5},{8,10},{9,11},{10,... | collective-permute-start | bytes 3145736 | tf_op jit(solution)/shard_map/ppermute | solution.py:1343
  220.3 24.9 %collective-permute-start.32 = (bf16[64,2048]{1,0:T(8,128)(2,1)}, bf16[64,2048]{1,0:T(8,128)(2,1)}, u32[]{:S(2)}, u32[]{:S(2)}) collective-permute-start(bf16[64,2048]{1,0:T(8,128)(2,1)} %get-tuple-element.302), channel_id=1, source_target_pairs={{0,8},{4,12},{8,16},{12,20},{16,24},{20,28},{24,0},{28,4},{1,9},{5... | collective-permute-start | bytes 786440 | tf_op jit(solution)/shard_map/ppermute | solution.py:1340
  220.9 24.3 %collective-permute-start.33 = (bf16[64,2048]{1,0:T(8,128)(2,1)}, bf16[64,2048]{1,0:T(8,128)(2,1)}, u32[]{:S(2)}, u32[]{:S(2)}) collective-permute-start(bf16[64,2048]{1,0:T(8,128)(2,1)} %get-tuple-element.301), channel_id=1, source_target_pairs={{0,16},{4,20},{8,24},{12,28},{16,0},{20,4},{24,8},{28,12},{1,17},{... | collective-permute-start | bytes 786440 | tf_op jit(solution)/shard_map/ppermute | solution.py:1340
  222.2 23.1 %collective-permute-start.34 = (bf16[64,2048]{1,0:T(8,128)(2,1)}, bf16[64,2048]{1,0:T(8,128)(2,1)}, u32[]{:S(2)}, u32[]{:S(2)}) collective-permute-start(bf16[64,2048]{1,0:T(8,128)(2,1)} %get-tuple-element.300), channel_id=1, source_target_pairs={{0,24},{4,28},{8,0},{12,4},{16,8},{20,12},{24,16},{28,20},{1,25},{... | collective-permute-start | bytes 786440 | tf_op jit(solution)/shard_map/ppermute | solution.py:1340
  238.5 25.6 %collective-permute-start.38 = (bf16[2,128,2048]{2,1,0:T(8,128)(2,1)S(1)}, bf16[2,128,2048]{2,1,0:T(8,128)(2,1)S(1)}, u32[]{:S(2)}, u32[]{:S(2)}) collective-permute-start(bf16[2,128,2048]{2,1,0:T(8,128)(2,1)S(1)} %fusion.3.refs_0_.refs_4_), channel_id=1, source_target_pairs={{0,2},{1,3},{2,0},{3,1},{4,6},{5,7},{6,4},{7,5},{8,10},{9,11},{10,... | collective-permute-start | bytes 3145736 | tf_op jit(solution)/shard_map/ppermute | solution.py:1343
  245.5 19.5 %collective-permute-start.35 = (bf16[4,64,1408]{2,1,0:T(8,128)(2,1)S(1)}, bf16[4,64,1408]{2,1,0:T(8,128)(2,1)S(1)}, u32[]{:S(2)}, u32[]{:S(2)}) collective-permute-start(bf16[4,64,1408]{2,1,0:T(8,128)(2,1)S(1)} %bitcast.190), channel_id=1, source_target_pairs={{0,4},{4,0},{8,12},{12,8},{16,20},{20,16},{24,28},{28,24},{1,5},{5... | collective-permute-start | bytes 2162696 | tf_op jit(solution)/shard_map/ppermute | solution.py:1337
  246.9 18.0 %collective-permute-start.39 = (bf16[2,64,640]{2,1,0:T(8,128)(2,1)S(1)}, bf16[2,64,640]{2,1,0:T(8,128)(2,1)S(1)}, u32[]{:S(2)}, u32[]{:S(2)}) collective-permute-start(bf16[2,64,640]{2,1,0:T(8,128)(2,1)S(1)} %get-tuple-element.251), channel_id=1, source_target_pairs={{0,16},{4,20},{8,24},{12,28},{16,0},{20,4},{24,8},{28,12},{1,17},{... | collective-permute-start | bytes 491528 | tf_op jit(solution)/shard_map/ppermute | solution.py:1340
  248.1 16.9 %collective-permute-start.40 = (bf16[2,64,640]{2,1,0:T(8,128)(2,1)S(1)}, bf16[2,64,640]{2,1,0:T(8,128)(2,1)S(1)}, u32[]{:S(2)}, u32[]{:S(2)}) collective-permute-start(bf16[2,64,640]{2,1,0:T(8,128)(2,1)S(1)} %get-tuple-element.252), channel_id=1, source_target_pairs={{0,24},{4,28},{8,0},{12,4},{16,8},{20,12},{24,16},{28,20},{1,25},{... | collective-permute-start | bytes 491528 | tf_op jit(solution)/shard_map/ppermute | solution.py:1340
  264.0 14.5 %collective-permute-start.45 = (bf16[128,2048]{1,0:T(8,128)(2,1)S(1)}, bf16[128,2048]{1,0:T(8,128)(2,1)S(1)}, u32[]{:S(2)}, u32[]{:S(2)}) collective-permute-start(bf16[128,2048]{1,0:T(8,128)(2,1)S(1)} %slice_bitcast_fusion.3), channel_id=1, source_target_pairs={{0,2},{1,3},{2,0},{3,1},{4,6},{5,7},{6,4},{7,5},{8,10},{9,11},{10,... | collective-permute-start | bytes 1572872 | tf_op jit(solution)/shard_map/ppermute | solution.py:1343
  265.2 18.4 %collective-permute-start.47 = (bf16[64,1408]{1,0:T(8,128)(2,1)S(1)}, bf16[64,1408]{1,0:T(8,128)(2,1)S(1)}, u32[]{:S(2)}, u32[]{:S(2)}) collective-permute-start(bf16[64,1408]{1,0:T(8,128)(2,1)S(1)} %get-tuple-element.305), channel_id=1, source_target_pairs={{0,8},{4,12},{8,16},{12,20},{16,24},{20,28},{24,0},{28,4},{1,9},{5... | collective-permute-start | bytes 540680 | tf_op jit(solution)/shard_map/ppermute | solution.py:1340
  265.3 18.3 %collective-permute-start.48 = (bf16[64,1408]{1,0:T(8,128)(2,1)S(1)}, bf16[64,1408]{1,0:T(8,128)(2,1)S(1)}, u32[]{:S(2)}, u32[]{:S(2)}) collective-permute-start(bf16[64,1408]{1,0:T(8,128)(2,1)S(1)} %get-tuple-element.304), channel_id=1, source_target_pairs={{0,16},{4,20},{8,24},{12,28},{16,0},{20,4},{24,8},{28,12},{1,17},{... | collective-permute-start | bytes 540680 | tf_op jit(solution)/shard_map/ppermute | solution.py:1340
  267.9 15.7 %collective-permute-start.49 = (bf16[64,1408]{1,0:T(8,128)(2,1)S(1)}, bf16[64,1408]{1,0:T(8,128)(2,1)S(1)}, u32[]{:S(2)}, u32[]{:S(2)}) collective-permute-start(bf16[64,1408]{1,0:T(8,128)(2,1)S(1)} %get-tuple-element.303), channel_id=1, source_target_pairs={{0,24},{4,28},{8,0},{12,4},{16,8},{20,12},{24,16},{28,20},{1,25},{... | collective-permute-start | bytes 540680 | tf_op jit(solution)/shard_map/ppermute | solution.py:1340
  269.5 13.6 %collective-permute-start.44 = (f32[44,512]{1,0:T(8,128)S(1)}, f32[44,512]{1,0:T(8,128)S(1)}, u32[]{:S(2)}, u32[]{:S(2)}) collective-permute-start(f32[44,512]{1,0:T(8,128)S(1)} %add.256), channel_id=1, source_target_pairs={{0,2},{1,3},{2,0},{3,1},{4,6},{5,7},{6,4},{7,5},{8,10},{9,11},{10,... | collective-permute-start | bytes 270344 | tf_op jit(solution)/shard_map/ppermute | solution.py:1343
  283.7 20.5 %collective-permute-start.53 = (bf16[128,2048]{1,0:T(8,128)(2,1)S(1)}, bf16[128,2048]{1,0:T(8,128)(2,1)S(1)}, u32[]{:S(2)}, u32[]{:S(2)}) collective-permute-start(bf16[128,2048]{1,0:T(8,128)(2,1)S(1)} %fusion.6.refs_0_), channel_id=1, source_target_pairs={{0,2},{1,3},{2,0},{3,1},{4,6},{5,7},{6,4},{7,5},{8,10},{9,11},{10,... | collective-permute-start | bytes 1572872 | tf_op jit(solution)/shard_map/ppermute | solution.py:1343
  284.6 19.6 %collective-permute-start.54 = (bf16[128,2048]{1,0:T(8,128)(2,1)S(1)}, bf16[128,2048]{1,0:T(8,128)(2,1)S(1)}, u32[]{:S(2)}, u32[]{:S(2)}) collective-permute-start(bf16[128,2048]{1,0:T(8,128)(2,1)S(1)} %fusion.6.refs_0_), channel_id=1, source_target_pairs={{0,1},{1,0},{2,3},{3,2},{4,5},{5,4},{6,7},{7,6},{8,9},{9,8},{10,11... | collective-permute-start | bytes 1572872 | tf_op jit(solution)/shard_map/ppermute | solution.py:1343
  285.1 19.0 %collective-permute-start.50 = (bf16[64,2048]{1,0:T(8,128)(2,1)S(1)}, bf16[64,2048]{1,0:T(8,128)(2,1)S(1)}, u32[]{:S(2)}, u32[]{:S(2)}) collective-permute-start(bf16[64,2048]{1,0:T(8,128)(2,1)S(1)} %multiply_convert_fusion.1.refs_0_), channel_id=1, source_target_pairs={{0,2},{1,3},{2,0},{3,1},{4,6},{5,7},{6,4},{7,5},{8,10},{9,11},{10,... | collective-permute-start | bytes 786440 | tf_op jit(solution)/shard_map/ppermute | solution.py:1343
  286.4 17.8 %collective-permute-start.51 = (bf16[64,2048]{1,0:T(8,128)(2,1)S(1)}, bf16[64,2048]{1,0:T(8,128)(2,1)S(1)}, u32[]{:S(2)}, u32[]{:S(2)}) collective-permute-start(bf16[64,2048]{1,0:T(8,128)(2,1)S(1)} %multiply_convert_fusion.1.refs_0_), channel_id=1, source_target_pairs={{0,1},{1,0},{2,3},{3,2},{4,5},{5,4},{6,7},{7,6},{8,9},{9,8},{10,11... | collective-permute-start | bytes 786440 | tf_op jit(solution)/shard_map/ppermute | solution.py:1343
  292.5 22.9 %collective-permute-start.41 = (bf16[64,2048]{1,0:T(8,128)(2,1)S(1)}, bf16[64,2048]{1,0:T(8,128)(2,1)S(1)}, u32[]{:S(2)}, u32[]{:S(2)}) collective-permute-start(bf16[64,2048]{1,0:T(8,128)(2,1)S(1)} %fusion.10.refs_0_), channel_id=1, source_target_pairs={{0,2},{1,3},{2,0},{3,1},{4,6},{5,7},{6,4},{7,5},{8,10},{9,11},{10,... | collective-permute-start | bytes 786440 | tf_op jit(solution)/shard_map/ppermute | solution.py:1343
  (77 other events, 728.3 us)
Sparse Core Ops, SparseCore 0:
  37.5 59.8 all-gather.2

commit v4 on v3

--- a/solution.py
+++ b/solution.py
@@ -1606,7 +1606,7 @@
     def backed(rows, weight):
         return lax.dot_general(rows, weight, contract_cols, preferred_element_type=wide)
 
-    edge = width * 11 // 16
+    edge = width * 5 // 8
     left, right = slice(0, edge), slice(edge, width)
     other, same = slice(rows_q // 2, rows_q), slice(0, rows_q // 2)
     left_sent = backed(dboth[other], in_flat[left]).astype(low).reshape(4, quarter, edge)
@@ -1623,7 +1623,8 @@
 
     left_came = moves.over_y(left_sent)
     right_along = [moves.over_z(right_sent[hops - 1], hops) for hops in (1, 2, 3)]
-    gain_came = moves.over_state(gain, 1)
+    gain = gain + moves.over_state(gain, 1)
+    gain_came = moves.over_state(gain, 2)
     left_kept = backed(after(dboth, right_along[0])[same], in_flat[left])
     left_kept = left_kept.reshape(4, quarter, edge)
     branch = total_of(branch[0], branches)
@@ -1640,12 +1641,10 @@
     right_came = moves.over_y(right_sum[1].astype(low))
     inner_sum = added(inner_kept, inner_came)
     inner_came = moves.over_state(inner_sum[1], 2)
-    gain = gain + gain_came
-    gain_came = moves.over_state(gain, 2)
     small_core = moves.over_state(small, 1)
-    tie = tied(right_came, gain, gain_came, inner_came, small_core, *left_along)
-    right_came, gain, gain_came, inner_came, small_core = tie[:5]
-    left_along = tie[5:]
+    tie = tied(right_came, inner_came, small_core, *left_along)
+    right_came, inner_came, small_core = tie[:3]
+    left_along = tie[3:]
 
     for piece in left_along:
         left_sum = left_sum + piece.astype(wide)

time: 337 us -> 337 us (level)
    ppermute x21, waiting for transfers between devices: 9.79 us -> 14 us  [over_z(): lax.ppermute(values, 'chan', [(i, (i + 2 * hops) % 8) for i in range(8)])]
  transfers between devices with their start and end apart: 70 -> 70, of which waited for: 20 -> 21; matrix products, arithmetic and copies ran while one was open for 13% -> 12% of each run, Pallas kernels for 22% -> 22%
where the time goes in v4:
time: 337 us; the launch traced here: 335 us
  waiting for transfers between devices  99.4 us (29%)
  Pallas kernels  90.8 us (27%)
  starting transfers between devices  81.3 us (24%)
  other arithmetic  25.8 us (8%)
  local copies, waits for them, and re-layouts  18.1 us (5%)
  between operations  15 us (4%)
  matrix products  5.02 us (1%)
    ppermute x12, waiting for transfers between devices, over_y(): return lax.ppermute(values, 'chan', [(i, i ^ 1) for i in range(8)])  49 us
    ppermute x32, waiting for transfers between devices, over_state(): return lax.ppermute(values, 'state', [(i, i ^ bits) for i in range(4)])  36.4 us
    ppermute x21, starting transfers between devices, over_z(): lax.ppermute(values, 'chan', [(i, (i + 2 * hops) % 8) for i in range(8)])  35.2 us
    pallas_call x1, Pallas kernels, backward_scan(): pl.pallas_call(functools.partial(backward_body, parts), grid_spec=pltpu.P...  21.5 us
    ppermute x32, starting transfers between devices, over_state(): return lax.ppermute(values, 'state', [(i, i ^ bits) for i in range(4)])  18.7 us
    all_to_all x4, starting transfers between devices, swap_state(): return lax.all_to_all(values, 'state', 0, 0, tiled=True)  14.5 us
    pallas_call x1, Pallas kernels, forward_scan(): pl.pallas_call(functools.partial(forward_body, parts), grid_spec=pltpu.Pr...  14.1 us
    ppermute x21, waiting for transfers between devices, over_z(): lax.ppermute(values, 'chan', [(i, (i + 2 * hops) % 8) for i in range(8)])  14 us
  transfers between devices with their start and end apart: 70, of which 21 were waited for; matrix products, arithmetic and copies ran while one was open for 12% of the time, Pallas kernels for 22%

profile of v4, /device:TPU:0, one launch (start us, length us, event | category | flops | bytes accessed | tf_op | source)
XLA Modules:
  0.0 335.5 jit_solution(14123163324817275851)
XLA Ops:
  11.2 3.0 collective-permute-start
  20.3 3.8 %all-to-all-start = ((f32[4,4,128]{2,1,0:T(4,128)}), f32[4,4,128]{2,1,0:T(4,128)}, u32[]{:S(2)}, u32[]{:S(2)}) async-start(f32[4,4,128]{2,1,0:T(4,128)} %bitcast.2), calls=%async_computation | async-start | bytes 16384 | tf_op jit(solution)/shard_map/all_to_all | solution.py:1346
  27.8 5.4 %copy.53 = bf16[256,8,2,512]{3,1,2,0:T(8,128)(2,1)} copy(bf16[256,8,2,512]{3,2,1,0:T(2,128)(2,1)} %bitcast.166) | data formatting | bytes 8388608
  33.9 3.4 %collective-permute-done.2.refs_2_ = bf16[72,2048]{1,0:T(8,128)(2,1)S(1)} collective-permute-done((bf16[72,2048]{1,0:T(8,128)(2,1)S(1)}, bf16[72,2048]{1,0:T(8,128)(2,1)S(1)}, u32[]{:S(2)}, u32[]{:S(2)}) %collective-permute-start.2) | collective-permute-done | bytes 294944 | tf_op jit(solution)/shard_map/ppermute | solution.py:1340
  46.0 5.9 %collective-permute-done.6.refs_5_ = bf16[72,2048]{1,0:T(8,128)(2,1)S(1)} collective-permute-done((bf16[72,2048]{1,0:T(8,128)(2,1)S(1)}, bf16[72,2048]{1,0:T(8,128)(2,1)S(1)}, u32[]{:S(2)}, u32[]{:S(2)}) %collective-permute-start.6) | collective-permute-done | bytes 294944 | tf_op jit(solution)/shard_map/ppermute | solution.py:1337
  51.9 9.1 %collective-permute-done.7.refs_6_ = bf16[72,2048]{1,0:T(8,128)(2,1)S(1)} collective-permute-done((bf16[72,2048]{1,0:T(8,128)(2,1)S(1)}, bf16[72,2048]{1,0:T(8,128)(2,1)S(1)}, u32[]{:S(2)}, u32[]{:S(2)}) %collective-permute-start.7) | collective-permute-done | bytes 294944 | tf_op jit(solution)/shard_map/ppermute | solution.py:1337
  61.0 5.3 %collective-permute-done.8.refs_7_ = bf16[72,2048]{1,0:T(8,128)(2,1)S(1)} collective-permute-done((bf16[72,2048]{1,0:T(8,128)(2,1)}, bf16[72,2048]{1,0:T(8,128)(2,1)S(1)}, u32[]{:S(2)}, u32[]{:S(2)}) %collective-permute-start.8) | collective-permute-done | bytes 294944 | tf_op jit(solution)/shard_map/ppermute | solution.py:1337
  68.0 11.5 %project.1 = (bf16[512,2048]{1,0:T(8,128)(2,1)}, f32[8,80,512]{2,1,0:T(8,128)}, bf16[4,2,8,64,128]{4,3,2,1,0:T(8,128)(2,1)}, f32[4,64,160]{2,1,0:T(8,128)S(1)}, ...) custom-call(s32[20]{0:T(128)S(1)} %pad_add_fusion.1.place_ref, bf16[72,2048]{1,0:T(8,128)(2,1)} %copy-done.21, ...), custom_call_target="tpu_custom_call" | custom-call | bytes 28800000 | tf_op jit(solution)/shard_map/project/pallas_call | solution.py:957
  80.1 7.2 %collective-permute-done.10 = bf16[4,64,160]{2,1,0:T(8,128)(2,1)S(1)} collective-permute-done((bf16[4,64,160]{2,1,0:T(8,128)(2,1)S(1)}, bf16[4,64,160]{2,1,0:T(8,128)(2,1)S(1)}, u32[]{:S(2)}, u32[]{:S(2)}) %collective-permute-start.10) | collective-permute-done | bytes 81952 | tf_op jit(solution)/shard_map/ppermute | solution.py:1337
  87.3 4.2 %collective-permute-start.11 = (bf16[4,64,160]{2,1,0:T(8,128)(2,1)S(1)}, bf16[4,64,160]{2,1,0:T(8,128)(2,1)}, u32[]{:S(2)}, u32[]{:S(2)}) collective-permute-start(bf16[4,64,160]{2,1,0:T(8,128)(2,1)S(1)} %add_convert_fusion.8), channel_id=1, source_target_pairs={{0,8},{4,12},{8,16},{12,20},{16,24},{20,28},{24,0},{28,4},{1,9},{5... | collective-permute-start | bytes 245768 | tf_op jit(solution)/shard_map/ppermute | solution.py:1340
  94.0 3.5 %all-to-all-start.1 = ((bf16[4,2,8,64,128]{4,3,2,1,0:T(8,128)(2,1)}), bf16[4,2,8,64,128]{4,3,2,1,0:T(8,128)(2,1)S(1)}, u32[]{:S(2)}, u32[]{:S(2)}) async-start(bf16[4,2,8,64,128]{4,3,2,1,0:T(8,128)(2,1)} %get-tuple-element.179), calls=%async_computation.1 | async-start | bytes 2097152 | tf_op jit(solution)/shard_map/all_to_all | solution.py:1346
  97.6 5.7 %pull.1 = (bf16[512,2048]{1,0:T(8,128)(2,1)}, bf16[8,64,128]{2,1,0:T(8,128)(2,1)}, bf16[8,64,128]{2,1,0:T(8,128)(2,1)}, bf16[8,64,128]{2,1,0:T(8,128)(2,1)}, bf16[8,64,128]{2,1,0:T(8,128)(2,1)}) custom-call(s32[9]{0:T(128)S(1)} %add_convert_fusion.9.order_ref, bf16[8,64,2048]{2,1,0:T(8,128)(2,1)} %bitcast.167, bf16[512,2048]{1,0:T(8,128)(2,1)} %refs_1_.1), custom_call_target="tpu_custom_call" | custom-call | bytes 21600000 | tf_op jit(solution)/shard_map/pull/pallas_call | solution.py:1032
  105.1 5.3 %collective-permute-done.14 = bf16[4,64,160]{2,1,0:T(8,128)(2,1)S(1)} collective-permute-done((bf16[4,64,160]{2,1,0:T(8,128)(2,1)S(1)}, bf16[4,64,160]{2,1,0:T(8,128)(2,1)S(1)}, u32[]{:S(2)}, u32[]{:S(2)}) %collective-permute-start.14) | collective-permute-done | bytes 81952 | tf_op jit(solution)/shard_map/ppermute | solution.py:1337
  115.6 5.0 %collective-permute-done.16.refs_2_ = bf16[8,64,160]{2,1,0:T(8,128)(2,1)} collective-permute-done((bf16[8,64,160]{2,1,0:T(8,128)(2,1)}, bf16[8,64,160]{2,1,0:T(8,128)(2,1)}, u32[]{:S(2)}, u32[]{:S(2)}) %collective-permute-start.16) | collective-permute-done | bytes 163872 | tf_op jit(solution)/shard_map/ppermute | solution.py:1343
  124.9 14.1 %forward_scan.1 = (bf16[32768,128]{1,0:T(8,128)(2,1)}, f32[2048,128]{1,0:T(8,128)}, bf16[4,2,8,64,128]{4,3,2,1,0:T(8,128)(2,1)}) custom-call(s32[17]{0:T(128)S(1)} %add_convert_fusion.10.order_ref, bf16[8,64,160]{2,1,0:T(8,128)(2,1)} %pad_maximum_fusion.2.refs_0_, bf16[8,64,160]{2,1,0:T(8,128)(2,1)} %collective-permute-done.15.refs_1_, ...), custom_call_target="tpu_custom_call" | custom-call | bytes 43200000 | tf_op jit(solution)/shard_map/forward_scan/pallas_call | solution.py:695
  139.0 3.7 %all-to-all-start.2 = ((bf16[4,2,8,64,128]{4,3,2,1,0:T(8,128)(2,1)}), bf16[4,2,8,64,128]{4,3,2,1,0:T(8,128)(2,1)S(1)}, u32[]{:S(2)}, u32[]{:S(2)}) async-start(bf16[4,2,8,64,128]{4,3,2,1,0:T(8,128)(2,1)} %get-tuple-element.197), calls=%async_computation.2 | async-start | bytes 2097152 | tf_op jit(solution)/shard_map/all_to_all | solution.py:1346
  142.7 21.5 %backward_scan.1 = (bf16[2,8,80,160]{3,2,1,0:T(8,128)(2,1)}, bf16[2,8,80,160]{3,2,1,0:T(8,128)(2,1)}, bf16[4,8,80,128]{3,2,1,0:T(8,128)(2,1)}, f32[128,128]{1,0:...) custom-call(s32[17]{0:T(128)S(1)} %add_convert_fusion.10.order_ref, ...), custom_call_target="tpu_custom_call" | custom-call | bytes 68400000 | tf_op jit(solution)/shard_map/backward_scan/pallas_call | solution.py:744
  169.9 9.5 %emit.1 = (bf16[4,64,2048]{2,1,0:T(8,128)(2,1)}, bf16[4,64,2048]{2,1,0:T(8,128)(2,1)}, bf16[2,2,128,2048]{3,2,1,0:T(8,128)(2,1)}, bf16[2,2,128,2048]{3,2,1,0:T(8...) custom-call(s32[9]{0:T(128)S(1)} %add_convert_fusion.9.order_ref, bf16[4,2,8,64,128]{4,3,2,1,0:T(8,128)(2,1)} %copy-done.20, ...), custom_call_target="tpu_custom_call" | custom-call | bytes 21600000 | tf_op jit(solution)/shard_map/emit/pallas_call | solution.py:1105
  180.2 3.5 %all-to-all-start.3 = ((bf16[4,8,80,128]{3,2,1,0:T(8,128)(2,1)}), bf16[4,8,80,128]{3,2,1,0:T(8,128)(2,1)S(1)}, u32[]{:S(2)}, u32[]{:S(2)}) async-start(bf16[4,8,80,128]{3,2,1,0:T(8,128)(2,1)} %get-tuple-element.216), calls=%async_computation.3 | async-start | bytes 1310720 | tf_op jit(solution)/shard_map/all_to_all | solution.py:1346
  192.0 3.0 add_convert_fusion
  197.3 4.9 %collective-permute-done.26 = bf16[4,80,160]{2,1,0:T(8,128)(2,1)S(1)} collective-permute-done((bf16[4,80,160]{2,1,0:T(8,128)(2,1)S(1)}, bf16[4,80,160]{2,1,0:T(8,128)(2,1)S(1)}, u32[]{:S(2)}, u32[]{:S(2)}) %collective-permute-start.26) | collective-permute-done | bytes 102432 | tf_op jit(solution)/shard_map/ppermute | solution.py:1340
  202.2 13.5 %collective-permute-done.28 = bf16[4,64,2048]{2,1,0:T(8,128)(2,1)} collective-permute-done((bf16[4,64,2048]{2,1,0:T(8,128)(2,1)}, bf16[4,64,2048]{2,1,0:T(8,128)(2,1)}, u32[]{:S(2)}, u32[]{:S(2)}) %collective-permute-start.28) | collective-permute-done | bytes 1048608 | tf_op jit(solution)/shard_map/ppermute | solution.py:1337
  226.7 5.9 %turn_back.1 = (bf16[512,1024]{1,0:T(8,128)(2,1)S(1)}, bf16[512,128]{1,0:T(8,128)(2,1)}, f32[40,512]{1,0:T(8,128)S(1)}) custom-call(s32[9]{0:T(128)S(1)} %add_convert_fusion.9.order_ref, bf16[4,80,160]{2,1,0:T(8,128)(2,1)S(1)} %add_convert_fusion.4.refs_0_, bf16[4,80,160]{2,1,0:T(8,128)(2,1)S(1)} %collective-permute-done.29.refs_1_, ...), custom_call_target="tpu_custom_call" | custom-call | bytes 19800000 | tf_op jit(solution)/shard_map/turn_back/pallas_call | solution.py:1275
  232.6 5.7 %weigh.1 = (bf16[2,128,2048]{2,1,0:T(8,128)(2,1)}, bf16[2,128,2048]{2,1,0:T(8,128)(2,1)}, f32[1,2048]{1,0:T(1,128)S(1)}) custom-call(s32[9]{0:T(128)S(1)} %add_convert_fusion.9.order_ref, bf16[512,1024]{1,0:T(8,128)(2,1)S(1)} %get-tuple-element.243.rows_ref, bf16[512,2048]{1,0:T(8,128)(2,1)} %get-tuple-element.207.refs_3_.normed_ref, ...), custom_call_target="tpu_custom_call" | custom-call | bytes 14400000 | tf_op jit(solution)/shard_map/weigh/pallas_call | solution.py:1161
  239.4 2.9 convolution_convert_fusion
  255.9 8.6 %collective-permute-done.39.refs_2_.refs_6_ = bf16[2,128,2048]{2,1,0:T(8,128)(2,1)S(1)} collective-permute-done((bf16[2,128,2048]{2,1,0:T(8,128)(2,1)S(1)}, bf16[2,128,2048]{2,1,0:T(8,128)(2,1)S(1)}, u32[]{:S(2)}, u32[]{:S(2)}) %collective-permute-start.39) | collective-permute-done | bytes 1048608 | tf_op jit(solution)/shard_map/ppermute | solution.py:1343
  272.3 5.2 %collective-permute-done.45 = bf16[128,2048]{1,0:T(8,128)(2,1)S(1)} collective-permute-done((bf16[128,2048]{1,0:T(8,128)(2,1)S(1)}, bf16[128,2048]{1,0:T(8,128)(2,1)S(1)}, u32[]{:S(2)}, u32[]{:S(2)}) %collective-permute-start.45) | collective-permute-done | bytes 524320 | tf_op jit(solution)/shard_map/ppermute | solution.py:1343
  278.0 3.6 %collective-permute-done.48 = bf16[64,1280]{1,0:T(8,128)(2,1)S(1)} collective-permute-done((bf16[64,1280]{1,0:T(8,128)(2,1)S(1)}, bf16[64,1280]{1,0:T(8,128)(2,1)S(1)}, u32[]{:S(2)}, u32[]{:S(2)}) %collective-permute-start.48) | collective-permute-done | bytes 163872 | tf_op jit(solution)/shard_map/ppermute | solution.py:1340
  287.3 3.0 placed.3
  291.5 10.8 %collective-permute-done.50.refs_2_ = bf16[64,2048]{1,0:T(8,128)(2,1)S(1)} collective-permute-done((bf16[64,2048]{1,0:T(8,128)(2,1)S(1)}, bf16[64,2048]{1,0:T(8,128)(2,1)S(1)}, u32[]{:S(2)}, u32[]{:S(2)}) %collective-permute-start.50) | collective-permute-done | bytes 262176 | tf_op jit(solution)/shard_map/ppermute | solution.py:1343
  304.7 9.0 %interleave.1 = f32[2048,2,512]{2,1,0:T(2,128)} custom-call(s32[4]{0:T(128)S(1)} %xor_convert_fusion.order_ref, bf16[128,2048]{1,0:T(8,128)(2,1)S(1)} %fusion.6.refs_0_, bf16[128,2048]{1,0:T(8,128)(2,1)S(1)} %collective-permute-done.54.refs_1_, bf16[128,2048]{1,0:T(8,128)(2,1)S(1)} %collective-permute-done.53.refs_2_, ...), custom_call_target="tpu_custom_call" | custom-call | bytes 18000000 | tf_op jit(solution)/shard_map/interleave/pallas_call | solution.py:806
  313.7 3.5 %collective-permute-start.61 = (f32[2048]{0:T(1024)S(1)}, f32[2048]{0:T(1024)S(1)}, u32[]{:S(2)}, u32[]{:S(2)}) collective-permute-start(f32[2048]{0:T(1024)S(1)} %add.267), channel_id=1, source_target_pairs={{0,8},{4,12},{8,16},{12,20},{16,24},{20,28},{24,0},{28,4},{1,9},{5... | collective-permute-start | bytes 24584 | tf_op jit(solution)/shard_map/ppermute | solution.py:1340
  (311 shorter events, 110.2 us)
Async XLA Ops:
  11.2 22.7 %collective-permute-start = (bf16[72,2048]{1,0:T(8,128)(2,1)S(1)}, bf16[72,2048]{1,0:T(8,128)(2,1)S(1)}, u32[]{:S(2)}, u32[]{:S(2)}) collective-permute-start(bf16[72,2048]{1,0:T(8,128)(2,1)S(1)} %get-tuple-element.292.refs_0_), channel_id=1, source_target_pairs={{0,4},{4,0},{8,12},{12,8},{16,20},{20,16},{24,28},{28,24},{1,5},{5... | collective-permute-start | bytes 884744 | tf_op jit(solution)/shard_map/ppermute | solution.py:1337
  14.2 19.7 %collective-permute-start.1 = (bf16[72,2048]{1,0:T(8,128)(2,1)S(1)}, bf16[72,2048]{1,0:T(8,128)(2,1)S(1)}, u32[]{:S(2)}, u32[]{:S(2)}) collective-permute-start(bf16[72,2048]{1,0:T(8,128)(2,1)S(1)} %get-tuple-element.292.refs_0_), channel_id=1, source_target_pairs={{0,8},{4,12},{8,16},{12,20},{16,24},{20,28},{24,0},{28,4},{1,9},{5... | collective-permute-start | bytes 884744 | tf_op jit(solution)/shard_map/ppermute | solution.py:1340
  15.8 21.5 %collective-permute-start.2 = (bf16[72,2048]{1,0:T(8,128)(2,1)S(1)}, bf16[72,2048]{1,0:T(8,128)(2,1)S(1)}, u32[]{:S(2)}, u32[]{:S(2)}) collective-permute-start(bf16[72,2048]{1,0:T(8,128)(2,1)S(1)} %get-tuple-element.292.refs_0_), channel_id=1, source_target_pairs={{0,16},{4,20},{8,24},{12,28},{16,0},{20,4},{24,8},{28,12},{1,17},{... | collective-permute-start | bytes 884744 | tf_op jit(solution)/shard_map/ppermute | solution.py:1340
  18.4 18.9 %collective-permute-start.3 = (bf16[72,2048]{1,0:T(8,128)(2,1)S(1)}, bf16[72,2048]{1,0:T(8,128)(2,1)}, u32[]{:S(2)}, u32[]{:S(2)}) collective-permute-start(bf16[72,2048]{1,0:T(8,128)(2,1)S(1)} %get-tuple-element.292.refs_0_), channel_id=1, source_target_pairs={{0,24},{4,28},{8,0},{12,4},{16,8},{20,12},{24,16},{28,20},{1,25},{... | collective-permute-start | bytes 884744 | tf_op jit(solution)/shard_map/ppermute | solution.py:1340
  20.3 13.6 %all-to-all-start = ((f32[4,4,128]{2,1,0:T(4,128)}), f32[4,4,128]{2,1,0:T(4,128)}, u32[]{:S(2)}, u32[]{:S(2)}) async-start(f32[4,4,128]{2,1,0:T(4,128)} %bitcast.2), calls=%async_computation | async-start | bytes 16384 | tf_op jit(solution)/shard_map/all_to_all | solution.py:1346
  24.1 73.5 %all-gather.3.cloned.1.call-start = ((), (), s32[]{:S(2)}) async-start(), calls=%async_computation.4 | async-start | bytes 2359296 | tf_op jit(solution)/shard_map/all_gather | solution.py:1476
  42.5 18.5 %collective-permute-start.7 = (bf16[72,2048]{1,0:T(8,128)(2,1)S(1)}, bf16[72,2048]{1,0:T(8,128)(2,1)S(1)}, u32[]{:S(2)}, u32[]{:S(2)}) collective-permute-start(bf16[72,2048]{1,0:T(8,128)(2,1)S(1)} %collective-permute-done.2.refs_2_), channel_id=1, source_target_pairs={{0,4},{4,0},{8,12},{12,8},{16,20},{20,16},{24,28},{28,24},{1,5},{5... | collective-permute-start | bytes 884744 | tf_op jit(solution)/shard_map/ppermute | solution.py:1337
  44.0 22.3 %collective-permute-start.8 = (bf16[72,2048]{1,0:T(8,128)(2,1)}, bf16[72,2048]{1,0:T(8,128)(2,1)S(1)}, u32[]{:S(2)}, u32[]{:S(2)}) collective-permute-start(bf16[72,2048]{1,0:T(8,128)(2,1)} %collective-permute-done.3.refs_3_), channel_id=1, source_target_pairs={{0,4},{4,0},{8,12},{12,8},{16,20},{20,16},{24,28},{28,24},{1,5},{5... | collective-permute-start | bytes 884744 | tf_op jit(solution)/shard_map/ppermute | solution.py:1337
  87.3 16.0 %collective-permute-start.11 = (bf16[4,64,160]{2,1,0:T(8,128)(2,1)S(1)}, bf16[4,64,160]{2,1,0:T(8,128)(2,1)}, u32[]{:S(2)}, u32[]{:S(2)}) collective-permute-start(bf16[4,64,160]{2,1,0:T(8,128)(2,1)S(1)} %add_convert_fusion.8), channel_id=1, source_target_pairs={{0,8},{4,12},{8,16},{12,20},{16,24},{20,28},{24,0},{28,4},{1,9},{5... | collective-permute-start | bytes 245768 | tf_op jit(solution)/shard_map/ppermute | solution.py:1340
  94.0 26.6 %all-to-all-start.1 = ((bf16[4,2,8,64,128]{4,3,2,1,0:T(8,128)(2,1)}), bf16[4,2,8,64,128]{4,3,2,1,0:T(8,128)(2,1)S(1)}, u32[]{:S(2)}, u32[]{:S(2)}) async-start(bf16[4,2,8,64,128]{4,3,2,1,0:T(8,128)(2,1)} %get-tuple-element.179), calls=%async_computation.1 | async-start | bytes 2097152 | tf_op jit(solution)/shard_map/all_to_all | solution.py:1346
  139.0 25.3 %all-to-all-start.2 = ((bf16[4,2,8,64,128]{4,3,2,1,0:T(8,128)(2,1)}), bf16[4,2,8,64,128]{4,3,2,1,0:T(8,128)(2,1)S(1)}, u32[]{:S(2)}, u32[]{:S(2)}) async-start(bf16[4,2,8,64,128]{4,3,2,1,0:T(8,128)(2,1)} %get-tuple-element.197), calls=%async_computation.2 | async-start | bytes 2097152 | tf_op jit(solution)/shard_map/all_to_all | solution.py:1346
  180.2 17.0 %all-to-all-start.3 = ((bf16[4,8,80,128]{3,2,1,0:T(8,128)(2,1)}), bf16[4,8,80,128]{3,2,1,0:T(8,128)(2,1)S(1)}, u32[]{:S(2)}, u32[]{:S(2)}) async-start(bf16[4,8,80,128]{3,2,1,0:T(8,128)(2,1)} %get-tuple-element.216), calls=%async_computation.3 | async-start | bytes 1310720 | tf_op jit(solution)/shard_map/all_to_all | solution.py:1346
  188.1 14.1 %collective-permute-start.26 = (bf16[4,80,160]{2,1,0:T(8,128)(2,1)S(1)}, bf16[4,80,160]{2,1,0:T(8,128)(2,1)S(1)}, u32[]{:S(2)}, u32[]{:S(2)}) collective-permute-start(bf16[4,80,160]{2,1,0:T(8,128)(2,1)S(1)} %add_convert_fusion.5), channel_id=1, source_target_pairs={{0,16},{4,20},{8,24},{12,28},{16,0},{20,4},{24,8},{28,12},{1,17},{... | collective-permute-start | bytes 307208 | tf_op jit(solution)/shard_map/ppermute | solution.py:1340
  189.3 12.9 %collective-permute-start.27 = (bf16[4,80,160]{2,1,0:T(8,128)(2,1)S(1)}, bf16[4,80,160]{2,1,0:T(8,128)(2,1)}, u32[]{:S(2)}, u32[]{:S(2)}) collective-permute-start(bf16[4,80,160]{2,1,0:T(8,128)(2,1)S(1)} %add_convert_fusion.5), channel_id=1, source_target_pairs={{0,24},{4,28},{8,0},{12,4},{16,8},{20,12},{24,16},{28,20},{1,25},{... | collective-permute-start | bytes 307208 | tf_op jit(solution)/shard_map/ppermute | solution.py:1340
  191.4 24.3 %collective-permute-start.28 = (bf16[4,64,2048]{2,1,0:T(8,128)(2,1)}, bf16[4,64,2048]{2,1,0:T(8,128)(2,1)}, u32[]{:S(2)}, u32[]{:S(2)}) collective-permute-start(bf16[4,64,2048]{2,1,0:T(8,128)(2,1)} %get-tuple-element.215), channel_id=1, source_target_pairs={{0,4},{4,0},{8,12},{12,8},{16,20},{20,16},{24,28},{28,24},{1,5},{5... | collective-permute-start | bytes 3145736 | tf_op jit(solution)/shard_map/ppermute | solution.py:1337
  196.7 28.3 %collective-permute-start.30 = (bf16[2,128,2048]{2,1,0:T(8,128)(2,1)}, bf16[2,128,2048]{2,1,0:T(8,128)(2,1)}, u32[]{:S(2)}, u32[]{:S(2)}) collective-permute-start(bf16[2,128,2048]{2,1,0:T(8,128)(2,1)} %slice_bitcast_fusion.1), channel_id=1, source_target_pairs={{0,2},{1,3},{2,0},{3,1},{4,6},{5,7},{6,4},{7,5},{8,10},{9,11},{10,... | collective-permute-start | bytes 3145736 | tf_op jit(solution)/shard_map/ppermute | solution.py:1343
  220.3 23.6 %collective-permute-start.32 = (bf16[64,2048]{1,0:T(8,128)(2,1)}, bf16[64,2048]{1,0:T(8,128)(2,1)}, u32[]{:S(2)}, u32[]{:S(2)}) collective-permute-start(bf16[64,2048]{1,0:T(8,128)(2,1)} %get-tuple-element.298), channel_id=1, source_target_pairs={{0,8},{4,12},{8,16},{12,20},{16,24},{20,28},{24,0},{28,4},{1,9},{5... | collective-permute-start | bytes 786440 | tf_op jit(solution)/shard_map/ppermute | solution.py:1340
  220.9 23.1 %collective-permute-start.33 = (bf16[64,2048]{1,0:T(8,128)(2,1)}, bf16[64,2048]{1,0:T(8,128)(2,1)}, u32[]{:S(2)}, u32[]{:S(2)}) collective-permute-start(bf16[64,2048]{1,0:T(8,128)(2,1)} %get-tuple-element.297), channel_id=1, source_target_pairs={{0,16},{4,20},{8,24},{12,28},{16,0},{20,4},{24,8},{28,12},{1,17},{... | collective-permute-start | bytes 786440 | tf_op jit(solution)/shard_map/ppermute | solution.py:1340
  222.2 21.9 %collective-permute-start.34 = (bf16[64,2048]{1,0:T(8,128)(2,1)}, bf16[64,2048]{1,0:T(8,128)(2,1)}, u32[]{:S(2)}, u32[]{:S(2)}) collective-permute-start(bf16[64,2048]{1,0:T(8,128)(2,1)} %get-tuple-element.296), channel_id=1, source_target_pairs={{0,24},{4,28},{8,0},{12,4},{16,8},{20,12},{24,16},{28,20},{1,25},{... | collective-permute-start | bytes 786440 | tf_op jit(solution)/shard_map/ppermute | solution.py:1340
  238.5 26.0 %collective-permute-start.39 = (bf16[2,128,2048]{2,1,0:T(8,128)(2,1)S(1)}, bf16[2,128,2048]{2,1,0:T(8,128)(2,1)S(1)}, u32[]{:S(2)}, u32[]{:S(2)}) collective-permute-start(bf16[2,128,2048]{2,1,0:T(8,128)(2,1)S(1)} %fusion.3.refs_0_.refs_4_), channel_id=1, source_target_pairs={{0,2},{1,3},{2,0},{3,1},{4,6},{5,7},{6,4},{7,5},{8,10},{9,11},{10,... | collective-permute-start | bytes 3145736 | tf_op jit(solution)/shard_map/ppermute | solution.py:1343
  245.5 20.7 %collective-permute-start.35 = (bf16[4,64,1280]{2,1,0:T(8,128)(2,1)S(1)}, bf16[4,64,1280]{2,1,0:T(8,128)(2,1)S(1)}, u32[]{:S(2)}, u32[]{:S(2)}) collective-permute-start(bf16[4,64,1280]{2,1,0:T(8,128)(2,1)S(1)} %bitcast.190), channel_id=1, source_target_pairs={{0,4},{4,0},{8,12},{12,8},{16,20},{20,16},{24,28},{28,24},{1,5},{5... | collective-permute-start | bytes 1966088 | tf_op jit(solution)/shard_map/ppermute | solution.py:1337
  246.9 19.2 %collective-permute-start.40 = (bf16[2,64,768]{2,1,0:T(8,128)(2,1)S(1)}, bf16[2,64,768]{2,1,0:T(8,128)(2,1)S(1)}, u32[]{:S(2)}, u32[]{:S(2)}) collective-permute-start(bf16[2,64,768]{2,1,0:T(8,128)(2,1)S(1)} %get-tuple-element.249), channel_id=1, source_target_pairs={{0,16},{4,20},{8,24},{12,28},{16,0},{20,4},{24,8},{28,12},{1,17},{... | collective-permute-start | bytes 589832 | tf_op jit(solution)/shard_map/ppermute | solution.py:1340
  249.9 16.3 %collective-permute-start.41 = (bf16[2,64,768]{2,1,0:T(8,128)(2,1)S(1)}, bf16[2,64,768]{2,1,0:T(8,128)(2,1)S(1)}, u32[]{:S(2)}, u32[]{:S(2)}) collective-permute-start(bf16[2,64,768]{2,1,0:T(8,128)(2,1)S(1)} %get-tuple-element.250), channel_id=1, source_target_pairs={{0,24},{4,28},{8,0},{12,4},{16,8},{20,12},{24,16},{28,20},{1,25},{... | collective-permute-start | bytes 589832 | tf_op jit(solution)/shard_map/ppermute | solution.py:1340
  253.9 12.3 %collective-permute-start.38 = (f32[44,512]{1,0:T(8,128)S(1)}, f32[44,512]{1,0:T(8,128)S(1)}, u32[]{:S(2)}, u32[]{:S(2)}) collective-permute-start(f32[44,512]{1,0:T(8,128)S(1)} %add.249), channel_id=1, source_target_pairs={{0,2},{1,3},{2,0},{3,1},{4,6},{5,7},{6,4},{7,5},{8,10},{9,11},{10,... | collective-permute-start | bytes 270344 | tf_op jit(solution)/shard_map/ppermute | solution.py:1343
  264.5 13.0 %collective-permute-start.45 = (bf16[128,2048]{1,0:T(8,128)(2,1)S(1)}, bf16[128,2048]{1,0:T(8,128)(2,1)S(1)}, u32[]{:S(2)}, u32[]{:S(2)}) collective-permute-start(bf16[128,2048]{1,0:T(8,128)(2,1)S(1)} %slice_bitcast_fusion.3), channel_id=1, source_target_pairs={{0,2},{1,3},{2,0},{3,1},{4,6},{5,7},{6,4},{7,5},{8,10},{9,11},{10,... | collective-permute-start | bytes 1572872 | tf_op jit(solution)/shard_map/ppermute | solution.py:1343
  266.7 15.0 %collective-permute-start.48 = (bf16[64,1280]{1,0:T(8,128)(2,1)S(1)}, bf16[64,1280]{1,0:T(8,128)(2,1)S(1)}, u32[]{:S(2)}, u32[]{:S(2)}) collective-permute-start(bf16[64,1280]{1,0:T(8,128)(2,1)S(1)} %get-tuple-element.303), channel_id=1, source_target_pairs={{0,16},{4,20},{8,24},{12,28},{16,0},{20,4},{24,8},{28,12},{1,17},{... | collective-permute-start | bytes 491528 | tf_op jit(solution)/shard_map/ppermute | solution.py:1340
  267.7 14.0 %collective-permute-start.49 = (bf16[64,1280]{1,0:T(8,128)(2,1)S(1)}, bf16[64,1280]{1,0:T(8,128)(2,1)S(1)}, u32[]{:S(2)}, u32[]{:S(2)}) collective-permute-start(bf16[64,1280]{1,0:T(8,128)(2,1)S(1)} %get-tuple-element.302), channel_id=1, source_target_pairs={{0,24},{4,28},{8,0},{12,4},{16,8},{20,12},{24,16},{28,20},{1,25},{... | collective-permute-start | bytes 491528 | tf_op jit(solution)/shard_map/ppermute | solution.py:1340
  281.8 20.6 %collective-permute-start.53 = (bf16[128,2048]{1,0:T(8,128)(2,1)S(1)}, bf16[128,2048]{1,0:T(8,128)(2,1)S(1)}, u32[]{:S(2)}, u32[]{:S(2)}) collective-permute-start(bf16[128,2048]{1,0:T(8,128)(2,1)S(1)} %fusion.6.refs_0_), channel_id=1, source_target_pairs={{0,2},{1,3},{2,0},{3,1},{4,6},{5,7},{6,4},{7,5},{8,10},{9,11},{10,... | collective-permute-start | bytes 1572872 | tf_op jit(solution)/shard_map/ppermute | solution.py:1343
  283.1 19.3 %collective-permute-start.54 = (bf16[128,2048]{1,0:T(8,128)(2,1)S(1)}, bf16[128,2048]{1,0:T(8,128)(2,1)S(1)}, u32[]{:S(2)}, u32[]{:S(2)}) collective-permute-start(bf16[128,2048]{1,0:T(8,128)(2,1)S(1)} %fusion.6.refs_0_), channel_id=1, source_target_pairs={{0,1},{1,0},{2,3},{3,2},{4,5},{5,4},{6,7},{7,6},{8,9},{9,8},{10,11... | collective-permute-start | bytes 1572872 | tf_op jit(solution)/shard_map/ppermute | solution.py:1343
  283.6 18.8 %collective-permute-start.50 = (bf16[64,2048]{1,0:T(8,128)(2,1)S(1)}, bf16[64,2048]{1,0:T(8,128)(2,1)S(1)}, u32[]{:S(2)}, u32[]{:S(2)}) collective-permute-start(bf16[64,2048]{1,0:T(8,128)(2,1)S(1)} %multiply_convert_fusion.1.refs_0_), channel_id=1, source_target_pairs={{0,2},{1,3},{2,0},{3,1},{4,6},{5,7},{6,4},{7,5},{8,10},{9,11},{10,... | collective-permute-start | bytes 786440 | tf_op jit(solution)/shard_map/ppermute | solution.py:1343
  284.5 17.9 %collective-permute-start.51 = (bf16[64,2048]{1,0:T(8,128)(2,1)S(1)}, bf16[64,2048]{1,0:T(8,128)(2,1)S(1)}, u32[]{:S(2)}, u32[]{:S(2)}) collective-permute-start(bf16[64,2048]{1,0:T(8,128)(2,1)S(1)} %multiply_convert_fusion.1.refs_0_), channel_id=1, source_target_pairs={{0,1},{1,0},{2,3},{3,2},{4,5},{5,4},{6,7},{7,6},{8,9},{9,8},{10,11... | collective-permute-start | bytes 786440 | tf_op jit(solution)/shard_map/ppermute | solution.py:1343
  290.3 23.3 %collective-permute-start.42 = (bf16[64,2048]{1,0:T(8,128)(2,1)S(1)}, bf16[64,2048]{1,0:T(8,128)(2,1)S(1)}, u32[]{:S(2)}, u32[]{:S(2)}) collective-permute-start(bf16[64,2048]{1,0:T(8,128)(2,1)S(1)} %fusion.10.refs_0_), channel_id=1, source_target_pairs={{0,2},{1,3},{2,0},{3,1},{4,6},{5,7},{6,4},{7,5},{8,10},{9,11},{10,... | collective-permute-start | bytes 786440 | tf_op jit(solution)/shard_map/ppermute | solution.py:1343
  (77 other events, 730.2 us)
Sparse Core Ops, SparseCore 0:
  37.5 59.8 all-gather.2
